TPU v7x, 32 devices: a whole 2x2x4 slice. The times are simulated.
32 devices in a mesh: seq: 16 (over z, y, core), tp: 2 (over x).
Axes of the slice: x: 2, y: 2, z: 4, core: 2. Of those that a mesh axis runs over, the one named last changes fastest.
Arguments:
- hidden_in: bfloat16 [384, 8192], P('seq', 'tp'), may hold values from -8 to 8
- kv_weight: bfloat16 [8192, 1024], P('tp'), may hold values from -0.0625 to 0.0625
- queries: bfloat16 [384, 4096], P('seq', 'tp'), may hold values from -15 to 15
- prefix_keys: bfloat16 [128, 128, 512], P('seq', None, 'tp'), may hold values from -6 to 6
- prefix_values: bfloat16 [128, 128, 512], P('seq', None, 'tp'), may hold values from -6 to 6
- page_table: int32 [128], replicated, may hold values from 0 to 127, each once
- suffix_lengths: int32 [2, 8], replicated, may hold values from 1 to 160, 192 in all within a row
- out_weight: bfloat16 [4096, 4096], P('tp'), may hold values from -0.09375 to 0.09375
Outputs:
- hidden: bfloat16 [384, 4096], P('seq', 'tp')
- new_pages: bfloat16 [384, 1024], P('seq', 'tp')
Inputs may be any that keep to these rules, and one draw needn't show every extreme that they name: `page_table`: a permutation of the 128 cache pages; entries 64 * g to 64 * g + 63 are group g's prefix pages. `suffix_lengths`: each row sums to 192; group g's requests take its suffix tokens in order of their place u; some request has exactly 160 tokens.
All inputs are finite; a program needn't handle non-finite values.
Results may differ from a plain program's by a relative error of at most 0.0095.
Values may be sent and summed in bfloat16 or wider, within the bound.
No kernel may reach another device: no remote copies, remote signals or barrier semaphores. Data moves between devices by JAX's collectives and lax.ppermute only.
A program may use at most 192 MiB of HBM per device.

v0:
```python
import math

import jax
import jax.numpy as jnp
from jax import lax
from jax.sharding import PartitionSpec as P

HD = 128
PAGE = 128
GROUPS = 2
REQS = 8
LONGEST = 160


masked_score = -1e30


def partner(block, axis, bit):
    count = lax.axis_size(axis)
    route = []
    for low in range(count):
        high = low | 1 << bit
        if high != low and high < count:
            route += [(low, high), (high, low)]
    return lax.ppermute(block, axis, route)


def passed_along(array, axis, by):
    length = lax.axis_size(axis)
    pairs = [(i, i + by) for i in range(length) if 0 <= i + by < length]
    return lax.ppermute(array, axis, pairs)


def place_tokens(tokens, block_rows):
    blocks = tokens // block_rows
    groups = blocks % GROUPS
    within = blocks // GROUPS * block_rows + tokens % block_rows
    return (groups, within)


def token_table(groups, within, lengths):
    picker = (groups[:, None] == jnp.arange(GROUPS, dtype=jnp.int32)[None, :]).astype(jnp.int32)
    end_marks = jnp.cumsum(lengths, axis=1)
    token_ends = jnp.sum(picker[:, :, None] * end_marks[None, :, :], axis=1)
    token_lens = jnp.sum(picker[:, :, None] * lengths[None, :, :], axis=1)
    passed = (within[:, None] >= token_ends).astype(jnp.int32)
    request = jnp.sum(passed, axis=1)
    offset = within - jnp.sum(passed * token_lens, axis=1)
    return (groups * REQS + request, offset)


def rotate(key_rows, positions):
    half_dim = HD // 2
    frequency = jnp.power(500000.0, -(jnp.arange(half_dim, dtype=jnp.float32) * 2.0 / HD))
    angles = positions.astype(jnp.float32)[:, None] * frequency[None, :]
    cosine = jnp.cos(angles)[:, None, :]
    sine_part = jnp.sin(angles)[:, None, :]
    leading = key_rows[..., :half_dim]
    trailing = key_rows[..., half_dim:]
    return jnp.concatenate(
        [leading * cosine - trailing * sine_part, trailing * cosine + leading * sine_part], axis=-1
    )


def slot_groups(slot_ids, page_table, group_pages):
    matches = page_table[None, :] == slot_ids[:, None]
    owners = jnp.arange(page_table.shape[0], dtype=jnp.int32) // group_pages
    return jnp.sum(jnp.where(matches, owners[None, :], 0), axis=1)


def online_update(running, scores, usable, values):
    row_top, totals, mixed_sum = running
    kept_scores = jnp.where(usable, scores, masked_score)
    new_top = jnp.maximum(row_top, jnp.max(kept_scores, axis=-1))
    weights = jnp.exp(kept_scores - new_top[..., None]) * usable.astype(jnp.float32)
    factor = jnp.exp(row_top - new_top)
    totals = totals * factor + jnp.sum(weights, axis=-1)
    product = jnp.einsum(
        "tkgp,pkd->tkgd", weights.astype(jnp.bfloat16), values, preferred_element_type=jnp.float32
    )
    mixed_sum = mixed_sum * factor[..., None] + product
    return (new_top, totals, mixed_sum)


def merge_states(first, second):
    first_top, first_totals, first_mixed = first
    second_top, second_totals, second_mixed = second
    new_top = jnp.maximum(first_top, second_top)
    first_factor = jnp.exp(first_top - new_top)
    second_factor = jnp.exp(second_top - new_top)
    totals = first_totals * first_factor + second_totals * second_factor
    mixed_sum = first_mixed * first_factor[..., None] + second_mixed * second_factor[..., None]
    return (new_top, totals, mixed_sum)


def blank_state(row_count, kv_heads, group_q):
    return (
        jnp.full((row_count, kv_heads, group_q), masked_score, jnp.float32),
        jnp.zeros((row_count, kv_heads, group_q), jnp.float32),
        jnp.zeros((row_count, kv_heads, group_q, HD), jnp.float32),
    )


def local(
    hidden_in,
    kv_weight,
    queries,
    prefix_keys,
    prefix_values,
    page_table,
    suffix_lengths,
    out_weight,
):
    row_count = hidden_in.shape[0]
    seq_count = lax.axis_size("seq")
    seq_rank = lax.axis_index("seq")
    suffix_total = row_count * seq_count
    half_total = suffix_total // GROUPS
    pages_here = prefix_keys.shape[0]
    group_pages = pages_here * seq_count // GROUPS
    prefix_len = group_pages * PAGE
    kv_heads = prefix_keys.shape[2] // HD
    head_count = queries.shape[1] // HD
    group_q = head_count // kv_heads
    score_scale = 1.0 / math.sqrt(HD)
    partial_kv = jnp.dot(hidden_in, kv_weight, preferred_element_type=jnp.float32)
    local_kv = lax.psum_scatter(partial_kv, "tp", scatter_dimension=1, tiled=True).reshape(
        row_count, kv_heads, 2, HD
    )
    tokens = seq_rank * row_count + jnp.arange(row_count, dtype=jnp.int32)
    groups, within = place_tokens(tokens, row_count)
    request_ids, offsets = token_table(groups, within, suffix_lengths)
    rotated = rotate(local_kv[:, :, 0], prefix_len + offsets)
    new_pages = (
        jnp.stack([rotated, local_kv[:, :, 1]], axis=2)
        .reshape(row_count, kv_heads * 2 * HD)
        .astype(jnp.bfloat16)
    )
    query_block = queries.reshape(row_count, kv_heads, group_q, HD)
    my_group = seq_rank % GROUPS
    my_block = seq_rank // GROUPS
    seq_bits = seq_count.bit_length() - 1
    partner_keys, partner_vals = partner((prefix_keys, prefix_values), "seq", 0)
    both_keys = jnp.concatenate([prefix_keys, partner_keys], axis=0)
    both_vals = jnp.concatenate([prefix_values, partner_vals], axis=0)
    partner_rank = jnp.bitwise_xor(seq_rank, 1)
    slot_ids = jnp.concatenate(
        [
            seq_rank * pages_here + jnp.arange(pages_here, dtype=jnp.int32),
            partner_rank * pages_here + jnp.arange(pages_here, dtype=jnp.int32),
        ]
    )
    slot_usable = slot_groups(slot_ids, page_table, group_pages) == my_group
    gathered = queries
    for bit_number in range(1, seq_bits):
        other_rows = partner(gathered, "seq", bit_number)
        upper_side = jnp.bitwise_and(jnp.right_shift(seq_rank, bit_number), 1) == 1
        gathered = jnp.where(
            upper_side,
            jnp.concatenate([other_rows, gathered], axis=0),
            jnp.concatenate([gathered, other_rows], axis=0),
        )
    group_rows = gathered.shape[0]
    group_query = gathered.reshape(group_rows, kv_heads, group_q, HD)
    slot_count = 2 * pages_here
    turn_pages = math.gcd(slot_count, 2)

    def slot_turn(turn_index, running):
        offset_row = turn_index * turn_pages
        keys_now = lax.dynamic_slice_in_dim(both_keys, offset_row, turn_pages, 0).reshape(
            turn_pages * PAGE, kv_heads, HD
        )
        vals_now = lax.dynamic_slice_in_dim(both_vals, offset_row, turn_pages, 0).reshape(
            turn_pages * PAGE, kv_heads, HD
        )
        usable = jnp.repeat(lax.dynamic_slice_in_dim(slot_usable, offset_row, turn_pages, 0), PAGE)
        scores = (
            jnp.einsum("tkgd,pkd->tkgp", group_query, keys_now, preferred_element_type=jnp.float32)
            * score_scale
        )
        return online_update(running, scores, usable[None, None, None, :], vals_now)

    state = lax.fori_loop(
        0, slot_count // turn_pages, slot_turn, blank_state(group_rows, kv_heads, group_q)
    )
    for bit_number in range(seq_bits - 1, 0, -1):
        span = state[0].shape[0] // 2
        upper_side = jnp.bitwise_and(jnp.right_shift(seq_rank, bit_number), 1) == 1
        keep_part = tuple((jnp.where(upper_side, member[span:], member[:span]) for member in state))
        give_part = tuple((jnp.where(upper_side, member[:span], member[span:]) for member in state))
        got_part = partner((give_part[0], give_part[1], give_part[2]), "seq", bit_number)
        state = merge_states(keep_part, got_part)
    reach_blocks = (min(LONGEST, half_total - REQS + 1) + row_count - 2) // row_count
    earlier = []
    for distance in range(reach_blocks, 0, -1):
        earlier.append(passed_along(new_pages, "seq", GROUPS * distance))
    window = jnp.concatenate(earlier + [new_pages], axis=0)
    window_len = window.shape[0]
    window_places = (my_block - reach_blocks) * row_count + jnp.arange(window_len, dtype=jnp.int32)
    inside = window_places >= 0
    window_groups = jnp.zeros((window_len,), jnp.int32) + my_group
    window_ids, unused_offsets = token_table(
        window_groups, jnp.maximum(window_places, 0), suffix_lengths
    )
    visible = (
        inside[None, :]
        & (window_ids[None, :] == request_ids[:, None])
        & (window_places[None, :] <= within[:, None])
    )
    window_kv = window.reshape(window_len, kv_heads, 2, HD)
    suffix_scores = (
        jnp.einsum(
            "tkgd,pkd->tkgp", query_block, window_kv[:, :, 0], preferred_element_type=jnp.float32
        )
        * score_scale
    )
    final_top, totals, mixed_sum = online_update(
        state, suffix_scores, visible[:, None, None, :], window_kv[:, :, 1]
    )
    attended = (
        (mixed_sum / totals[..., None]).reshape(row_count, head_count * HD).astype(jnp.bfloat16)
    )
    partial_out = jnp.dot(attended, out_weight, preferred_element_type=jnp.float32)
    hidden = lax.psum_scatter(partial_out, "tp", scatter_dimension=1, tiled=True).astype(
        jnp.bfloat16
    )
    return (hidden, new_pages)


def solution(mesh):
    return jax.shard_map(
        local,
        mesh=mesh,
        in_specs=(
            P("seq", "tp"),
            P("tp", None),
            P("seq", "tp"),
            P("seq", None, "tp"),
            P("seq", None, "tp"),
            P(),
            P(),
            P("tp", None),
        ),
        out_specs=(P("seq", "tp"), P("seq", "tp")),
        check_vma=False,
    )
```

profile of v0, /device:TPU:0, one launch (start us, length us, event | category | flops | bytes accessed | tf_op | source)
XLA Modules:
  0.0 246.4 jit_solution(2898867444431742420)
XLA Ops:
  7.3 3.0 %collective-permute-start.1 = (bf16[24,2048]{1,0:T(8,128)(2,1)}, bf16[24,2048]{1,0:T(8,128)(2,1)S(1)}, u32[]{:S(2)}, u32[]{:S(2)}) collective-permute-start(bf16[24,2048]{1,0:T(8,128)(2,1)} %param.12), channel_id=1, source_target_pairs={{0,4},{4,0},{2,6},{6,2},{8,12},{12,8},{10,14},{14,10},{16,20},{20,... | collective-permute-start | bytes 294920 | tf_op jit(solution)/shard_map/ppermute | solution.py:25
  10.8 5.2 %fusion.44 = f32[24,1024]{1,0:T(8,128)} fusion(bf16[24,4096]{1,0:T(8,128)(2,1)S(1)} %copy-done, bf16[4096,1024]{1,0:T(8,128)(2,1)} %param.11), kind=kOutput, calls=%fused_computation.134 | convolution fusion | flops 201326592 | bytes 8683520 | tf_op jit(solution)/shard_map/dot_general | solution.py:126
  18.5 1.6 collective-permute-start.2
  20.1 6.3 %reduce-scatter.3.cloned.1.call-done = f32[24,512]{1,0:T(8,128)} async-done(((f32[24,1024]{1,0:T(8,128)}), f32[24,512]{1,0:T(8,128)}) %reduce-scatter.3.cloned.1.call-update) | async-done | bytes 49168 | tf_op jit(solution)/shard_map/reduce_scatter | solution.py:127
  27.6 6.1 %collective-permute-start.11 = (bf16[24,512]{1,0:T(8,128)(2,1)S(1)}, bf16[24,512]{1,0:T(8,128)(2,1)S(1)}, u32[]{:S(2)}, u32[]{:S(2)}) collective-permute-start(bf16[24,512]{1,0:T(8,128)(2,1)S(1)} %convert_element_type.76), channel_id=1, source_target_pairs={{0,28},{2,30},{1,29},{3,31}} | collective-permute-start | bytes 73736 | tf_op jit(solution)/shard_map/ppermute | solution.py:31
  38.1 8.1 %collective-permute-start.15 = (bf16[24,512]{1,0:T(8,128)(2,1)S(1)}, bf16[24,512]{1,0:T(8,128)(2,1)S(1)}, u32[]{:S(2)}, u32[]{:S(2)}) collective-permute-start(bf16[24,512]{1,0:T(8,128)(2,1)S(1)} %convert_element_type.76), channel_id=1, source_target_pairs={{0,12},{2,14},{4,16},{6,18},{8,20},{10,22},{12,24},{14,26},{16,28}... | collective-permute-start | bytes 73736 | tf_op jit(solution)/shard_map/ppermute | solution.py:31
  46.3 1.5 collective-permute-start.16
  47.8 2.9 %collective-permute-start.17 = (bf16[24,512]{1,0:T(8,128)(2,1)S(1)}, bf16[24,512]{1,0:T(8,128)(2,1)S(1)}, u32[]{:S(2)}, u32[]{:S(2)}) collective-permute-start(bf16[24,512]{1,0:T(8,128)(2,1)S(1)} %convert_element_type.76), channel_id=1, source_target_pairs={{0,4},{2,6},{4,8},{6,10},{8,12},{10,14},{12,16},{14,18},{16,20},{1... | collective-permute-start | bytes 73736 | tf_op jit(solution)/shard_map/ppermute | solution.py:31
  50.7 1.5 collective-permute-done.17
  53.4 11.0 %collective-permute-start.3 = (bf16[96,2048]{1,0:T(8,128)(2,1)S(1)}, bf16[96,2048]{1,0:T(8,128)(2,1)S(1)}, u32[]{:S(2)}, u32[]{:S(2)}) collective-permute-start(bf16[96,2048]{1,0:T(8,128)(2,1)S(1)} %maximum_select_fusion.1), channel_id=1, source_target_pairs={{0,16},{16,0},{2,18},{18,2},{4,20},{20,4},{6,22},{22,6},{8,24},{24... | collective-permute-start | bytes 1179656 | tf_op jit(solution)/shard_map/ppermute | solution.py:25
  66.7 7.1 %collective-permute-done.3 = bf16[96,2048]{1,0:T(8,128)(2,1)S(1)} collective-permute-done((bf16[96,2048]{1,0:T(8,128)(2,1)S(1)}, bf16[96,2048]{1,0:T(8,128)(2,1)S(1)}, u32[]{:S(2)}, u32[]{:S(2)}) %collective-permute-start.3) | collective-permute-done | bytes 393248 | tf_op jit(solution)/shard_map/ppermute | solution.py:25
  75.1 84.6 %while.18 = (s32[]{:T(128)}, f32[192,2,8]{0,2,1:T(8,128)S(1)}, f32[192,2,8]{0,2,1:T(8,128)S(1)}, f32[192,2,8,128]{3,0,2,1:T(8,128)}, pred[16]{0:T(512)(128)(4,1)...) while((s32[]{:T(128)}, f32[192,2,8]{0,2,1:T(8,128)S(1)}, ...), condition=%wide.region_4.5_spmd.clone, body=%wide.region_1.4_spmd.clone.sunk | while | flops 414072064 | bytes 14880957 | solution.py:183
  77.6 2.1 bitcast_reduce_fusion.2
  79.7 1.3 fusion.57
  81.7 3.3 %bitcast_add_fusion.2 = f32[192,2,8,128]{3,0,2,1:T(8,128)} fusion(f32[192,2,8,128]{3,0,2,1:T(8,128)} %get-tuple-element.335, f32[2,256,192,8]{1,2,3,0:T(8,128)S(1)} %get-tuple-element.315, f32[256]{0:T(256)S(1)} %get-tuple-element.316, f32[192,2,8]{0,2,1:T(8,128)S(1)} %select_maximum_fusion.2, pred[256]{0:T(512)(128)(4,1)S(1)} %get-tuple-element.312, ...), kind=kOutput, calls=%fused_computation.8.clone.1 | convolution fusion | flops 206438400 | bytes 6448385 | tf_op jit(solution)/shard_map/while/body/eval_jaxpr/tkgp,pkd->tkgd/dot_general | solution.py:78
  87.6 2.1 bitcast_reduce_fusion.2
  89.7 1.3 fusion.57
  91.7 4.0 %bitcast_add_fusion.2 = f32[192,2,8,128]{3,0,2,1:T(8,128)} fusion(f32[192,2,8,128]{3,0,2,1:T(8,128)} %get-tuple-element.335, f32[2,256,192,8]{1,2,3,0:T(8,128)S(1)} %get-tuple-element.315, f32[256]{0:T(256)S(1)} %get-tuple-element.316, f32[192,2,8]{0,2,1:T(8,128)S(1)} %select_maximum_fusion.2, pred[256]{0:T(512)(128)(4,1)S(1)} %get-tuple-element.312, ...), kind=kOutput, calls=%fused_computation.8.clone.1 | convolution fusion | flops 206438400 | bytes 6448385 | tf_op jit(solution)/shard_map/while/body/eval_jaxpr/tkgp,pkd->tkgd/dot_general | solution.py:78
  98.2 2.1 bitcast_reduce_fusion.2
  100.4 1.3 fusion.57
  102.4 4.0 %bitcast_add_fusion.2 = f32[192,2,8,128]{3,0,2,1:T(8,128)} fusion(f32[192,2,8,128]{3,0,2,1:T(8,128)} %get-tuple-element.335, f32[2,256,192,8]{1,2,3,0:T(8,128)S(1)} %get-tuple-element.315, f32[256]{0:T(256)S(1)} %get-tuple-element.316, f32[192,2,8]{0,2,1:T(8,128)S(1)} %select_maximum_fusion.2, pred[256]{0:T(512)(128)(4,1)S(1)} %get-tuple-element.312, ...), kind=kOutput, calls=%fused_computation.8.clone.1 | convolution fusion | flops 206438400 | bytes 6448385 | tf_op jit(solution)/shard_map/while/body/eval_jaxpr/tkgp,pkd->tkgd/dot_general | solution.py:78
  108.9 2.1 bitcast_reduce_fusion.2
  111.0 1.3 fusion.57
  113.0 4.0 %bitcast_add_fusion.2 = f32[192,2,8,128]{3,0,2,1:T(8,128)} fusion(f32[192,2,8,128]{3,0,2,1:T(8,128)} %get-tuple-element.335, f32[2,256,192,8]{1,2,3,0:T(8,128)S(1)} %get-tuple-element.315, f32[256]{0:T(256)S(1)} %get-tuple-element.316, f32[192,2,8]{0,2,1:T(8,128)S(1)} %select_maximum_fusion.2, pred[256]{0:T(512)(128)(4,1)S(1)} %get-tuple-element.312, ...), kind=kOutput, calls=%fused_computation.8.clone.1 | convolution fusion | flops 206438400 | bytes 6448385 | tf_op jit(solution)/shard_map/while/body/eval_jaxpr/tkgp,pkd->tkgd/dot_general | solution.py:78
  119.5 2.1 bitcast_reduce_fusion.2
  121.7 1.3 fusion.57
  123.7 4.0 %bitcast_add_fusion.2 = f32[192,2,8,128]{3,0,2,1:T(8,128)} fusion(f32[192,2,8,128]{3,0,2,1:T(8,128)} %get-tuple-element.335, f32[2,256,192,8]{1,2,3,0:T(8,128)S(1)} %get-tuple-element.315, f32[256]{0:T(256)S(1)} %get-tuple-element.316, f32[192,2,8]{0,2,1:T(8,128)S(1)} %select_maximum_fusion.2, pred[256]{0:T(512)(128)(4,1)S(1)} %get-tuple-element.312, ...), kind=kOutput, calls=%fused_computation.8.clone.1 | convolution fusion | flops 206438400 | bytes 6448385 | tf_op jit(solution)/shard_map/while/body/eval_jaxpr/tkgp,pkd->tkgd/dot_general | solution.py:78
  130.2 2.1 bitcast_reduce_fusion.2
  132.3 1.3 fusion.57
  134.3 4.0 %bitcast_add_fusion.2 = f32[192,2,8,128]{3,0,2,1:T(8,128)} fusion(f32[192,2,8,128]{3,0,2,1:T(8,128)} %get-tuple-element.335, f32[2,256,192,8]{1,2,3,0:T(8,128)S(1)} %get-tuple-element.315, f32[256]{0:T(256)S(1)} %get-tuple-element.316, f32[192,2,8]{0,2,1:T(8,128)S(1)} %select_maximum_fusion.2, pred[256]{0:T(512)(128)(4,1)S(1)} %get-tuple-element.312, ...), kind=kOutput, calls=%fused_computation.8.clone.1 | convolution fusion | flops 206438400 | bytes 6448385 | tf_op jit(solution)/shard_map/while/body/eval_jaxpr/tkgp,pkd->tkgd/dot_general | solution.py:78
  140.9 2.1 bitcast_reduce_fusion.2
  143.0 1.3 fusion.57
  145.0 4.0 %bitcast_add_fusion.2 = f32[192,2,8,128]{3,0,2,1:T(8,128)} fusion(f32[192,2,8,128]{3,0,2,1:T(8,128)} %get-tuple-element.335, f32[2,256,192,8]{1,2,3,0:T(8,128)S(1)} %get-tuple-element.315, f32[256]{0:T(256)S(1)} %get-tuple-element.316, f32[192,2,8]{0,2,1:T(8,128)S(1)} %select_maximum_fusion.2, pred[256]{0:T(512)(128)(4,1)S(1)} %get-tuple-element.312, ...), kind=kOutput, calls=%fused_computation.8.clone.1 | convolution fusion | flops 206438400 | bytes 6448385 | tf_op jit(solution)/shard_map/while/body/eval_jaxpr/tkgp,pkd->tkgd/dot_general | solution.py:78
  151.5 2.1 bitcast_reduce_fusion.2
  153.6 1.3 fusion.57
  155.6 4.0 %bitcast_add_fusion.2 = f32[192,2,8,128]{3,0,2,1:T(8,128)} fusion(f32[192,2,8,128]{3,0,2,1:T(8,128)} %get-tuple-element.335, f32[2,256,192,8]{1,2,3,0:T(8,128)S(1)} %get-tuple-element.315, f32[256]{0:T(256)S(1)} %get-tuple-element.316, f32[192,2,8]{0,2,1:T(8,128)S(1)} %select_maximum_fusion.2, pred[256]{0:T(512)(128)(4,1)S(1)} %get-tuple-element.312, ...), kind=kOutput, calls=%fused_computation.8.clone.1 | convolution fusion | flops 206438400 | bytes 6448385 | tf_op jit(solution)/shard_map/while/body/eval_jaxpr/tkgp,pkd->tkgd/dot_general | solution.py:78
  159.8 2.9 %collective-permute-start.5 = (f32[96,2,8]{0,2,1:T(8,128)S(1)}, f32[96,2,8]{0,2,1:T(8,128)S(1)}, u32[]{:S(2)}, u32[]{:S(2)}) collective-permute-start(f32[96,2,8]{0,2,1:T(8,128)S(1)} %slice_select_fusion.10), channel_id=1, source_target_pairs={{0,16},{16,0},{2,18},{18,2},{4,20},{20,4},{6,22},{22,6},{8,24},{24... | collective-permute-start | bytes 18440 | tf_op jit(solution)/shard_map/ppermute | solution.py:25
  162.7 1.5 slice_select_fusion
  164.8 3.1 %collective-permute-start.19 = (f32[48,2,8]{0,2,1:T(8,128)S(1)}, f32[48,2,8]{0,2,1:T(8,128)S(1)}, u32[]{:S(2)}, u32[]{:S(2)}) collective-permute-start(f32[48,2,8]{0,2,1:T(8,128)S(1)} %slice_select_fusion.4), channel_id=1, source_target_pairs={{0,8},{8,0},{2,10},{10,2},{4,12},{12,4},{6,14},{14,6},{16,24},{24,... | collective-permute-start | bytes 9224 | tf_op jit(solution)/shard_map/ppermute | solution.py:25
  169.3 4.8 %collective-permute-done.19 = f32[48,2,8]{0,2,1:T(8,128)S(1)} collective-permute-done((f32[48,2,8]{0,2,1:T(8,128)S(1)}, f32[48,2,8]{0,2,1:T(8,128)S(1)}, u32[]{:S(2)}, u32[]{:S(2)}) %collective-permute-start.19) | collective-permute-done | bytes 3104 | tf_op jit(solution)/shard_map/ppermute | solution.py:25
  174.4 7.4 %collective-permute-start.9 = (f32[24,2,8]{0,2,1:T(8,128)S(1)}, f32[24,2,8]{0,2,1:T(8,128)S(1)}, u32[]{:S(2)}, u32[]{:S(2)}) collective-permute-start(f32[24,2,8]{0,2,1:T(8,128)S(1)} %slice_select_fusion.5), channel_id=1, source_target_pairs={{0,4},{4,0},{2,6},{6,2},{8,12},{12,8},{10,14},{14,10},{16,20},{20,... | collective-permute-start | bytes 4616 | tf_op jit(solution)/shard_map/ppermute | solution.py:25
  181.7 11.2 %collective-permute-done.6 = f32[96,2,8,128]{3,0,2,1:T(8,128)S(1)} collective-permute-done((f32[96,2,8,128]{3,0,2,1:T(8,128)S(1)}, f32[96,2,8,128]{3,0,2,1:T(8,128)S(1)}, u32[]{:S(2)}, u32[]{:S(2)}) %collective-permute-start.6) | collective-permute-done | bytes 786464 | tf_op jit(solution)/shard_map/ppermute | solution.py:25
  193.6 7.9 %collective-permute-start.20 = (f32[24,2,8]{0,2,1:T(8,128)S(1)}, f32[24,2,8]{0,2,1:T(8,128)S(1)}, u32[]{:S(2)}, u32[]{:S(2)}) collective-permute-start(f32[24,2,8]{0,2,1:T(8,128)S(1)} %slice_select_fusion.3), channel_id=1, source_target_pairs={{0,4},{4,0},{2,6},{6,2},{8,12},{12,8},{10,14},{14,10},{16,20},{20,... | collective-permute-start | bytes 4616 | tf_op jit(solution)/shard_map/ppermute | solution.py:25
  202.1 10.7 %collective-permute-start.10 = (f32[24,2,8,128]{3,0,2,1:T(8,128)S(1)}, f32[24,2,8,128]{3,0,2,1:T(8,128)S(1)}, u32[]{:S(2)}, u32[]{:S(2)}) collective-permute-start(f32[24,2,8,128]{3,0,2,1:T(8,128)S(1)} %slice_select_fusion.2), channel_id=1, source_target_pairs={{0,4},{4,0},{2,6},{6,2},{8,12},{12,8},{10,14},{14,10},{16,20},{20,... | collective-permute-start | bytes 589832 | tf_op jit(solution)/shard_map/ppermute | solution.py:25
  212.9 4.2 %collective-permute-done.10 = f32[24,2,8,128]{3,0,2,1:T(8,128)S(1)} collective-permute-done((f32[24,2,8,128]{3,0,2,1:T(8,128)S(1)}, f32[24,2,8,128]{3,0,2,1:T(8,128)S(1)}, u32[]{:S(2)}, u32[]{:S(2)}) %collective-permute-start.10) | collective-permute-done | bytes 196640 | tf_op jit(solution)/shard_map/ppermute | solution.py:25
  217.4 8.8 %fusion.26 = f32[24,4096]{1,0:T(8,128)} fusion(bf16[2048,4096]{1,0:T(8,128)(2,1)} %param.17, bf16[3,8,16,128]{3,2,1,0:T(8,128)(2,1)S(1)} %bitcast.90), kind=kOutput, calls=%fused_computation.50 | convolution fusion | flops 402653184 | bytes 17268736 | tf_op jit(solution)/shard_map/dot_general | solution.py:223
  226.3 11.7 %reduce-scatter.5.cloned.1.call-done = f32[24,2048]{1,0:T(8,128)} async-done(((f32[24,4096]{1,0:T(8,128)}), f32[24,2048]{1,0:T(8,128)}) %reduce-scatter.5.cloned.1.call-update) | async-done | bytes 196624 | tf_op jit(solution)/shard_map/reduce_scatter | solution.py:224
  238.0 1.6 convert_element_type.81
  (189 shorter events, 42.7 us)
Async XLA Ops:
  7.2 3.6 %copy-start = (bf16[24,4096]{1,0:T(8,128)(2,1)S(1)}, bf16[24,4096]{1,0:T(8,128)(2,1)}, u32[]{:S(2)}) copy-start(bf16[24,4096]{1,0:T(8,128)(2,1)} %param.10) | copy-start | bytes 589828
  7.2 11.2 %copy-start.4 = (bf16[24,2048]{1,0:T(8,128)(2,1)S(1)}, bf16[24,2048]{1,0:T(8,128)(2,1)}, u32[]{:S(2)}) copy-start(bf16[24,2048]{1,0:T(8,128)(2,1)} %param.12) | copy-start | bytes 294916
  7.2 9.0 %copy-start.9 = (s32[2,8]{1,0:T(2,128)S(1)}, s32[2,8]{1,0:T(2,128)}, u32[]{:S(2)}) copy-start(s32[2,8]{1,0:T(2,128)} %param.16) | copy-start | bytes 196
  7.2 9.7 %copy-start.10 = (s32[128]{0:T(128)S(1)}, s32[128]{0:T(128)}, u32[]{:S(2)}) copy-start(s32[128]{0:T(128)} %param.15) | copy-start | bytes 1540
  7.2 19.3 %reduce-scatter.3.cloned.1.call-start = ((), (), s32[]{:S(2)}) async-start(), calls=%async_computation.2 | async-start | bytes 147456 | tf_op jit(solution)/shard_map/reduce_scatter | solution.py:127
  7.3 11.2 %collective-permute-start.1 = (bf16[24,2048]{1,0:T(8,128)(2,1)}, bf16[24,2048]{1,0:T(8,128)(2,1)S(1)}, u32[]{:S(2)}, u32[]{:S(2)}) collective-permute-start(bf16[24,2048]{1,0:T(8,128)(2,1)} %param.12), channel_id=1, source_target_pairs={{0,4},{4,0},{2,6},{6,2},{8,12},{12,8},{10,14},{14,10},{16,20},{20,... | collective-permute-start | bytes 294920 | tf_op jit(solution)/shard_map/ppermute | solution.py:25
  10.3 54.2 %collective-permute-start = (bf16[8,128,256]{2,1,0:T(8,128)(2,1)}, bf16[8,128,256]{2,1,0:T(8,128)(2,1)S(1)}, u32[]{:S(2)}, u32[]{:S(2)}) collective-permute-start(bf16[8,128,256]{2,1,0:T(8,128)(2,1)} %param.13), channel_id=1, source_target_pairs={{0,2},{2,0},{4,6},{6,4},{8,10},{10,8},{12,14},{14,12},{16,18},{18,... | collective-permute-start | bytes 1572872 | tf_op jit(solution)/shard_map/ppermute | solution.py:25
  10.3 55.3 %collective-permute-start.4 = (bf16[8,128,256]{2,1,0:T(8,128)(2,1)}, bf16[8,128,256]{2,1,0:T(8,128)(2,1)S(1)}, u32[]{:S(2)}, u32[]{:S(2)}) collective-permute-start(bf16[8,128,256]{2,1,0:T(8,128)(2,1)} %param.14), channel_id=1, source_target_pairs={{0,2},{2,0},{4,6},{6,4},{8,10},{10,8},{12,14},{14,12},{16,18},{18,... | collective-permute-start | bytes 1572872 | tf_op jit(solution)/shard_map/ppermute | solution.py:25
  16.0 48.5 %copy-start.2 = (bf16[8,128,256]{2,1,0:T(8,128)(2,1)S(1)}, bf16[8,128,256]{2,1,0:T(8,128)(2,1)}, u32[]{:S(2)}) copy-start(bf16[8,128,256]{2,1,0:T(8,128)(2,1)} %param.13) | copy-start | bytes 1572868
  16.0 221.9 %reduce-scatter.5.cloned.1.call-start = ((), (), s32[]{:S(2)}) async-start(), calls=%async_computation.3 | async-start | bytes 589824 | tf_op jit(solution)/shard_map/reduce_scatter | solution.py:224
  18.4 33.8 %copy-start.5 = (bf16[3,8,16,128]{3,2,1,0:T(8,128)(2,1)}, bf16[3,8,16,128]{3,2,1,0:T(8,128)(2,1)S(1)}, u32[]{:S(2)}) copy-start(bf16[3,8,16,128]{3,2,1,0:T(8,128)(2,1)S(1)} %copy.55) | copy-start | bytes 294916
  18.5 34.8 %collective-permute-start.2 = (bf16[48,2048]{1,0:T(8,128)(2,1)S(1)}, bf16[48,2048]{1,0:T(8,128)(2,1)S(1)}, u32[]{:S(2)}, u32[]{:S(2)}) collective-permute-start(bf16[48,2048]{1,0:T(8,128)(2,1)S(1)} %maximum_select_fusion.3), channel_id=1, source_target_pairs={{0,8},{8,0},{2,10},{10,2},{4,12},{12,4},{6,14},{14,6},{16,24},{24,... | collective-permute-start | bytes 589832 | tf_op jit(solution)/shard_map/ppermute | solution.py:25
  27.4 38.2 %copy-start.3 = (bf16[8,128,256]{2,1,0:T(8,128)(2,1)S(1)}, bf16[8,128,256]{2,1,0:T(8,128)(2,1)}, u32[]{:S(2)}) copy-start(bf16[8,128,256]{2,1,0:T(8,128)(2,1)} %param.14) | copy-start | bytes 1572868
  27.6 24.6 %copy-start.7 = (bf16[24,512]{1,0:T(8,128)(2,1)}, bf16[24,512]{1,0:T(8,128)(2,1)S(1)}, u32[]{:S(2)}) copy-start(bf16[24,512]{1,0:T(8,128)(2,1)S(1)} %convert_element_type.76) | copy-start | bytes 73732
  27.6 7.7 %collective-permute-start.11 = (bf16[24,512]{1,0:T(8,128)(2,1)S(1)}, bf16[24,512]{1,0:T(8,128)(2,1)S(1)}, u32[]{:S(2)}, u32[]{:S(2)}) collective-permute-start(bf16[24,512]{1,0:T(8,128)(2,1)S(1)} %convert_element_type.76), channel_id=1, source_target_pairs={{0,28},{2,30},{1,29},{3,31}} | collective-permute-start | bytes 73736 | tf_op jit(solution)/shard_map/ppermute | solution.py:31
  33.8 2.9 %collective-permute-start.12 = (bf16[24,512]{1,0:T(8,128)(2,1)S(1)}, bf16[24,512]{1,0:T(8,128)(2,1)S(1)}, u32[]{:S(2)}, u32[]{:S(2)}) collective-permute-start(bf16[24,512]{1,0:T(8,128)(2,1)S(1)} %convert_element_type.76), channel_id=1, source_target_pairs={{0,24},{2,26},{4,28},{6,30},{1,25},{3,27},{5,29},{7,31}} | collective-permute-start | bytes 73736 | tf_op jit(solution)/shard_map/ppermute | solution.py:31
  35.3 2.8 %collective-permute-start.13 = (bf16[24,512]{1,0:T(8,128)(2,1)S(1)}, bf16[24,512]{1,0:T(8,128)(2,1)S(1)}, u32[]{:S(2)}, u32[]{:S(2)}) collective-permute-start(bf16[24,512]{1,0:T(8,128)(2,1)S(1)} %convert_element_type.76), channel_id=1, source_target_pairs={{0,20},{2,22},{4,24},{6,26},{8,28},{10,30},{1,21},{3,23},{5,25},{7... | collective-permute-start | bytes 73736 | tf_op jit(solution)/shard_map/ppermute | solution.py:31
  36.7 9.6 %collective-permute-start.14 = (bf16[24,512]{1,0:T(8,128)(2,1)S(1)}, bf16[24,512]{1,0:T(8,128)(2,1)S(1)}, u32[]{:S(2)}, u32[]{:S(2)}) collective-permute-start(bf16[24,512]{1,0:T(8,128)(2,1)S(1)} %convert_element_type.76), channel_id=1, source_target_pairs={{0,16},{2,18},{4,20},{6,22},{8,24},{10,26},{12,28},{14,30},{1,17},... | collective-permute-start | bytes 73736 | tf_op jit(solution)/shard_map/ppermute | solution.py:31
  38.1 9.7 %collective-permute-start.15 = (bf16[24,512]{1,0:T(8,128)(2,1)S(1)}, bf16[24,512]{1,0:T(8,128)(2,1)S(1)}, u32[]{:S(2)}, u32[]{:S(2)}) collective-permute-start(bf16[24,512]{1,0:T(8,128)(2,1)S(1)} %convert_element_type.76), channel_id=1, source_target_pairs={{0,12},{2,14},{4,16},{6,18},{8,20},{10,22},{12,24},{14,26},{16,28}... | collective-permute-start | bytes 73736 | tf_op jit(solution)/shard_map/ppermute | solution.py:31
  46.3 4.4 %collective-permute-start.16 = (bf16[24,512]{1,0:T(8,128)(2,1)S(1)}, bf16[24,512]{1,0:T(8,128)(2,1)S(1)}, u32[]{:S(2)}, u32[]{:S(2)}) collective-permute-start(bf16[24,512]{1,0:T(8,128)(2,1)S(1)} %convert_element_type.76), channel_id=1, source_target_pairs={{0,8},{2,10},{4,12},{6,14},{8,16},{10,18},{12,20},{14,22},{16,24},... | collective-permute-start | bytes 73736 | tf_op jit(solution)/shard_map/ppermute | solution.py:31
  47.8 4.4 %collective-permute-start.17 = (bf16[24,512]{1,0:T(8,128)(2,1)S(1)}, bf16[24,512]{1,0:T(8,128)(2,1)S(1)}, u32[]{:S(2)}, u32[]{:S(2)}) collective-permute-start(bf16[24,512]{1,0:T(8,128)(2,1)S(1)} %convert_element_type.76), channel_id=1, source_target_pairs={{0,4},{2,6},{4,8},{6,10},{8,12},{10,14},{12,16},{14,18},{16,20},{1... | collective-permute-start | bytes 73736 | tf_op jit(solution)/shard_map/ppermute | solution.py:31
  53.4 20.4 %collective-permute-start.3 = (bf16[96,2048]{1,0:T(8,128)(2,1)S(1)}, bf16[96,2048]{1,0:T(8,128)(2,1)S(1)}, u32[]{:S(2)}, u32[]{:S(2)}) collective-permute-start(bf16[96,2048]{1,0:T(8,128)(2,1)S(1)} %maximum_select_fusion.1), channel_id=1, source_target_pairs={{0,16},{16,0},{2,18},{18,2},{4,20},{20,4},{6,22},{22,6},{8,24},{24... | collective-permute-start | bytes 1179656 | tf_op jit(solution)/shard_map/ppermute | solution.py:25
  159.7 33.3 %copy-start.1 = (f32[192,2,8,128]{3,0,2,1:T(8,128)S(1)}, f32[192,2,8,128]{3,0,2,1:T(8,128)}, u32[]{:S(2)}) copy-start(f32[192,2,8,128]{3,0,2,1:T(8,128)} %get-tuple-element.143) | copy-start | bytes 4718596
  159.7 4.7 %collective-permute-start.18 = (f32[96,2,8]{0,2,1:T(8,128)S(1)}, f32[96,2,8]{0,2,1:T(8,128)S(1)}, u32[]{:S(2)}, u32[]{:S(2)}) collective-permute-start(f32[96,2,8]{0,2,1:T(8,128)S(1)} %slice_select_fusion.9), channel_id=1, source_target_pairs={{0,16},{16,0},{2,18},{18,2},{4,20},{20,4},{6,22},{22,6},{8,24},{24... | collective-permute-start | bytes 18440 | tf_op jit(solution)/shard_map/ppermute | solution.py:25
  159.8 4.8 %collective-permute-start.5 = (f32[96,2,8]{0,2,1:T(8,128)S(1)}, f32[96,2,8]{0,2,1:T(8,128)S(1)}, u32[]{:S(2)}, u32[]{:S(2)}) collective-permute-start(f32[96,2,8]{0,2,1:T(8,128)S(1)} %slice_select_fusion.10), channel_id=1, source_target_pairs={{0,16},{16,0},{2,18},{18,2},{4,20},{20,4},{6,22},{22,6},{8,24},{24... | collective-permute-start | bytes 18440 | tf_op jit(solution)/shard_map/ppermute | solution.py:25
  164.2 37.4 %copy-start.8 = (f32[24,192]{1,0:T(8,128)S(1)}, f32[24,192]{1,0:T(8,128)}, u32[]{:S(2)}) copy-start(f32[24,192]{1,0:T(8,128)} %get-tuple-element.243) | copy-start | bytes 55300
  164.2 28.7 %collective-permute-start.6 = (f32[96,2,8,128]{3,0,2,1:T(8,128)S(1)}, f32[96,2,8,128]{3,0,2,1:T(8,128)S(1)}, u32[]{:S(2)}, u32[]{:S(2)}) collective-permute-start(f32[96,2,8,128]{3,0,2,1:T(8,128)S(1)} %slice_select_fusion), channel_id=1, source_target_pairs={{0,16},{16,0},{2,18},{18,2},{4,20},{20,4},{6,22},{22,6},{8,24},{24... | collective-permute-start | bytes 2359304 | tf_op jit(solution)/shard_map/ppermute | solution.py:25
  164.8 9.3 %collective-permute-start.19 = (f32[48,2,8]{0,2,1:T(8,128)S(1)}, f32[48,2,8]{0,2,1:T(8,128)S(1)}, u32[]{:S(2)}, u32[]{:S(2)}) collective-permute-start(f32[48,2,8]{0,2,1:T(8,128)S(1)} %slice_select_fusion.4), channel_id=1, source_target_pairs={{0,8},{8,0},{2,10},{10,2},{4,12},{12,4},{6,14},{14,6},{16,24},{24,... | collective-permute-start | bytes 9224 | tf_op jit(solution)/shard_map/ppermute | solution.py:25
  168.0 6.2 %collective-permute-start.7 = (f32[48,2,8]{0,2,1:T(8,128)S(1)}, f32[48,2,8]{0,2,1:T(8,128)S(1)}, u32[]{:S(2)}, u32[]{:S(2)}) collective-permute-start(f32[48,2,8]{0,2,1:T(8,128)S(1)} %slice_select_fusion.7), channel_id=1, source_target_pairs={{0,8},{8,0},{2,10},{10,2},{4,12},{12,4},{6,14},{14,6},{16,24},{24,... | collective-permute-start | bytes 9224 | tf_op jit(solution)/shard_map/ppermute | solution.py:25
  174.4 27.1 %collective-permute-start.9 = (f32[24,2,8]{0,2,1:T(8,128)S(1)}, f32[24,2,8]{0,2,1:T(8,128)S(1)}, u32[]{:S(2)}, u32[]{:S(2)}) collective-permute-start(f32[24,2,8]{0,2,1:T(8,128)S(1)} %slice_select_fusion.5), channel_id=1, source_target_pairs={{0,4},{4,0},{2,6},{6,2},{8,12},{12,8},{10,14},{14,10},{16,20},{20,... | collective-permute-start | bytes 4616 | tf_op jit(solution)/shard_map/ppermute | solution.py:25
  192.9 24.1 %copy-start.6 = (bf16[192,2,1,128]{3,2,1,0:T(2,128)(2,1)S(1)}, bf16[192,2,1,128]{3,2,1,0:T(2,128)(2,1)}, u32[]{:S(2)}) copy-start(bf16[192,2,1,128]{3,2,1,0:T(2,128)(2,1)} %get-tuple-element.239) | copy-start | bytes 294916
  193.5 8.4 %collective-permute-start.8 = (f32[48,2,8,128]{3,0,2,1:T(8,128)S(1)}, f32[48,2,8,128]{3,0,2,1:T(8,128)S(1)}, u32[]{:S(2)}, u32[]{:S(2)}) collective-permute-start(f32[48,2,8,128]{3,0,2,1:T(8,128)S(1)} %slice_select_fusion.1), channel_id=1, source_target_pairs={{0,8},{8,0},{2,10},{10,2},{4,12},{12,4},{6,14},{14,6},{16,24},{24,... | collective-permute-start | bytes 1179656 | tf_op jit(solution)/shard_map/ppermute | solution.py:25
  193.6 19.2 %collective-permute-start.20 = (f32[24,2,8]{0,2,1:T(8,128)S(1)}, f32[24,2,8]{0,2,1:T(8,128)S(1)}, u32[]{:S(2)}, u32[]{:S(2)}) collective-permute-start(f32[24,2,8]{0,2,1:T(8,128)S(1)} %slice_select_fusion.3), channel_id=1, source_target_pairs={{0,4},{4,0},{2,6},{6,2},{8,12},{12,8},{10,14},{14,10},{16,20},{20,... | collective-permute-start | bytes 4616 | tf_op jit(solution)/shard_map/ppermute | solution.py:25
  202.1 14.9 %collective-permute-start.10 = (f32[24,2,8,128]{3,0,2,1:T(8,128)S(1)}, f32[24,2,8,128]{3,0,2,1:T(8,128)S(1)}, u32[]{:S(2)}, u32[]{:S(2)}) collective-permute-start(f32[24,2,8,128]{3,0,2,1:T(8,128)S(1)} %slice_select_fusion.2), channel_id=1, source_target_pairs={{0,4},{4,0},{2,6},{6,2},{8,12},{12,8},{10,14},{14,10},{16,20},{20,... | collective-permute-start | bytes 589832 | tf_op jit(solution)/shard_map/ppermute | solution.py:25
Sparse Core Ops, SparseCore 0:
  16.2 10.2 reduce-scatter.2
  226.4 11.5 reduce-scatter.4
where the time goes:
time: 248 us; the launch traced here: 246 us
  starting transfers between devices  70.9 us (29%)
  matrix products  63.8 us (26%)
  waiting for transfers between devices  47.7 us (19%)
  local copies, waits for them, and re-layouts  28.3 us (11%)
  other arithmetic  20.8 us (8%)
  between operations  14.6 us (6%)
    ppermute x14, starting transfers between devices, partner(): return lax.ppermute(block, axis, route)  48.4 us
    dot_general x9, matrix products, online_update(): jnp.einsum('tkgp,pkd->tkgd', weights.astype(jnp.bfloat16), values, prefer...  31.8 us
    ppermute x14, waiting for transfers between devices, partner(): return lax.ppermute(block, axis, route)  27.7 us
    ppermute x7, starting transfers between devices, passed_along(): return lax.ppermute(array, axis, pairs)  22.5 us
    dot_general x8, matrix products, slot_turn(): jnp.einsum('tkgd,pkd->tkgp', group_query, keys_now, preferred_element_typ...  16.7 us
    reduce_scatter x1, waiting for transfers between devices, local(): lax.psum_scatter(partial_out, 'tp', scatter_dimension=1, tiled=True)  11.7 us
    reduce_sum x9, other arithmetic, online_update(): totals = totals * factor + jnp.sum(weights, axis=-1)  10.7 us
    dot_general x1, matrix products, local(): jnp.dot(attended, out_weight, preferred_element_type=jnp.float32)  8.81 us
  transfers between devices with their start and end apart: 23, of which 12 were waited for; matrix products, arithmetic and copies ran while one was open for 7% of the time, Pallas kernels for 0%

commit v1 on v0

v1 whole, which is shorter than its diff:
```python
import functools
import math

import jax
import jax.numpy as jnp
from jax import lax
from jax.experimental import pallas as pl
from jax.experimental.pallas import tpu as pltpu
from jax.sharding import PartitionSpec as P

HD = 128
PAGE = 128
GROUPS = 2
REQS = 8
CHUNK = 4
LOW = -1e30
EXP2_SCALE = math.log2(math.e) / math.sqrt(HD)
F32 = jnp.float32
BF16 = jnp.bfloat16
MIB = 1 << 20

VMEM = pl.BlockSpec(memory_space=pltpu.VMEM)
SMEM = pl.BlockSpec(memory_space=pltpu.SMEM)
ANY = pl.BlockSpec(memory_space=pl.ANY)


def params(mib):
    return pltpu.CompilerParams(vmem_limit_bytes=mib * MIB)


def pack_pages(keys, values, place, splits):
    pages = keys.shape[0]

    def body(place_ref, *refs):
        half = len(refs) // 2
        for source, target in zip(refs[:half], refs[half:]):
            target[...] = source[...]

    def column(step):
        return pl.BlockSpec((pages, PAGE, HD), lambda i, place: (0, 0, place[1] ^ step))

    out = pl.BlockSpec((pages, PAGE, HD), lambda i, place: (0, 0, 0))
    shape = jax.ShapeDtypeStruct((pages, PAGE, HD), BF16)
    specs = [column(step) for step in range(splits) for _ in range(2)]
    return pl.pallas_call(
        body,
        grid_spec=pltpu.PrefetchScalarGridSpec(
            num_scalar_prefetch=1, grid=(1,), in_specs=specs, out_specs=[out] * (2 * splits)
        ),
        out_shape=[shape] * (2 * splits),
        compiler_params=params(16),
        cost_estimate=pl.CostEstimate(
            flops=0, bytes_accessed=4 * splits * pages * PAGE * HD * 2, transcendentals=0
        ),
    )(place, *([keys, values] * splits))


def finish_kv(mine, others, cosine, sine, heads):
    rows = mine.shape[0]

    def body(*refs):
        out = refs[-1]
        total = refs[0][...]
        for other in refs[1:-3]:
            total = total + other[...]
        cos, sin = refs[-3][...], refs[-2][...]
        for head in range(heads):
            key = total[:, head * 2 * HD : (head * 2 + 1) * HD]
            turned = key * cos + pltpu.roll(key, HD // 2, 1) * sin
            out[:, head * 2 * HD : (head * 2 + 1) * HD] = turned.astype(BF16)
            value = total[:, (head * 2 + 1) * HD : (head * 2 + 2) * HD]
            out[:, (head * 2 + 1) * HD : (head * 2 + 2) * HD] = value.astype(BF16)

    return pl.pallas_call(
        body,
        in_specs=[VMEM] * (3 + len(others)),
        out_specs=VMEM,
        out_shape=jax.ShapeDtypeStruct((rows, heads * 2 * HD), BF16),
    )(mine, *others, cosine, sine)


def collect_pages(page_table, place, sources, pages, splits):
    slots = pages * splits * GROUPS
    group_pages = page_table.shape[0] // GROUPS

    def body(table, place_ref, *refs):
        count = len(refs) - 7
        key_refs, value_refs = refs[0:count:2], refs[1:count:2]
        keys_out, values_out, number_out, keys, values, key_sem, value_sem = refs[count:]
        group, split = place_ref[0], place_ref[1]
        first = place_ref[2]

        def copies(which, page, at):
            rows = pl.ds(pl.multiple_of(at * PAGE, PAGE), PAGE)
            return (
                pltpu.make_async_copy(key_refs[which].at[page], keys.at[rows], key_sem.at[at]),
                pltpu.make_async_copy(
                    value_refs[which].at[page], values.at[rows, pl.ds(0, HD)], value_sem.at[at]
                ),
            )

        def look(i, number):
            slot = table[group * group_pages + i] - first
            here = jnp.logical_and(slot >= 0, slot < slots)

            @pl.when(here)
            def _():
                device = slot // pages
                page = slot - device * pages
                kind = jnp.bitwise_xor(device, split * GROUPS + group)
                for which in range(splits * GROUPS):

                    @pl.when(kind == which)
                    def _():
                        for copy in copies(which, page, number):
                            copy.start()

            return number + here.astype(jnp.int32)

        number = lax.fori_loop(0, group_pages, look, jnp.int32(0))
        number_out[0] = number
        values[:, HD:] = jnp.ones((slots * PAGE, HD), BF16)

        def clear(i, carry):
            rows = pl.ds(pl.multiple_of(i * PAGE, PAGE), PAGE)
            keys[rows, :] = jnp.zeros((PAGE, HD), BF16)
            values[rows, 0:HD] = jnp.zeros((PAGE, HD), BF16)
            return carry

        lax.fori_loop(number, slots, clear, 0)

        def land(i, carry):
            for copy in copies(0, 0, i):
                copy.wait()
            return carry

        lax.fori_loop(0, number, land, 0)
        keys_out[...] = keys[...]
        values_out[...] = values[...]

    return pl.pallas_call(
        body,
        in_specs=[SMEM, SMEM] + [ANY] * len(sources),
        out_specs=[VMEM, VMEM, SMEM],
        out_shape=[
            jax.ShapeDtypeStruct((slots * PAGE, HD), BF16),
            jax.ShapeDtypeStruct((slots * PAGE, 2 * HD), BF16),
            jax.ShapeDtypeStruct((1,), jnp.int32),
        ],
        scratch_shapes=[
            pltpu.VMEM((slots * PAGE, HD), BF16),
            pltpu.VMEM((slots * PAGE, 2 * HD), BF16),
            pltpu.SemaphoreType.DMA((slots,)),
            pltpu.SemaphoreType.DMA((slots,)),
        ],
        compiler_params=params(24),
    )(page_table, place, *sources)


def attend(number, lengths, place, far, query, suffix, keys, values, rows_each, splits):
    tokens = query.shape[0]
    heads = query.shape[1] // HD
    rows = tokens * heads
    slots = keys.shape[0] // PAGE
    chunks = -(-slots // CHUNK)
    wide = CHUNK * PAGE
    parts = -(-rows // HD)
    stat_rows = -(-3 * parts // 16) * 16

    def body(
        number_ref, len_ref, place_ref, query_ref, suffix_ref, keys_hbm, values_hbm, out,
        key_buf, value_buf, scores, top, total, column, stats, key_sem, value_sem,
    ):
        count = number_ref[0]
        turns = lax.div(count + (CHUNK - 1), CHUNK)

        def key_copy(c):
            span = pl.ds(pl.multiple_of(c * wide, wide), wide)
            return pltpu.make_async_copy(keys_hbm.at[span], key_buf.at[c], key_sem.at[c])

        def value_copy(c):
            span = pl.ds(pl.multiple_of(c * wide, wide), wide)
            return pltpu.make_async_copy(values_hbm.at[span], value_buf.at[c], value_sem.at[c])

        def begin(c, carry):
            key_copy(c).start()
            value_copy(c).start()
            return carry

        lax.fori_loop(0, turns, begin, 0)
        q = jnp.concatenate(
            [query_ref[:, h * HD : (h + 1) * HD].astype(F32) for h in range(heads)], axis=0
        ).astype(BF16)

        group, split = place_ref[0], place_ref[1]
        z_here = place_ref[3]
        z_query = jnp.bitwise_xor(z_here, far)

        def places(z, axis):
            index = lax.broadcasted_iota(jnp.int32, (tokens, tokens), axis)
            result = jnp.zeros((tokens, tokens), jnp.int32)
            for sub in range(splits):
                block = z * splits + jnp.bitwise_xor(split, sub)
                result = jnp.where(
                    index >= sub * rows_each, (block - sub) * rows_each + index, result
                )
            return result

        query_place, key_place = places(z_query, 0), places(z_here, 1)
        begins = jnp.zeros((tokens, tokens), jnp.int32)
        edge = jnp.int32(0)
        for r in range(REQS):
            edge = edge + len_ref[group, r]
            begins = jnp.where(query_place >= edge, edge, begins)
        seen = jnp.logical_and(key_place <= query_place, key_place >= begins)
        seen = jnp.concatenate([seen.astype(F32)] * heads, axis=0)
        own = lax.dot_general(
            q, suffix_ref[:, :HD], (((1,), (1,)), ((), ())), preferred_element_type=F32
        )
        own = jnp.where(seen > 0.0, own, LOW)
        top[...] = jnp.full((rows, HD), LOW, F32)

        def first_pass(c, carry):
            key_copy(c).wait()
            got = lax.dot_general(
                q, key_buf[c], (((1,), (1,)), ((), ())), preferred_element_type=F32
            )
            best = top[...]
            for j in range(CHUNK):
                piece = got[:, j * PAGE : (j + 1) * PAGE]
                piece = jnp.where(c * CHUNK + j < count, piece, LOW)
                scores[c, :, j * PAGE : (j + 1) * PAGE] = piece
                best = jnp.maximum(best, piece)
            top[...] = best
            return carry

        lax.fori_loop(0, turns, first_pass, 0)
        highest = jnp.maximum(
            jnp.max(top[...], axis=1, keepdims=True), jnp.max(own, axis=1, keepdims=True)
        )
        weights = jnp.exp2((own - highest) * EXP2_SCALE) * seen
        own_values = jnp.concatenate(
            [suffix_ref[:, HD : 2 * HD], jnp.ones((tokens, HD), BF16)], axis=1
        )
        total[...] = jnp.dot(weights.astype(BF16), own_values, preferred_element_type=F32)

        def second_pass(c, carry):
            value_copy(c).wait()
            weights = jnp.exp2((scores[c] - highest) * EXP2_SCALE).astype(BF16)
            total[...] += jnp.dot(weights, value_buf[c], preferred_element_type=F32)
            return carry

        lax.fori_loop(0, turns, second_pass, 0)
        sums = total[:, HD:]
        some = sums > 0.0
        safe = jnp.where(some, sums, 1.0)
        out[0:rows, :] = (total[:, :HD] / safe).astype(BF16)
        column[0:rows, :] = jnp.where(some, highest * EXP2_SCALE + jnp.log2(safe), LOW)
        stats[...] = jnp.zeros((stat_rows, HD), F32)
        for part in range(parts):
            line = column[part * HD : (part + 1) * HD, :].T[0:1, :]
            for piece in range(3):
                rounded = line.astype(BF16).astype(F32)
                stats[3 * part + piece : 3 * part + piece + 1, :] = rounded
                line = line - rounded
        out[rows : rows + stat_rows, :] = stats[...].astype(BF16)

    return pl.pallas_call(
        body,
        in_specs=[SMEM, SMEM, SMEM, VMEM, VMEM, ANY, ANY],
        out_specs=VMEM,
        out_shape=jax.ShapeDtypeStruct((rows + stat_rows, HD), BF16),
        scratch_shapes=[
            pltpu.VMEM((chunks, wide, HD), BF16),
            pltpu.VMEM((chunks, wide, 2 * HD), BF16),
            pltpu.VMEM((chunks, rows, wide), F32),
            pltpu.VMEM((rows, HD), F32),
            pltpu.VMEM((rows, 2 * HD), F32),
            pltpu.VMEM((parts * HD, HD), F32),
            pltpu.VMEM((stat_rows, HD), F32),
            pltpu.SemaphoreType.DMA((chunks,)),
            pltpu.SemaphoreType.DMA((chunks,)),
        ],
        compiler_params=params(32),
        cost_estimate=pl.CostEstimate(
            flops=2 * rows * slots * PAGE * HD,
            bytes_accessed=slots * PAGE * HD * 3,
            transcendentals=rows * slots * PAGE // 2,
        ),
    )(number, lengths, place, query, suffix, keys, values)


def project(place, partials, out_weight, rows_each, splits, ranks, heads):
    tokens = rows_each * splits
    rows = tokens * heads
    parts = -(-rows // HD)
    depth = heads * HD
    width = out_weight.shape[1] // ranks
    tile = min(width, 512)
    tiles = width // tile

    def body(place_ref, *refs):
        count = len(partials)
        partial_refs, weight_ref = refs[:count], refs[count]
        outs = refs[count + 1 : count + 1 + ranks * splits]
        merged, attended = refs[count + 1 + ranks * splits :]
        step = pl.program_id(0)

        @pl.when(step == 0)
        def _():
            for part in range(parts):
                length = min(HD, rows - part * HD)
                lines = []
                for ref in partial_refs:
                    stat = ref[rows:, :].astype(F32)
                    lines.append(
                        stat[3 * part : 3 * part + 1]
                        + stat[3 * part + 1 : 3 * part + 2]
                        + stat[3 * part + 2 : 3 * part + 3]
                    )
                best = functools.reduce(jnp.maximum, lines)
                shares = [jnp.exp2(line - best) for line in lines]
                whole = functools.reduce(jnp.add, shares)
                mixed = jnp.zeros((length, HD), F32)
                for share, ref in zip(shares, partial_refs):
                    factor = jnp.broadcast_to(share / whole, (HD, HD)).T[:length]
                    mixed = mixed + factor * ref[part * HD : part * HD + length, :].astype(F32)
                merged[part * HD : part * HD + length, :] = mixed
            for h in range(heads):
                attended[:, h * HD : (h + 1) * HD] = merged[
                    h * tokens : (h + 1) * tokens, :
                ].astype(BF16)

        product = jnp.dot(attended[...], weight_ref[...], preferred_element_type=F32)
        for rank in range(ranks):

            @pl.when(step // tiles == ranks - 1 - rank)
            def _():
                for sub in range(splits):
                    out = outs[rank * splits + sub]
                    piece = product[sub * rows_each : (sub + 1) * rows_each]
                    out[...] = piece.astype(out.dtype)

    def weight_at(i, place):
        rank = jnp.bitwise_xor(ranks - 1 - i // tiles, place[4])
        return (place[1], rank * tiles + i % tiles)

    def out_at(rank):
        def index(i, place):
            return (0, jnp.clip(i - (ranks - 1 - rank) * tiles, 0, tiles - 1))

        return index

    outs = [(rank, sub) for rank in range(ranks) for sub in range(splits)]
    whole_partial = pl.BlockSpec(partials[0].shape, lambda i, place: (0, 0))
    return pl.pallas_call(
        body,
        grid_spec=pltpu.PrefetchScalarGridSpec(
            num_scalar_prefetch=1,
            grid=(ranks * tiles,),
            in_specs=[whole_partial] * len(partials) + [pl.BlockSpec((depth, tile), weight_at)],
            out_specs=[pl.BlockSpec((rows_each, tile), out_at(rank)) for rank, _ in outs],
            scratch_shapes=[pltpu.VMEM((rows, HD), F32), pltpu.VMEM((tokens, depth), BF16)],
        ),
        out_shape=[
            jax.ShapeDtypeStruct((rows_each, width), F32 if pair == (0, 0) else BF16)
            for pair in outs
        ],
        compiler_params=params(32),
        cost_estimate=pl.CostEstimate(
            flops=2 * tokens * depth * width * ranks,
            bytes_accessed=depth * width * ranks * 2,
            transcendentals=0,
        ),
    )(place, *partials, out_weight)


def local(
    hidden_in,
    kv_weight,
    queries,
    prefix_keys,
    prefix_values,
    page_table,
    suffix_lengths,
    out_weight,
):
    rows = hidden_in.shape[0]
    seq_count, ranks = lax.axis_size("seq"), lax.axis_size("tp")
    seq_rank, tp_rank = lax.axis_index("seq"), lax.axis_index("tp")
    pages = prefix_keys.shape[0]
    splits = prefix_keys.shape[2] // HD
    heads = queries.shape[1] // HD // splits
    prefix_len = pages * seq_count // GROUPS * PAGE
    blocks = seq_count // GROUPS
    depth = blocks // splits
    group = seq_rank % GROUPS
    block = seq_rank // GROUPS
    split = block % splits
    place = jnp.stack(
        [group, split, (block - split) * GROUPS * pages, block // splits, tp_rank]
    ).astype(jnp.int32)

    def across(array, far=0, side=0, core=0):
        step = (far * splits + side) * GROUPS + core
        return lax.ppermute(array, "seq", [(i, i ^ step) for i in range(seq_count)])

    def columns(array, index, width):
        return lax.dynamic_slice_in_dim(array, index * width, width, 1)

    parts = [columns(queries, split, heads * HD)]
    for side in range(1, splits):
        parts.append(across(columns(queries, split ^ side, heads * HD), side=side))
    my_query = jnp.concatenate(parts, axis=0)

    packed = pack_pages(prefix_keys, prefix_values, place, splits)
    sources = []
    for side in range(splits):
        keys, values = packed[2 * side], packed[2 * side + 1]
        if side:
            keys, values = across(keys, side=side), across(values, side=side)
        sources += [keys, values, across(keys, core=1), across(values, core=1)]
    far_queries = [my_query] + [across(my_query, far=far) for far in range(1, depth)]

    partial = jnp.dot(hidden_in, kv_weight, preferred_element_type=F32)
    width = splits * 2 * HD
    others = []
    for rank in range(1, ranks):
        piece = columns(partial, tp_rank ^ rank, width)
        others.append(lax.ppermute(piece, "tp", [(i, i ^ rank) for i in range(ranks)]))
    within = block * rows + jnp.arange(rows, dtype=jnp.int32)
    lengths = jnp.sum(
        jnp.where(jnp.arange(GROUPS)[:, None] == group, suffix_lengths, 0), axis=0
    )
    ends = jnp.sum(
        jnp.where(jnp.arange(REQS)[None, :] <= jnp.arange(REQS)[:, None], lengths[None, :], 0),
        axis=1,
    )
    begins = jnp.max(jnp.where(within[:, None] >= ends[None, :], ends[None, :], 0), axis=1)
    positions = prefix_len + within - begins
    half = HD // 2
    frequency = jnp.power(500000.0, -(jnp.arange(half, dtype=F32) * 2.0 / HD))
    angles = positions.astype(F32)[:, None] * frequency[None, :]
    cosine, sine = jnp.cos(angles), jnp.sin(angles)
    cosine = jnp.concatenate([cosine, cosine], axis=1)
    sine = jnp.concatenate([-sine, sine], axis=1)
    new_pages = finish_kv(columns(partial, tp_rank, width), others, cosine, sine, splits)
    suffix = [columns(new_pages, split, 2 * HD)]
    for side in range(1, splits):
        suffix.append(across(columns(new_pages, split ^ side, 2 * HD), side=side))
    suffix = jnp.concatenate(suffix, axis=0)

    keys, values, number = collect_pages(page_table, place, sources, pages, splits)
    returned = []
    for far in range(depth - 1, -1, -1):
        partial_sum = attend(
            number, suffix_lengths, place, far, far_queries[far], suffix, keys, values, rows, splits
        )
        returned.append(across(partial_sum, far=far) if far else partial_sum)

    products = project(place, returned, out_weight, rows, splits, ranks, heads)
    hidden = products[0]
    for rank in range(ranks - 1, -1, -1):
        for side in range(splits - 1, -1, -1):
            if rank or side:
                step = side * GROUPS
                route = [
                    (i * ranks + j, (i ^ step) * ranks + (j ^ rank))
                    for i in range(seq_count)
                    for j in range(ranks)
                ]
                got = lax.ppermute(products[rank * splits + side], ("seq", "tp"), route)
                hidden = hidden + got.astype(F32)
    return (hidden.astype(BF16), new_pages)


def solution(mesh):
    return jax.shard_map(
        local,
        mesh=mesh,
        in_specs=(
            P("seq", "tp"),
            P("tp", None),
            P("seq", "tp"),
            P("seq", None, "tp"),
            P("seq", None, "tp"),
            P(),
            P(),
            P("tp", None),
        ),
        out_specs=(P("seq", "tp"), P("seq", "tp")),
        check_vma=False,
    )
```

time: 248 us -> 80 us (0.32)
  matrix products: 63.8 us -> 4.59 us
  starting transfers between devices: 70.9 us -> 26 us
  waiting for transfers between devices: 47.7 us -> 7.28 us
  Pallas kernels: 0 us -> 30.5 us
  other arithmetic: 20.8 us -> 1.83 us
  local copies, waits for them, and re-layouts: 28.3 us -> 9.34 us
  between operations: 14.6 us -> 0.88 us
    dot_general x20 -> x1, matrix products: 63.8 us -> 4.59 us  [local(): partial = jnp.dot(hidden_in, kv_weight, preferred_element_type=F32)]
    ppermute x21 -> x18, starting transfers between devices: 70.8 us -> 26 us  [the longest x14 20.5 us: across(): return lax.ppermute(array, 'seq', [(i, i ^ step) for i in range(seq_count)])]
    pallas_call x0 -> x8, Pallas kernels: none -> 30.5 us  [the longest x4 19.6 us: attend(): pl.pallas_call(body, in_specs=[SMEM, SMEM, SMEM, VMEM, VMEM, ANY, ANY], o...]
    ppermute x21 -> x18, waiting for transfers between devices: 29.6 us -> 7.28 us  [the longest x3 3.91 us: local(): got = lax.ppermute(products[rank * splits + side], ('seq', 'tp'), route)]
    reduce_scatter x2 -> x0, waiting for transfers between devices: 18 us -> none  [the longest x1 11.7 us: local(): lax.psum_scatter(partial_out, 'tp', scatter_dimension=1, tiled=True)]
    dynamic_slice x16 -> x3, local copies, waits for them, and re-layouts: 13.9 us -> 1.38 us  [columns(): return lax.dynamic_slice_in_dim(array, index * width, width, 1)]
    reshape x18 -> x0, local copies, waits for them, and re-layouts: 11.9 us -> none  [the longest x8 5.52 us: slot_turn(): lax.dynamic_slice_in_dim(both_keys, offset_row, turn_pages, 0)]
    reduce_sum x14 -> x2, other arithmetic: 11 us -> 0.2 us  [the longest x1 0.12 us: local(): jnp.sum(jnp.where(jnp.arange(REQS)[None, :] <= jnp.arange(REQS)[:, None],...]
  transfers between devices with their start and end apart: 23 -> 18, of which waited for: 12 -> 5; matrix products, arithmetic and copies ran while one was open for 7% -> 9% of each run, Pallas kernels for 0% -> 31%
where the time goes in v1:
time: 80 us; the launch traced here: 80.4 us
  Pallas kernels  30.5 us (38%)
  starting transfers between devices  26 us (32%)
  local copies, waits for them, and re-layouts  9.34 us (12%)
  waiting for transfers between devices  7.28 us (9%)
  matrix products  4.59 us (6%)
  other arithmetic  1.83 us (2%)
  between operations  0.88 us (1%)
    ppermute x14, starting transfers between devices, across(): return lax.ppermute(array, 'seq', [(i, i ^ step) for i in range(seq_count)])  20.5 us
    pallas_call x4, Pallas kernels, attend(): pl.pallas_call(body, in_specs=[SMEM, SMEM, SMEM, VMEM, VMEM, ANY, ANY], o...  19.6 us
    unnamed x16, local copies, waits for them, and re-layouts  7.88 us
    dot_general x1, matrix products, local(): partial = jnp.dot(hidden_in, kv_weight, preferred_element_type=F32)  4.59 us
    pallas_call x1, Pallas kernels, project(): pl.pallas_call(body, grid_spec=pltpu.PrefetchScalarGridSpec(num_scalar_pr...  4.39 us
    pallas_call x1, Pallas kernels, collect_pages(): pl.pallas_call(body, in_specs=[SMEM, SMEM] + [ANY] * len(sources), out_sp...  4.16 us
    ppermute x3, waiting for transfers between devices, local(): got = lax.ppermute(products[rank * splits + side], ('seq', 'tp'), route)  3.91 us
    ppermute x3, starting transfers between devices, local(): got = lax.ppermute(products[rank * splits + side], ('seq', 'tp'), route)  3.55 us
  transfers between devices with their start and end apart: 18, of which 5 were waited for; matrix products, arithmetic and copies ran while one was open for 9% of the time, Pallas kernels for 31%

profile of v1, /device:TPU:0, one launch (start us, length us, event | category | flops | bytes accessed | tf_op | source)
XLA Modules:
  0.0 80.4 jit_solution(10690138832327291625)
XLA Ops:
  0.6 0.0 copy-start
  0.7 0.1 stack.23.place_ref
  0.8 1.0 %copy-done.2 = bf16[8,128,256]{2,1,0:T(8,128)(2,1)S(1)} copy-done((bf16[8,128,256]{2,1,0:T(8,128)(2,1)S(1)}, bf16[8,128,256]{2,1,0:T(8,128)(2,1)}, u32[]{:S(2)}) %copy-start.2) | copy-done | bytes 524312
  1.8 1.0 %copy-done.3 = bf16[8,128,256]{2,1,0:T(8,128)(2,1)S(1)} copy-done((bf16[8,128,256]{2,1,0:T(8,128)(2,1)S(1)}, bf16[8,128,256]{2,1,0:T(8,128)(2,1)}, u32[]{:S(2)}) %copy-start.3) | copy-done | bytes 524312
  2.9 0.8 shard_map.95
  3.7 0.0 copy-start.4
  3.7 0.0 copy-start.6
  3.7 3.0 %collective-permute-start.2 = (bf16[8,128,128]{2,1,0:T(8,128)(2,1)S(1)}, bf16[8,128,128]{2,1,0:T(8,128)(2,1)S(1)}, u32[]{:S(2)}, u32[]{:S(2)}) collective-permute-start(bf16[8,128,128]{2,1,0:T(8,128)(2,1)S(1)} %get-tuple-element.15), channel_id=1, source_target_pairs={{0,4},{2,6},{4,0},{6,2},{8,12},{10,14},{12,8},{14,10},{16,20},{18,... | collective-permute-start | bytes 786440 | tf_op jit(solution)/shard_map/ppermute | solution.py:406
  6.7 0.1 collective-permute-start.3
  6.8 0.0 collective-permute-start
  6.8 0.5 collective-permute-start.1
  7.3 4.6 %fusion.1 = f32[24,1024]{1,0:T(8,128)S(1)} fusion(bf16[24,4096]{1,0:T(8,128)(2,1)S(1)} %copy-done, bf16[4096,1024]{1,0:T(8,128)(2,1)} %param.9), kind=kOutput, calls=%fused_computation.22 | convolution fusion | flops 201326592 | bytes 8683520 | tf_op jit(solution)/shard_map/dot_general | solution.py:425
  11.9 0.6 constant_dynamic-slice_fusion.2
  12.5 1.9 %collective-permute-start.8 = (f32[24,512]{1,0:T(8,128)S(1)}, f32[24,512]{1,0:T(8,128)S(1)}, u32[]{:S(2)}, u32[]{:S(2)}) collective-permute-start(f32[24,512]{1,0:T(8,128)S(1)} %get-tuple-element.24), channel_id=1, source_target_pairs={{0,1},{1,0},{2,3},{3,2},{4,5},{5,4},{6,7},{7,6},{8,9},{9,8},{10,11... | collective-permute-start | bytes 147464 | tf_op jit(solution)/shard_map/ppermute | solution.py:430
  14.5 0.1 select_reduce_fusion.2
  14.6 0.1 select_reduce_fusion.1
  14.7 0.1 select_reduce_fusion
  14.8 0.1 fusion
  15.0 0.7 pad_maximum_fusion.2
  15.7 1.0 %collective-permute-done.8.refs_1_ = f32[24,512]{1,0:T(8,128)S(1)} collective-permute-done((f32[24,512]{1,0:T(8,128)S(1)}, f32[24,512]{1,0:T(8,128)S(1)}, u32[]{:S(2)}, u32[]{:S(2)}) %collective-permute-start.8) | collective-permute-done | bytes 49184 | tf_op jit(solution)/shard_map/ppermute | solution.py:430
  16.6 1.9 %collective-permute-start.6 = (bf16[24,1024]{1,0:T(8,128)(2,1)S(1)}, bf16[24,1024]{1,0:T(8,128)(2,1)S(1)}, u32[]{:S(2)}, u32[]{:S(2)}) collective-permute-start(bf16[24,1024]{1,0:T(8,128)(2,1)S(1)} %get-tuple-element.27), channel_id=1, source_target_pairs={{0,4},{2,6},{4,0},{6,2},{8,12},{10,14},{12,8},{14,10},{16,20},{18,... | collective-permute-start | bytes 147464 | tf_op jit(solution)/shard_map/ppermute | solution.py:406
  18.6 1.5 %shard_map.97 = bf16[24,512]{1,0:T(8,128)(2,1)} custom-call(f32[24,512]{1,0:T(8,128)} %get-tuple-element.25.refs_0_, f32[24,512]{1,0:T(8,128)} %copy-done.7, f32[24,128]{1,0:T(8,128)} %get-tuple-element.33.refs_2_, f32[24,128]{1,0:T(8,128)} %get-tuple-element.34.refs_3_), custom_call_target="tpu_custom_call" | custom-call | tf_op jit(solution)/shard_map/pallas_call | solution.py:74
  20.1 0.0 collective-permute-done.2.refs_4_
  20.1 0.5 collective-permute-start.5
  20.6 0.7 constant_dynamic-slice_fusion
  21.3 1.3 %collective-permute-start.9 = (bf16[24,256]{1,0:T(8,128)(2,1)S(1)}, bf16[24,256]{1,0:T(8,128)(2,1)S(1)}, u32[]{:S(2)}, u32[]{:S(2)}) collective-permute-start(bf16[24,256]{1,0:T(8,128)(2,1)S(1)} %get-tuple-element.29), channel_id=1, source_target_pairs={{0,4},{2,6},{4,0},{6,2},{8,12},{10,14},{12,8},{14,10},{16,20},{18,... | collective-permute-start | bytes 36872 | tf_op jit(solution)/shard_map/ppermute | solution.py:406
  22.7 2.4 %collective-permute-done.9 = bf16[24,256]{1,0:T(8,128)(2,1)S(1)} collective-permute-done((bf16[24,256]{1,0:T(8,128)(2,1)S(1)}, bf16[24,256]{1,0:T(8,128)(2,1)S(1)}, u32[]{:S(2)}, u32[]{:S(2)}) %collective-permute-start.9) | collective-permute-done | bytes 12320 | tf_op jit(solution)/shard_map/ppermute | solution.py:406
  25.0 1.6 %collective-permute-start.13 = (bf16[48,1024]{1,0:T(8,128)(2,1)S(1)}, bf16[48,1024]{1,0:T(8,128)(2,1)S(1)}, u32[]{:S(2)}, u32[]{:S(2)}) collective-permute-start(bf16[48,1024]{1,0:T(8,128)(2,1)S(1)} %pad_maximum_fusion.query_ref), channel_id=1, source_target_pairs={{0,8},{2,10},{4,12},{6,14},{8,0},{10,2},{12,4},{14,6},{16,24},{18,... | collective-permute-start | bytes 294920 | tf_op jit(solution)/shard_map/ppermute | solution.py:406
  26.6 2.6 %collective-permute-start.11 = (bf16[48,1024]{1,0:T(8,128)(2,1)S(1)}, bf16[48,1024]{1,0:T(8,128)(2,1)S(1)}, u32[]{:S(2)}, u32[]{:S(2)}) collective-permute-start(bf16[48,1024]{1,0:T(8,128)(2,1)S(1)} %pad_maximum_fusion.query_ref), channel_id=1, source_target_pairs={{0,16},{2,18},{4,20},{6,22},{8,24},{10,26},{12,28},{14,30},{16,0},... | collective-permute-start | bytes 294920 | tf_op jit(solution)/shard_map/ppermute | solution.py:406
  29.2 0.2 collective-permute-start.7
  29.5 4.2 %shard_map.96 = (bf16[4096,128]{1,0:T(8,128)(2,1)S(1)}, bf16[4096,256]{1,0:T(8,128)(2,1)S(1)}, s32[1]{0:T(128)}) custom-call(s32[128]{0:T(128)S(1)} %copy-done.5, s32[5]{0:T(128)S(1)} %stack.23.place_ref, bf16[8,128,128]{2,1,0:T(8,128)(2,1)S(1)} %get-tuple-element.13.refs_0_, bf16[8,128,128]{2,1,0:T(8,128)(2,1)S(1)} %get-tuple-element.14.refs_1_, ...), custom_call_target="tpu_custom_call" | custom-call | tf_op jit(solution)/shard_map/pallas_call | solution.py:141
  33.6 4.9 %shard_map.100 = bf16[400,128]{1,0:T(8,128)(2,1)S(1)} custom-call(s32[1]{0:T(128)} %get-tuple-element.17.number_ref, s32[2,8]{1,0:T(2,128)S(1)} %copy-done.4, s32[5]{0:T(128)S(1)} %stack.23.place_ref, bf16[48,1024]{1,0:T(8,128)(2,1)S(1)} %collective-permute-done.13.query_ref, bf16[48,256]{1,0:T(8,128)(2,1)S(1)} %pad_maximum_fusion.1.suffix_ref, ...), custom_call_target="tpu_custom_call" | custom-call | flops 402653184 | bytes 1572864 | tf_op jit(solution)/shard_map/pallas_call | solution.py:268
  38.6 0.6 collective-permute-start.14
  39.2 4.9 %shard_map.99 = bf16[400,128]{1,0:T(8,128)(2,1)S(1)} custom-call(s32[1]{0:T(128)} %get-tuple-element.17.number_ref, s32[2,8]{1,0:T(2,128)S(1)} %copy-done.4, s32[5]{0:T(128)S(1)} %stack.23.place_ref, bf16[48,1024]{1,0:T(8,128)(2,1)S(1)} %collective-permute-done.11.query_ref, bf16[48,256]{1,0:T(8,128)(2,1)S(1)} %pad_maximum_fusion.1.suffix_ref, ...), custom_call_target="tpu_custom_call" | custom-call | flops 402653184 | bytes 1572864 | tf_op jit(solution)/shard_map/pallas_call | solution.py:268
  44.1 5.6 %collective-permute-start.12 = (bf16[400,128]{1,0:T(8,128)(2,1)S(1)}, bf16[400,128]{1,0:T(8,128)(2,1)S(1)}, u32[]{:S(2)}, u32[]{:S(2)}) collective-permute-start(bf16[400,128]{1,0:T(8,128)(2,1)S(1)} %shard_map.99), channel_id=1, source_target_pairs={{0,16},{2,18},{4,20},{6,22},{8,24},{10,26},{12,28},{14,30},{16,0},... | collective-permute-start | bytes 307208 | tf_op jit(solution)/shard_map/ppermute | solution.py:406
  49.7 4.9 %shard_map.98 = bf16[400,128]{1,0:T(8,128)(2,1)S(1)} custom-call(s32[1]{0:T(128)} %get-tuple-element.17.number_ref, s32[2,8]{1,0:T(2,128)S(1)} %copy-done.4, s32[5]{0:T(128)S(1)} %stack.23.place_ref, bf16[48,1024]{1,0:T(8,128)(2,1)S(1)} %collective-permute-done.7.query_ref, bf16[48,256]{1,0:T(8,128)(2,1)S(1)} %pad_maximum_fusion.1.suffix_ref, ...), custom_call_target="tpu_custom_call" | custom-call | flops 402653184 | bytes 1572864 | tf_op jit(solution)/shard_map/pallas_call | solution.py:268
  54.6 2.5 %collective-permute-start.10 = (bf16[400,128]{1,0:T(8,128)(2,1)S(1)}, bf16[400,128]{1,0:T(8,128)(2,1)S(1)}, u32[]{:S(2)}, u32[]{:S(2)}) collective-permute-start(bf16[400,128]{1,0:T(8,128)(2,1)S(1)} %shard_map.98), channel_id=1, source_target_pairs={{0,24},{2,26},{4,28},{6,30},{8,16},{10,18},{12,20},{14,22},{16,8},... | collective-permute-start | bytes 307208 | tf_op jit(solution)/shard_map/ppermute | solution.py:406
  57.1 4.9 %shard_map.101.refs_3_ = bf16[400,128]{1,0:T(8,128)(2,1)S(1)} custom-call(s32[1]{0:T(128)} %get-tuple-element.17.number_ref, s32[2,8]{1,0:T(2,128)S(1)} %copy-done.4, s32[5]{0:T(128)S(1)} %stack.23.place_ref, bf16[48,1024]{1,0:T(8,128)(2,1)S(1)} %pad_maximum_fusion.query_ref, bf16[48,256]{1,0:T(8,128)(2,1)S(1)} %pad_maximum_fusion.1.suffix_ref, ...), custom_call_target="tpu_custom_call" | custom-call | flops 402653184 | bytes 1572864 | tf_op jit(solution)/shard_map/pallas_call | solution.py:268
  62.0 0.0 copy-start.1
  62.0 5.8 %copy-done.1 = bf16[2048,4096]{1,0:T(8,128)(2,1)S(1)} copy-done((bf16[2048,4096]{1,0:T(8,128)(2,1)S(1)}, bf16[2048,4096]{1,0:T(8,128)(2,1)}, u32[]{:S(2)}) %copy-start.1) | copy-done | bytes 16777240
  67.8 4.4 %shard_map.102 = (f32[24,2048]{1,0:T(8,128)S(1)}, bf16[24,2048]{1,0:T(8,128)(2,1)S(1)}, bf16[24,2048]{1,0:T(8,128)(2,1)S(1)}, bf16[24,2048]{1,0:T(8,128)(2,1)S(1)}) custom-call(s32[5]{0:T(128)S(1)} %stack.23.place_ref, bf16[400,128]{1,0:T(8,128)(2,1)S(1)} %collective-permute-done.10.refs_0_, bf16[400,128]{1,0:T(8,128)(2,1)S(1)} %collective-permute-done.12.refs_1_, ...), custom_call_target="tpu_custom_call" | custom-call | flops 402653184 | bytes 8388608 | tf_op jit(solution)/shard_map/pallas_call | solution.py:356
  72.2 2.3 %collective-permute-start.15 = (bf16[24,2048]{1,0:T(8,128)(2,1)S(1)}, bf16[24,2048]{1,0:T(8,128)(2,1)S(1)}, u32[]{:S(2)}, u32[]{:S(2)}) collective-permute-start(bf16[24,2048]{1,0:T(8,128)(2,1)S(1)} %get-tuple-element.21), channel_id=1, source_target_pairs={{0,5},{1,4},{2,7},{3,6},{4,1},{5,0},{6,3},{7,2},{8,13},{9,12},{10,... | collective-permute-start | bytes 294920 | tf_op jit(solution)/shard_map/ppermute | solution.py:472
  74.5 0.5 collective-permute-start.16
  75.1 0.7 collective-permute-start.17
  75.8 2.0 %collective-permute-done.15 = bf16[24,2048]{1,0:T(8,128)(2,1)S(1)} collective-permute-done((bf16[24,2048]{1,0:T(8,128)(2,1)S(1)}, bf16[24,2048]{1,0:T(8,128)(2,1)S(1)}, u32[]{:S(2)}, u32[]{:S(2)}) %collective-permute-start.15) | collective-permute-done | bytes 98336 | tf_op jit(solution)/shard_map/ppermute | solution.py:472
  77.8 1.4 %collective-permute-done.16 = bf16[24,2048]{1,0:T(8,128)(2,1)S(1)} collective-permute-done((bf16[24,2048]{1,0:T(8,128)(2,1)S(1)}, bf16[24,2048]{1,0:T(8,128)(2,1)S(1)}, u32[]{:S(2)}, u32[]{:S(2)}) %collective-permute-start.16) | collective-permute-done | bytes 98336 | tf_op jit(solution)/shard_map/ppermute | solution.py:472
  79.1 0.5 collective-permute-done.17
  79.7 0.7 add_convert_fusion
  (29 shorter events, 0.1 us)
Async XLA Ops:
  0.6 6.7 %copy-start = (bf16[24,4096]{1,0:T(8,128)(2,1)S(1)}, bf16[24,4096]{1,0:T(8,128)(2,1)}, u32[]{:S(2)}) copy-start(bf16[24,4096]{1,0:T(8,128)(2,1)} %param.8) | copy-start | bytes 589828
  0.8 1.0 %copy-start.2 = (bf16[8,128,256]{2,1,0:T(8,128)(2,1)S(1)}, bf16[8,128,256]{2,1,0:T(8,128)(2,1)}, u32[]{:S(2)}) copy-start(bf16[8,128,256]{2,1,0:T(8,128)(2,1)} %refs_2_.1) | copy-start | bytes 1572868
  1.8 1.0 %copy-start.3 = (bf16[8,128,256]{2,1,0:T(8,128)(2,1)S(1)}, bf16[8,128,256]{2,1,0:T(8,128)(2,1)}, u32[]{:S(2)}) copy-start(bf16[8,128,256]{2,1,0:T(8,128)(2,1)} %refs_3_.1) | copy-start | bytes 1572868
  3.7 10.8 %copy-start.4 = (s32[2,8]{1,0:T(2,128)S(1)}, s32[2,8]{1,0:T(2,128)}, u32[]{:S(2)}) copy-start(s32[2,8]{1,0:T(2,128)} %len_ref.7) | copy-start | bytes 196
  3.7 11.3 %copy-start.6 = (bf16[24,2048]{1,0:T(8,128)(2,1)S(1)}, bf16[24,2048]{1,0:T(8,128)(2,1)}, u32[]{:S(2)}) copy-start(bf16[24,2048]{1,0:T(8,128)(2,1)} %param.10) | copy-start | bytes 294916
  3.7 16.4 %collective-permute-start.2 = (bf16[8,128,128]{2,1,0:T(8,128)(2,1)S(1)}, bf16[8,128,128]{2,1,0:T(8,128)(2,1)S(1)}, u32[]{:S(2)}, u32[]{:S(2)}) collective-permute-start(bf16[8,128,128]{2,1,0:T(8,128)(2,1)S(1)} %get-tuple-element.15), channel_id=1, source_target_pairs={{0,4},{2,6},{4,0},{6,2},{8,12},{10,14},{12,8},{14,10},{16,20},{18,... | collective-permute-start | bytes 786440 | tf_op jit(solution)/shard_map/ppermute | solution.py:406
  6.7 13.4 %collective-permute-start.3 = (bf16[8,128,128]{2,1,0:T(8,128)(2,1)S(1)}, bf16[8,128,128]{2,1,0:T(8,128)(2,1)S(1)}, u32[]{:S(2)}, u32[]{:S(2)}) collective-permute-start(bf16[8,128,128]{2,1,0:T(8,128)(2,1)S(1)} %get-tuple-element.16), channel_id=1, source_target_pairs={{0,4},{2,6},{4,0},{6,2},{8,12},{10,14},{12,8},{14,10},{16,20},{18,... | collective-permute-start | bytes 786440 | tf_op jit(solution)/shard_map/ppermute | solution.py:406
  6.8 19.8 %collective-permute-start = (bf16[8,128,128]{2,1,0:T(8,128)(2,1)S(1)}, bf16[8,128,128]{2,1,0:T(8,128)(2,1)S(1)}, u32[]{:S(2)}, u32[]{:S(2)}) collective-permute-start(bf16[8,128,128]{2,1,0:T(8,128)(2,1)S(1)} %get-tuple-element.13.refs_0_), channel_id=1, source_target_pairs={{0,2},{2,0},{4,6},{6,4},{8,10},{10,8},{12,14},{14,12},{16,18},{18,... | collective-permute-start | bytes 786440 | tf_op jit(solution)/shard_map/ppermute | solution.py:406
  6.8 22.4 %collective-permute-start.1 = (bf16[8,128,128]{2,1,0:T(8,128)(2,1)S(1)}, bf16[8,128,128]{2,1,0:T(8,128)(2,1)S(1)}, u32[]{:S(2)}, u32[]{:S(2)}) collective-permute-start(bf16[8,128,128]{2,1,0:T(8,128)(2,1)S(1)} %get-tuple-element.14.refs_1_), channel_id=1, source_target_pairs={{0,2},{2,0},{4,6},{6,4},{8,10},{10,8},{12,14},{14,12},{16,18},{18,... | collective-permute-start | bytes 786440 | tf_op jit(solution)/shard_map/ppermute | solution.py:406
  7.3 22.1 %copy-start.5 = (s32[128]{0:T(128)S(1)}, s32[128]{0:T(128)}, u32[]{:S(2)}) copy-start(s32[128]{0:T(128)} %table.1) | copy-start | bytes 1540
  12.5 4.1 %collective-permute-start.8 = (f32[24,512]{1,0:T(8,128)S(1)}, f32[24,512]{1,0:T(8,128)S(1)}, u32[]{:S(2)}, u32[]{:S(2)}) collective-permute-start(f32[24,512]{1,0:T(8,128)S(1)} %get-tuple-element.24), channel_id=1, source_target_pairs={{0,1},{1,0},{2,3},{3,2},{4,5},{5,4},{6,7},{7,6},{8,9},{9,8},{10,11... | collective-permute-start | bytes 147464 | tf_op jit(solution)/shard_map/ppermute | solution.py:430
  16.6 2.0 %copy-start.7 = (f32[24,512]{1,0:T(8,128)}, f32[24,512]{1,0:T(8,128)S(1)}, u32[]{:S(2)}) copy-start(f32[24,512]{1,0:T(8,128)S(1)} %collective-permute-done.8.refs_1_) | copy-start | bytes 147460
  16.6 4.7 %collective-permute-start.6 = (bf16[24,1024]{1,0:T(8,128)(2,1)S(1)}, bf16[24,1024]{1,0:T(8,128)(2,1)S(1)}, u32[]{:S(2)}, u32[]{:S(2)}) collective-permute-start(bf16[24,1024]{1,0:T(8,128)(2,1)S(1)} %get-tuple-element.27), channel_id=1, source_target_pairs={{0,4},{2,6},{4,0},{6,2},{8,12},{10,14},{12,8},{14,10},{16,20},{18,... | collective-permute-start | bytes 147464 | tf_op jit(solution)/shard_map/ppermute | solution.py:406
  20.1 9.3 %collective-permute-start.4 = (bf16[8,128,128]{2,1,0:T(8,128)(2,1)S(1)}, bf16[8,128,128]{2,1,0:T(8,128)(2,1)S(1)}, u32[]{:S(2)}, u32[]{:S(2)}) collective-permute-start(bf16[8,128,128]{2,1,0:T(8,128)(2,1)S(1)} %collective-permute-done.2.refs_4_), channel_id=1, source_target_pairs={{0,2},{2,0},{4,6},{6,4},{8,10},{10,8},{12,14},{14,12},{16,18},{18,... | collective-permute-start | bytes 786440 | tf_op jit(solution)/shard_map/ppermute | solution.py:406
  20.1 9.3 %collective-permute-start.5 = (bf16[8,128,128]{2,1,0:T(8,128)(2,1)S(1)}, bf16[8,128,128]{2,1,0:T(8,128)(2,1)S(1)}, u32[]{:S(2)}, u32[]{:S(2)}) collective-permute-start(bf16[8,128,128]{2,1,0:T(8,128)(2,1)S(1)} %collective-permute-done.3.refs_5_), channel_id=1, source_target_pairs={{0,2},{2,0},{4,6},{6,4},{8,10},{10,8},{12,14},{14,12},{16,18},{18,... | collective-permute-start | bytes 786440 | tf_op jit(solution)/shard_map/ppermute | solution.py:406
  21.3 3.7 %collective-permute-start.9 = (bf16[24,256]{1,0:T(8,128)(2,1)S(1)}, bf16[24,256]{1,0:T(8,128)(2,1)S(1)}, u32[]{:S(2)}, u32[]{:S(2)}) collective-permute-start(bf16[24,256]{1,0:T(8,128)(2,1)S(1)} %get-tuple-element.29), channel_id=1, source_target_pairs={{0,4},{2,6},{4,0},{6,2},{8,12},{10,14},{12,8},{14,10},{16,20},{18,... | collective-permute-start | bytes 36872 | tf_op jit(solution)/shard_map/ppermute | solution.py:406
  25.0 8.6 %collective-permute-start.13 = (bf16[48,1024]{1,0:T(8,128)(2,1)S(1)}, bf16[48,1024]{1,0:T(8,128)(2,1)S(1)}, u32[]{:S(2)}, u32[]{:S(2)}) collective-permute-start(bf16[48,1024]{1,0:T(8,128)(2,1)S(1)} %pad_maximum_fusion.query_ref), channel_id=1, source_target_pairs={{0,8},{2,10},{4,12},{6,14},{8,0},{10,2},{12,4},{14,6},{16,24},{18,... | collective-permute-start | bytes 294920 | tf_op jit(solution)/shard_map/ppermute | solution.py:406
  26.6 12.5 %collective-permute-start.11 = (bf16[48,1024]{1,0:T(8,128)(2,1)S(1)}, bf16[48,1024]{1,0:T(8,128)(2,1)S(1)}, u32[]{:S(2)}, u32[]{:S(2)}) collective-permute-start(bf16[48,1024]{1,0:T(8,128)(2,1)S(1)} %pad_maximum_fusion.query_ref), channel_id=1, source_target_pairs={{0,16},{2,18},{4,20},{6,22},{8,24},{10,26},{12,28},{14,30},{16,0},... | collective-permute-start | bytes 294920 | tf_op jit(solution)/shard_map/ppermute | solution.py:406
  29.2 20.5 %collective-permute-start.7 = (bf16[48,1024]{1,0:T(8,128)(2,1)S(1)}, bf16[48,1024]{1,0:T(8,128)(2,1)S(1)}, u32[]{:S(2)}, u32[]{:S(2)}) collective-permute-start(bf16[48,1024]{1,0:T(8,128)(2,1)S(1)} %pad_maximum_fusion.query_ref), channel_id=1, source_target_pairs={{0,24},{2,26},{4,28},{6,30},{8,16},{10,18},{12,20},{14,22},{16,8},... | collective-permute-start | bytes 294920 | tf_op jit(solution)/shard_map/ppermute | solution.py:406
  38.6 23.5 %collective-permute-start.14 = (bf16[400,128]{1,0:T(8,128)(2,1)S(1)}, bf16[400,128]{1,0:T(8,128)(2,1)S(1)}, u32[]{:S(2)}, u32[]{:S(2)}) collective-permute-start(bf16[400,128]{1,0:T(8,128)(2,1)S(1)} %shard_map.100), channel_id=1, source_target_pairs={{0,8},{2,10},{4,12},{6,14},{8,0},{10,2},{12,4},{14,6},{16,24},{18,... | collective-permute-start | bytes 307208 | tf_op jit(solution)/shard_map/ppermute | solution.py:406
  44.1 17.9 %collective-permute-start.12 = (bf16[400,128]{1,0:T(8,128)(2,1)S(1)}, bf16[400,128]{1,0:T(8,128)(2,1)S(1)}, u32[]{:S(2)}, u32[]{:S(2)}) collective-permute-start(bf16[400,128]{1,0:T(8,128)(2,1)S(1)} %shard_map.99), channel_id=1, source_target_pairs={{0,16},{2,18},{4,20},{6,22},{8,24},{10,26},{12,28},{14,30},{16,0},... | collective-permute-start | bytes 307208 | tf_op jit(solution)/shard_map/ppermute | solution.py:406
  54.6 7.5 %collective-permute-start.10 = (bf16[400,128]{1,0:T(8,128)(2,1)S(1)}, bf16[400,128]{1,0:T(8,128)(2,1)S(1)}, u32[]{:S(2)}, u32[]{:S(2)}) collective-permute-start(bf16[400,128]{1,0:T(8,128)(2,1)S(1)} %shard_map.98), channel_id=1, source_target_pairs={{0,24},{2,26},{4,28},{6,30},{8,16},{10,18},{12,20},{14,22},{16,8},... | collective-permute-start | bytes 307208 | tf_op jit(solution)/shard_map/ppermute | solution.py:406
  62.0 5.8 %copy-start.1 = (bf16[2048,4096]{1,0:T(8,128)(2,1)S(1)}, bf16[2048,4096]{1,0:T(8,128)(2,1)}, u32[]{:S(2)}) copy-start(bf16[2048,4096]{1,0:T(8,128)(2,1)} %refs_4_.1) | copy-start | bytes 50331652
  72.2 5.6 %collective-permute-start.15 = (bf16[24,2048]{1,0:T(8,128)(2,1)S(1)}, bf16[24,2048]{1,0:T(8,128)(2,1)S(1)}, u32[]{:S(2)}, u32[]{:S(2)}) collective-permute-start(bf16[24,2048]{1,0:T(8,128)(2,1)S(1)} %get-tuple-element.21), channel_id=1, source_target_pairs={{0,5},{1,4},{2,7},{3,6},{4,1},{5,0},{6,3},{7,2},{8,13},{9,12},{10,... | collective-permute-start | bytes 294920 | tf_op jit(solution)/shard_map/ppermute | solution.py:472
  74.5 4.6 %collective-permute-start.16 = (bf16[24,2048]{1,0:T(8,128)(2,1)S(1)}, bf16[24,2048]{1,0:T(8,128)(2,1)S(1)}, u32[]{:S(2)}, u32[]{:S(2)}) collective-permute-start(bf16[24,2048]{1,0:T(8,128)(2,1)S(1)} %get-tuple-element.22), channel_id=1, source_target_pairs={{0,1},{1,0},{2,3},{3,2},{4,5},{5,4},{6,7},{7,6},{8,9},{9,8},{10,11... | collective-permute-start | bytes 294920 | tf_op jit(solution)/shard_map/ppermute | solution.py:472
  75.1 4.6 %collective-permute-start.17 = (bf16[24,2048]{1,0:T(8,128)(2,1)S(1)}, bf16[24,2048]{1,0:T(8,128)(2,1)S(1)}, u32[]{:S(2)}, u32[]{:S(2)}) collective-permute-start(bf16[24,2048]{1,0:T(8,128)(2,1)S(1)} %get-tuple-element.23), channel_id=1, source_target_pairs={{0,4},{1,5},{2,6},{3,7},{4,0},{5,1},{6,2},{7,3},{8,12},{9,13},{10,... | collective-permute-start | bytes 294920 | tf_op jit(solution)/shard_map/ppermute | solution.py:472

commit v2 on v1

v2 whole, which is shorter than its diff:
```python
import functools
import math

import jax
import jax.numpy as jnp
from jax import lax
from jax.experimental import pallas as pl
from jax.experimental.pallas import tpu as pltpu
from jax.sharding import PartitionSpec as P

HD = 128
PAGE = 128
GROUPS = 2
REQS = 8
PLACE = 5
CHUNK = 4
BLOCKS = 2
AHEAD = 8
LOW = -1e30
EXP2_SCALE = math.log2(math.e) / math.sqrt(HD)
F32 = jnp.float32
BF16 = jnp.bfloat16
MIB = 1 << 20

NT = (((1,), (1,)), ((), ()))

VMEM = pl.BlockSpec(memory_space=pltpu.VMEM)
SMEM = pl.BlockSpec(memory_space=pltpu.SMEM)
ANY = pl.BlockSpec(memory_space=pl.ANY)
HBM = pl.BlockSpec(memory_space=pltpu.HBM)


TINY = pl.CostEstimate(flops=1, bytes_accessed=1, transcendentals=0)


def params(mib):
    return pltpu.CompilerParams(vmem_limit_bytes=mib * MIB)


def array_after(array, *awaited):
    def body(*refs):
        pass

    return pl.pallas_call(
        body,
        in_specs=[ANY] * (1 + len(awaited)),
        out_specs=ANY,
        out_shape=jax.ShapeDtypeStruct(array.shape, array.dtype),
        input_output_aliases={0: 0},
        compiler_params=params(2),
        cost_estimate=TINY,
    )(array, *awaited)


def list_pages(page_table, place, pages, splits, awaited):
    slots = pages * splits * GROUPS
    group_pages = page_table.shape[0] // GROUPS

    def body(table, place_ref, awaited_ref, out):
        for i in range(PLACE):
            out[i] = place_ref[i]
        group, first = place_ref[0], place_ref[2]

        def look(i, number):
            slot = table[group * group_pages + i] - first
            here = jnp.logical_and(slot >= 0, slot < slots)
            out[number + PLACE + 1] = slot
            return number + here.astype(jnp.int32)

        out[PLACE] = lax.fori_loop(0, group_pages, look, jnp.int32(0), unroll=8)

    return pl.pallas_call(
        body,
        in_specs=[SMEM, SMEM, ANY],
        out_specs=SMEM,
        out_shape=jax.ShapeDtypeStruct((PLACE + 2 + slots,), jnp.int32),
        compiler_params=params(2),
        cost_estimate=TINY,
    )(page_table, place, awaited)


def project_kv(hidden_in, weight, place, ranks, splits):
    rows, deep = hidden_in.shape
    width = weight.shape[1] // ranks
    steps = 8
    part = deep // steps
    kinds = [(rank, step) for rank in range(ranks) for step in range(splits)]

    def body(place_ref, hidden_ref, weight_ref, *refs):
        outs, (buffer, sums, sem) = refs[: len(kinds)], refs[len(kinds) :]
        copies = [
            pltpu.make_async_copy(weight_ref.at[pl.ds(i * part, part)], buffer.at[i], sem.at[i])
            for i in range(steps)
        ]
        for copy in copies[:AHEAD]:
            copy.start()
        for i, copy in enumerate(copies):
            copy.wait()
            if i + AHEAD < steps:
                copies[i + AHEAD].start()
            product = jnp.dot(
                hidden_ref[:, i * part : (i + 1) * part],
                buffer[i],
                preferred_element_type=F32,
            )
            sums[...] = product if i == 0 else sums[...] + product
        for out, (rank, step) in zip(outs, kinds):
            start = jnp.bitwise_xor(place_ref[4], rank) * width
            if step:
                start = start + jnp.bitwise_xor(place_ref[1], step) * (2 * HD)
            out[...] = sums[:, pl.ds(pl.multiple_of(start, 2 * HD), out.shape[1])]

    return pl.pallas_call(
        body,
        in_specs=[SMEM, VMEM, HBM],
        out_specs=[VMEM] * len(kinds),
        out_shape=[
            jax.ShapeDtypeStruct((rows, 2 * HD if step else width), F32) for _, step in kinds
        ],
        scratch_shapes=[
            pltpu.VMEM((steps, part, weight.shape[1]), BF16),
            pltpu.VMEM((rows, weight.shape[1]), F32),
            pltpu.SemaphoreType.DMA((steps,)),
        ],
        compiler_params=params(48),
        cost_estimate=TINY,
    )(place, hidden_in, weight)


def finish_kv(place, own, others, cosine, sine, heads, awaited):
    rows = own[0].shape[0]
    ranks = len(own)
    splits = 1 + len(others)

    def body(place_ref, *refs):
        own_refs, refs = refs[:ranks], refs[ranks:]
        other_refs, refs = refs[: (splits - 1) * ranks], refs[(splits - 1) * ranks :]
        cos_ref, sin_ref, _, out, suffix = refs

        def turned(key, sub):
            cos, sin = cos_ref[sub * rows : (sub + 1) * rows], sin_ref[sub * rows : (sub + 1) * rows]
            return (key * cos + pltpu.roll(key, HD // 2, 1) * sin).astype(BF16)

        total = functools.reduce(jnp.add, [ref[...] for ref in own_refs])
        pieces = []
        for head in range(heads):
            key = turned(total[:, head * 2 * HD : (head * 2 + 1) * HD], 0)
            value = total[:, (head * 2 + 1) * HD : (head * 2 + 2) * HD].astype(BF16)
            out[:, head * 2 * HD : (head * 2 + 1) * HD] = key
            out[:, (head * 2 + 1) * HD : (head * 2 + 2) * HD] = value
            pieces.append(jnp.concatenate([key, value], axis=1).astype(F32))
        mine = pieces[0]
        for head in range(1, heads):
            mine = jnp.where(place_ref[1] == head, pieces[head], mine)
        blocks = [mine]
        for sub in range(1, splits):
            group = other_refs[(sub - 1) * ranks : sub * ranks]
            total = functools.reduce(jnp.add, [ref[...] for ref in group])
            key = turned(total[:, :HD], sub)
            blocks.append(
                jnp.concatenate([key, total[:, HD:].astype(BF16)], axis=1).astype(F32)
            )
        suffix[...] = jnp.concatenate(blocks, axis=0).astype(BF16)

    flat = [array for arrays in others for array in arrays]
    return pl.pallas_call(
        body,
        in_specs=[SMEM] + [VMEM] * (ranks + len(flat) + 2) + [ANY],
        out_specs=[VMEM, VMEM],
        out_shape=[
            jax.ShapeDtypeStruct((rows, heads * 2 * HD), BF16),
            jax.ShapeDtypeStruct((rows * splits, 2 * HD), BF16),
        ],
        compiler_params=params(4),
        cost_estimate=TINY,
    )(place, *own, *flat, cosine, sine, awaited)


def collect_pages(listed, place, sources, pages, splits):
    slots = pages * splits * GROUPS

    def body(list_ref, place_ref, *refs):
        count = len(sources)
        own_keys, own_values, *others = refs[:count]
        keys_out, values_out, key_sem, value_sem = refs[count:]
        here = place_ref[1] * GROUPS + place_ref[0]
        number = list_ref[PLACE]

        def copies(which, page, at):
            rows = pl.ds(pl.multiple_of(at * PAGE, PAGE), PAGE)
            if which:
                views = [others[which - 1].at[kind, page] for kind in range(2)]
            else:
                view = (page, slice(None), pl.ds(pl.multiple_of(place_ref[1] * HD, HD), HD))
                views = [ref.at[view] for ref in (own_keys, own_values)]
            return (
                pltpu.make_async_copy(views[0], keys_out.at[rows], key_sem.at[at]),
                pltpu.make_async_copy(views[1], values_out.at[rows], value_sem.at[at]),
            )

        def begin(i, carry):
            slot = list_ref[PLACE + 1 + i]
            device = slot // pages
            page = slot - device * pages
            kind = jnp.bitwise_xor(device, here)
            for which in range(splits * GROUPS):

                @pl.when(kind == which)
                def _():
                    for copy in copies(which, page, i):
                        copy.start()

            return carry

        lax.fori_loop(0, number, begin, 0)

        def clear(i, carry):
            rows = pl.ds(pl.multiple_of(i * PAGE, PAGE), PAGE)
            values_out[rows, :] = jnp.zeros((PAGE, HD), BF16)
            return carry

        lax.fori_loop(number, jnp.minimum(number + CHUNK - 1, slots), clear, 0)

        def land(i, carry):
            for copy in copies(0, 0, i):
                copy.wait()
            return carry

        lax.fori_loop(0, number, land, 0)

    return pl.pallas_call(
        body,
        in_specs=[SMEM, SMEM] + [ANY] * len(sources),
        out_specs=[VMEM, VMEM],
        out_shape=[
            jax.ShapeDtypeStruct((slots * PAGE, HD), BF16),
            jax.ShapeDtypeStruct((slots * PAGE, HD), BF16),
        ],
        scratch_shapes=[pltpu.SemaphoreType.DMA((slots,)), pltpu.SemaphoreType.DMA((slots,))],
        compiler_params=params(16),
        cost_estimate=TINY,
    )(listed, place, *sources)


def attend(listed, lengths, place, fars, queries, suffix, keys, values, rows_each):
    tokens = queries[0].shape[0]
    splits = tokens // rows_each
    heads = queries[0].shape[1] // HD
    rows = tokens * heads
    slots = keys.shape[0] // PAGE
    wide = CHUNK * PAGE
    parts = -(-rows // HD)
    stat_rows = -(-3 * parts // 16) * 16
    blocks = len(queries)

    def body(list_ref, len_ref, place_ref, *refs):
        query_refs, refs = refs[:blocks], refs[blocks:]
        suffix_ref, keys_ref, values_ref, refs = refs[0], refs[1], refs[2], refs[3:]
        outs, (stacked, top, total, column, stats) = refs[:blocks], refs[blocks:]
        count = list_ref[PLACE]
        turns = lax.div(count + (CHUNK - 1), CHUNK)
        group, split, z_here = place_ref[0], place_ref[1], place_ref[3]

        def places(z, axis):
            index = lax.broadcasted_iota(jnp.int32, (tokens, tokens), axis)
            result = jnp.zeros((tokens, tokens), jnp.int32)
            for sub in range(splits):
                block = z * splits + jnp.bitwise_xor(split, sub)
                result = jnp.where(
                    index >= sub * rows_each, (block - sub) * rows_each + index, result
                )
            return result

        own_keys = suffix_ref[:, :HD]
        own_values = jnp.concatenate([suffix_ref[:, HD:], jnp.ones((tokens, HD), BF16)], axis=1)
        key_place = places(z_here, 1)
        for b in range(blocks):
            q = jnp.concatenate(
                [query_refs[b][:, h * HD : (h + 1) * HD].astype(F32) for h in range(heads)], axis=0
            ).astype(BF16)
            stacked[b] = q
            query_place = places(jnp.bitwise_xor(z_here, fars[b]), 0)
            begins = jnp.zeros((tokens, tokens), jnp.int32)
            edge = jnp.int32(0)
            for r in range(REQS):
                edge = edge + len_ref[group, r]
                begins = jnp.where(query_place >= edge, edge, begins)
            seen = jnp.logical_and(key_place <= query_place, key_place >= begins)
            seen = jnp.concatenate([seen.astype(F32)] * heads, axis=0)
            own = lax.dot_general(q, own_keys, NT, preferred_element_type=F32)
            own = jnp.where(seen > 0.0, own, LOW)
            highest = jnp.max(own, axis=1, keepdims=True)
            weights = jnp.exp2((own - highest) * EXP2_SCALE) * seen
            total[b] = jnp.dot(weights.astype(BF16), own_values, preferred_element_type=F32)
            top[b] = jnp.broadcast_to(highest, (rows, HD))

        def turn(c, carry):
            span = pl.ds(pl.multiple_of(c * wide, wide), wide)
            chunk_keys = keys_ref[span, :]
            chunk_values = jnp.concatenate(
                [values_ref[span, :], jnp.ones((wide, HD), BF16)], axis=1
            )
            found = [
                lax.dot_general(stacked[b], chunk_keys, NT, preferred_element_type=F32)
                for b in range(blocks)
            ]
            for b in range(blocks):
                pieces = [
                    jnp.where(c * CHUNK + j < count, found[b][:, j * PAGE : (j + 1) * PAGE], LOW)
                    for j in range(CHUNK)
                ]
                best = functools.reduce(jnp.maximum, pieces)
                before = top[b]
                highest = jnp.maximum(before, jnp.max(best, axis=1, keepdims=True))
                weights = jnp.concatenate(
                    [jnp.exp2((piece - highest) * EXP2_SCALE).astype(BF16) for piece in pieces],
                    axis=1,
                )
                factor = jnp.exp2((before - highest) * EXP2_SCALE)
                added = jnp.dot(weights, chunk_values, preferred_element_type=F32)
                total[b] = total[b] * jnp.concatenate([factor, factor], axis=1) + added
                top[b] = highest
            return carry

        lax.fori_loop(0, turns, turn, 0)
        for b in range(blocks):
            sums = total[b, :, HD:]
            some = sums > 0.0
            safe = jnp.where(some, sums, 1.0)
            outs[b][0:rows, :] = (total[b, :, :HD] / safe).astype(BF16)
            column[0:rows, :] = jnp.where(some, top[b] * EXP2_SCALE + jnp.log2(safe), LOW)
            stats[...] = jnp.zeros((stat_rows, HD), F32)
            for part in range(parts):
                line = column[part * HD : (part + 1) * HD, :].T[0:1, :]
                for piece in range(3):
                    rounded = line.astype(BF16).astype(F32)
                    stats[3 * part + piece : 3 * part + piece + 1, :] = rounded
                    line = line - rounded
            outs[b][rows : rows + stat_rows, :] = stats[...].astype(BF16)

    return pl.pallas_call(
        body,
        in_specs=[SMEM, SMEM, SMEM] + [VMEM] * (blocks + 3),
        out_specs=[VMEM] * blocks,
        out_shape=[jax.ShapeDtypeStruct((rows + stat_rows, HD), BF16)] * blocks,
        scratch_shapes=[
            pltpu.VMEM((blocks, rows, HD), BF16),
            pltpu.VMEM((blocks, rows, HD), F32),
            pltpu.VMEM((blocks, rows, 2 * HD), F32),
            pltpu.VMEM((parts * HD, HD), F32),
            pltpu.VMEM((stat_rows, HD), F32),
        ],
        compiler_params=params(16),
        cost_estimate=pl.CostEstimate(
            flops=4 * blocks * rows * slots * PAGE * HD,
            bytes_accessed=slots * PAGE * HD * 3,
            transcendentals=blocks * rows * slots * PAGE // 2,
        ),
    )(listed, lengths, place, *queries, suffix, keys, values)


def fetch_rows(weight, place, depth, after):
    def body(place_ref, weight_ref, after_ref, out, sem):
        start = pl.multiple_of(place_ref[1] * depth, depth)
        copy = pltpu.make_async_copy(weight_ref.at[pl.ds(start, depth)], out, sem)
        copy.start()
        copy.wait()

    return pl.pallas_call(
        body,
        in_specs=[SMEM, HBM, ANY],
        out_specs=VMEM,
        out_shape=jax.ShapeDtypeStruct((depth, weight.shape[1]), BF16),
        scratch_shapes=[pltpu.SemaphoreType.DMA],
        compiler_params=params(40),
        cost_estimate=pl.CostEstimate(
            flops=0, bytes_accessed=4 * depth * weight.shape[1], transcendentals=0
        ),
    )(place, weight, after)


def project(place, partials, weight, rows_each, splits, ranks, heads):
    tokens = rows_each * splits
    rows = tokens * heads
    parts = -(-rows // HD)
    width = weight.shape[1] // ranks

    def body(place_ref, *refs):
        count = len(partials)
        partial_refs, weight_ref, outs = refs[:count], refs[count], refs[count + 1 : -2]
        merged, attended = refs[-2:]
        for part in range(parts):
            length = min(HD, rows - part * HD)
            lines = []
            for ref in partial_refs:
                stat = ref[rows:, :].astype(F32)
                lines.append(
                    stat[3 * part : 3 * part + 1]
                    + stat[3 * part + 1 : 3 * part + 2]
                    + stat[3 * part + 2 : 3 * part + 3]
                )
            best = functools.reduce(jnp.maximum, lines)
            shares = [jnp.exp2(line - best) for line in lines]
            whole = functools.reduce(jnp.add, shares)
            mixed = jnp.zeros((length, HD), F32)
            for share, ref in zip(shares, partial_refs):
                factor = jnp.broadcast_to(share / whole, (HD, HD)).T[:length]
                mixed = mixed + factor * ref[part * HD : part * HD + length, :].astype(F32)
            merged[part * HD : part * HD + length, :] = mixed
        for h in range(heads):
            attended[:, h * HD : (h + 1) * HD] = merged[h * tokens : (h + 1) * tokens, :].astype(
                BF16
            )
        for rank in range(ranks):
            start = pl.multiple_of(jnp.bitwise_xor(place_ref[4], rank) * width, width)
            product = jnp.dot(
                attended[...], weight_ref[:, pl.ds(start, width)], preferred_element_type=F32
            )
            for sub in range(splits):
                out = outs[rank * splits + sub]
                out[...] = product[sub * rows_each : (sub + 1) * rows_each].astype(out.dtype)

    return pl.pallas_call(
        body,
        in_specs=[SMEM] + [VMEM] * (len(partials) + 1),
        out_specs=[VMEM] * (ranks * splits),
        out_shape=[
            jax.ShapeDtypeStruct((rows_each, width), BF16 if i else F32)
            for i in range(ranks * splits)
        ],
        scratch_shapes=[pltpu.VMEM((rows, HD), F32), pltpu.VMEM((tokens, heads * HD), BF16)],
        compiler_params=params(16),
        cost_estimate=pl.CostEstimate(
            flops=2 * tokens * weight.size, bytes_accessed=weight.size, transcendentals=0
        ),
    )(place, *partials, weight)


def local(
    hidden_in,
    kv_weight,
    queries,
    prefix_keys,
    prefix_values,
    page_table,
    suffix_lengths,
    out_weight,
):
    rows = hidden_in.shape[0]
    seq_count, ranks = lax.axis_size("seq"), lax.axis_size("tp")
    seq_rank, tp_rank = lax.axis_index("seq"), lax.axis_index("tp")
    pages = prefix_keys.shape[0]
    splits = prefix_keys.shape[2] // HD
    heads = queries.shape[1] // HD // splits
    prefix_len = pages * seq_count // GROUPS * PAGE
    blocks = seq_count // GROUPS
    depth = blocks // splits
    group = seq_rank % GROUPS
    block = seq_rank // GROUPS
    split = block % splits
    place = jnp.stack(
        [group, split, (block - split) * GROUPS * pages, block // splits, tp_rank]
    ).astype(jnp.int32)

    def across(array, far=0, side=0, core=0):
        step = (far * splits + side) * GROUPS + core
        return lax.ppermute(array, "seq", [(i, i ^ step) for i in range(seq_count)])

    def columns(array, index, width):
        return lax.dynamic_slice_in_dim(array, index * width, width, 1)

    def quad(array, rank, side):
        step = side * GROUPS
        route = [
            (i * ranks + j, (i ^ step) * ranks + (j ^ rank))
            for i in range(seq_count)
            for j in range(ranks)
        ]
        return lax.ppermute(array, ("seq", "tp"), route)

    def columns(array, index, width):
        return lax.dynamic_slice_in_dim(array, index * width, width, array.ndim - 1)

    parts = [columns(queries, split, heads * HD)]
    for side in range(1, splits):
        parts.append(across(columns(queries, split ^ side, heads * HD), side=side))
    my_query = jnp.concatenate(parts, axis=0)
    listed = list_pages(page_table, place, pages, splits, my_query)
    far_queries = [my_query] + [across(my_query, far=far) for far in range(1, depth)]
    sent = [
        jnp.stack([columns(array, split ^ side, HD) for array in (prefix_keys, prefix_values)])
        for side in range(splits)
    ]
    arrived = [across(sent[side], side=side) for side in range(1, splits)]
    sources = [prefix_keys, prefix_values, across(sent[0], core=1)]

    projected = project_kv(hidden_in, kv_weight, listed, ranks, splits)
    own = [projected[0]] + [quad(projected[rank * splits], rank, 0) for rank in range(1, ranks)]
    others = [
        [quad(projected[rank * splits + side], rank, side) for rank in range(ranks)]
        for side in range(1, splits)
    ]
    for array in arrived:
        array = array_after(array, projected[0], *far_queries[1:])
        sources += [array, across(array, core=1)]
    keys, values = collect_pages(listed, place, sources, pages, splits)
    lengths = jnp.sum(
        jnp.where(jnp.arange(GROUPS)[:, None] == group, suffix_lengths, 0), axis=0
    )
    ends = jnp.sum(
        jnp.where(jnp.arange(REQS)[None, :] <= jnp.arange(REQS)[:, None], lengths[None, :], 0),
        axis=1,
    )
    index = jnp.arange(rows * splits, dtype=jnp.int32)
    within = (block - split + (split ^ (index // rows))) * rows + index % rows
    begins = jnp.max(jnp.where(within[:, None] >= ends[None, :], ends[None, :], 0), axis=1)
    positions = prefix_len + within - begins
    half = HD // 2
    frequency = jnp.power(500000.0, -(jnp.arange(half, dtype=F32) * 2.0 / HD))
    angles = positions.astype(F32)[:, None] * frequency[None, :]
    cosine, sine = jnp.cos(angles), jnp.sin(angles)
    cosine = jnp.concatenate([cosine, cosine], axis=1)
    sine = jnp.concatenate([-sine, sine], axis=1)
    new_pages, suffix = finish_kv(place, own, others, cosine, sine, splits, keys)

    returned = []
    order = list(range(depth - 1, -1, -1))
    for first in range(0, depth, BLOCKS):
        fars = order[first : first + BLOCKS]
        sums = attend(
            listed, suffix_lengths, place, fars, [far_queries[far] for far in fars],
            suffix, keys, values, rows,
        )
        returned += [across(part, far=far) if far else part for far, part in zip(fars, sums)]

    weight = fetch_rows(out_weight, place, heads * HD, returned[-1])
    products = project(place, returned, weight, rows, splits, ranks, heads)
    hidden = products[0]
    for rank in range(ranks - 1, -1, -1):
        for side in range(splits - 1, -1, -1):
            if rank or side:
                hidden = hidden + quad(products[rank * splits + side], rank, side).astype(F32)
    return (hidden.astype(BF16), new_pages)


def solution(mesh):
    return jax.shard_map(
        local,
        mesh=mesh,
        in_specs=(
            P("seq", "tp"),
            P("tp", None),
            P("seq", "tp"),
            P("seq", None, "tp"),
            P("seq", None, "tp"),
            P(),
            P(),
            P("tp", None),
        ),
        out_specs=(P("seq", "tp"), P("seq", "tp")),
        check_vma=False,
    )
```

time: 80 us -> 58.3 us (0.73)
  starting transfers between devices: 26 us -> 18.7 us
  local copies, waits for them, and re-layouts: 9.34 us -> 3.86 us
  matrix products: 4.59 us -> 0 us
  Pallas kernels: 30.5 us -> 26.6 us
  waiting for transfers between devices: 7.28 us -> 5.76 us
    ppermute x14 -> x10, starting transfers between devices: 20.5 us -> 11.6 us  [across(): return lax.ppermute(array, 'seq', [(i, i ^ step) for i in range(seq_count)])]
    unnamed x16 -> x10, local copies, waits for them, and re-layouts: 7.88 us -> 1.59 us
    dot_general x1 -> x0, matrix products: 4.59 us -> none  [local(): partial = jnp.dot(hidden_in, kv_weight, preferred_element_type=F32)]
    pallas_call x7 -> x8, Pallas kernels: 26.3 us -> 23.6 us  [the longest x2 10.4 us: attend(): pl.pallas_call(body, in_specs=[SMEM, SMEM, SMEM] + [VMEM] * (blocks + 3),...]
    ppermute x4 -> x6, starting transfers between devices: 5.47 us -> 7.11 us  [quad(): return lax.ppermute(array, ('seq', 'tp'), route)]
    another operation x0 -> x1, local copies, waits for them, and re-layouts: none -> 1.27 us  [local(): jnp.stack([columns(array, split ^ side, HD) for array in (prefix_keys, pr...]
    pallas_call x1, Pallas kernels: 4.16 us -> 3.09 us  [collect_pages(): pl.pallas_call(body, in_specs=[SMEM, SMEM] + [ANY] * len(sources), out_sp...]
    ppermute x4 -> x6, waiting for transfers between devices: 4.89 us -> 4.08 us  [quad(): return lax.ppermute(array, ('seq', 'tp'), route)]
  transfers between devices with their start and end apart: 18 -> 16, of which waited for: 5 -> 7; matrix products, arithmetic and copies ran while one was open for 9% -> 5% of each run, Pallas kernels for 31% -> 31%
where the time goes in v2:
time: 58.3 us; the launch traced here: 58 us
  Pallas kernels  26.6 us (46%)
  starting transfers between devices  18.7 us (32%)
  waiting for transfers between devices  5.76 us (10%)
  local copies, waits for them, and re-layouts  3.86 us (7%)
  other arithmetic  2.06 us (4%)
  between operations  0.89 us (2%)
    ppermute x10, starting transfers between devices, across(): return lax.ppermute(array, 'seq', [(i, i ^ step) for i in range(seq_count)])  11.6 us
    pallas_call x2, Pallas kernels, attend(): pl.pallas_call(body, in_specs=[SMEM, SMEM, SMEM] + [VMEM] * (blocks + 3),...  10.4 us
    ppermute x6, starting transfers between devices, quad(): return lax.ppermute(array, ('seq', 'tp'), route)  7.11 us
    pallas_call x1, Pallas kernels, project_kv(): pl.pallas_call(body, in_specs=[SMEM, VMEM, HBM], out_specs=[VMEM] * len(k...  4.31 us
    ppermute x6, waiting for transfers between devices, quad(): return lax.ppermute(array, ('seq', 'tp'), route)  4.08 us
    pallas_call x1, Pallas kernels, fetch_rows(): pl.pallas_call(body, in_specs=[SMEM, HBM, ANY], out_specs=VMEM, out_shape...  3.93 us
    pallas_call x1, Pallas kernels, collect_pages(): pl.pallas_call(body, in_specs=[SMEM, SMEM] + [ANY] * len(sources), out_sp...  3.09 us
    pallas_call x1, Pallas kernels, project(): pl.pallas_call(body, in_specs=[SMEM] + [VMEM] * (len(partials) + 1), out_...  2.3 us
  transfers between devices with their start and end apart: 16, of which 7 were waited for; matrix products, arithmetic and copies ran while one was open for 5% of the time, Pallas kernels for 31%

profile of v2, /device:TPU:0, one launch (start us, length us, event | category | flops | bytes accessed | tf_op | source)
XLA Modules:
  0.0 58.0 jit_solution(2281830388984179080)
XLA Ops:
  0.6 0.0 copy-start.1
  0.6 0.0 copy-start
  0.7 0.9 %constant_dynamic-slice_fusion.1 = (bf16[24,1024]{1,0:T(8,128)(2,1)S(1)}, bf16[24,1024]{1,0:T(8,128)(2,1)S(1)}) fusion(bf16[24,2048]{1,0:T(8,128)(2,1)} %param.10, s32[]{:T(128)S(6)} %select_n.73, s32[]{:T(128)S(6)} %select_n.74), kind=kLoop, calls=%fused_computation.19 | loop fusion | bytes 196616 | tf_op jit(solution)/shard_map/dynamic_slice | solution.py:482
  1.6 3.0 %collective-permute-start = (bf16[24,1024]{1,0:T(8,128)(2,1)S(1)}, bf16[24,1024]{1,0:T(8,128)(2,1)S(1)}, u32[]{:S(2)}, u32[]{:S(2)}) collective-permute-start(bf16[24,1024]{1,0:T(8,128)(2,1)S(1)} %get-tuple-element.39), channel_id=1, source_target_pairs={{0,4},{2,6},{4,0},{6,2},{8,12},{10,14},{12,8},{14,10},{16,20},{18,... | collective-permute-start | bytes 147464 | tf_op jit(solution)/shard_map/ppermute | solution.py:467
  4.6 1.3 %dynamic-slice_bitcast_fusion = (bf16[1,8,128,128]{3,2,1,0:T(8,128)(2,1)S(1)}, bf16[1,8,128,128]{3,2,1,0:T(8,128)(2,1)S(1)}, bf16[1,8,128,128]{3,2,1,0:T(8,128)(2,1)S(1)}, bf16[1,8,128,128]{3,2,1,0:T(8,128)(2,1)S(1)}) fusion(bf16[8,128,256]{2,1,0:T(8,128)(2,1)} %refs_1_.1, s32[]{:T(128)S(6)} %select_n.81, s32[]{:T(128)S(6)} %select_n.80, ...), kind=kLoop, calls=%fused_computation.2 | loop fusion | bytes 2097160 | tf_op jit(solution)/shard_map/stack | solution.py:491
  5.9 0.0 copy-start.3
  5.9 0.1 pad_maximum_fusion
  6.0 0.1 collective-permute-start.6
  6.1 0.1 pad_maximum_fusion.1
  6.1 0.1 collective-permute-start.7
  6.2 0.8 %select_reduce_fusion.2 = s32[8]{0:T(128)S(1)} fusion(s32[2,8]{1,0:T(2,128)} %len_ref.3, pred[2]{0:T(512)(128)(4,1)S(1)} %iota_compare_fusion.1), kind=kLoop, calls=%fused_computation.20 | loop fusion | flops 24 | bytes 98 | tf_op jit(solution)/shard_map/reduce_sum | solution.py:507
  7.0 0.1 select_reduce_fusion.1
  7.1 0.1 select_reduce_fusion
  7.2 0.1 stack.41.place_ref
  7.3 2.1 %collective-permute-start.8 = (bf16[48,1024]{1,0:T(8,128)(2,1)S(1)}, bf16[48,1024]{1,0:T(8,128)(2,1)S(1)}, u32[]{:S(2)}, u32[]{:S(2)}) collective-permute-start(bf16[48,1024]{1,0:T(8,128)(2,1)S(1)} %pad_maximum_fusion.2.awaited_ref.refs_1_), channel_id=1, source_target_pairs={{0,8},{2,10},{4,12},{6,14},{8,0},{10,2},{12,4},{14,6},{16,24},{18,... | collective-permute-start | bytes 294920 | tf_op jit(solution)/shard_map/ppermute | solution.py:467
  9.4 2.6 %collective-permute-start.2 = (bf16[48,1024]{1,0:T(8,128)(2,1)S(1)}, bf16[48,1024]{1,0:T(8,128)(2,1)S(1)}, u32[]{:S(2)}, u32[]{:S(2)}) collective-permute-start(bf16[48,1024]{1,0:T(8,128)(2,1)S(1)} %pad_maximum_fusion.2.awaited_ref.refs_1_), channel_id=1, source_target_pairs={{0,16},{2,18},{4,20},{6,22},{8,24},{10,26},{12,28},{14,30},{16,0},... | collective-permute-start | bytes 294920 | tf_op jit(solution)/shard_map/ppermute | solution.py:467
  12.0 0.0 collective-permute-start.1
  12.0 0.0 copy-start.4
  12.0 0.6 %copy-done.4 = s32[128]{0:T(128)S(1)} copy-done((s32[128]{0:T(128)S(1)}, s32[128]{0:T(128)}, u32[]{:S(2)}) %copy-start.4) | copy-done | bytes 536
  12.7 1.4 %shard_map.95.place_ref.list_ref = s32[39]{0:T(128)S(1)} custom-call(s32[128]{0:T(128)S(1)} %copy-done.4, s32[5]{0:T(128)S(1)} %stack.41.place_ref, bf16[48,1024]{1,0:T(8,128)(2,1)S(1)} %pad_maximum_fusion.2.awaited_ref.refs_1_), custom_call_target="tpu_custom_call" | custom-call | flops 1 | bytes 1 | tf_op jit(solution)/shard_map/pallas_call | solution.py:72
  14.1 0.0 copy-start.2
  14.1 0.9 %copy-done.2 = bf16[24,4096]{1,0:T(8,128)(2,1)S(1)} copy-done((bf16[24,4096]{1,0:T(8,128)(2,1)S(1)}, bf16[24,4096]{1,0:T(8,128)(2,1)}, u32[]{:S(2)}) %copy-start.2) | copy-done | bytes 196632
  15.0 4.3 %shard_map.96 = (f32[24,512]{1,0:T(8,128)S(1)}, f32[24,256]{1,0:T(8,128)S(1)}, f32[24,512]{1,0:T(8,128)S(1)}, f32[24,256]{1,0:T(8,128)S(1)}) custom-call(s32[39]{0:T(128)S(1)} %shard_map.95.place_ref.list_ref, bf16[24,4096]{1,0:T(8,128)(2,1)S(1)} %copy-done.2, bf16[4096,1024]{1,0:T(8,128)(2,1)} %weight_ref.2), custom_call_target="tpu_custom_call" | custom-call | flops 1 | bytes 1 | tf_op jit(solution)/shard_map/pallas_call | solution.py:113
  19.3 0.0 collective-permute-done.8.refs_2_.refs_0_
  19.3 0.7 %collective-permute-done.2.refs_3_.refs_1_ = bf16[48,1024]{1,0:T(8,128)(2,1)S(1)} collective-permute-done((bf16[48,1024]{1,0:T(8,128)(2,1)S(1)}, bf16[48,1024]{1,0:T(8,128)(2,1)S(1)}, u32[]{:S(2)}, u32[]{:S(2)}) %collective-permute-start.2) | collective-permute-done | bytes 98336 | tf_op jit(solution)/shard_map/ppermute | solution.py:467
  20.0 0.5 collective-permute-done.7.refs_0_
  20.5 0.2 fusion
  20.7 1.2 %collective-permute-start.4 = (f32[24,256]{1,0:T(8,128)S(1)}, f32[24,256]{1,0:T(8,128)S(1)}, u32[]{:S(2)}, u32[]{:S(2)}) collective-permute-start(f32[24,256]{1,0:T(8,128)S(1)} %get-tuple-element.20), channel_id=1, source_target_pairs={{0,4},{1,5},{2,6},{3,7},{4,0},{5,1},{6,2},{7,3},{8,12},{9,13},{10,... | collective-permute-start | bytes 73736 | tf_op jit(solution)/shard_map/ppermute | solution.py:479
  21.9 1.8 %collective-permute-start.5 = (f32[24,256]{1,0:T(8,128)S(1)}, f32[24,256]{1,0:T(8,128)S(1)}, u32[]{:S(2)}, u32[]{:S(2)}) collective-permute-start(f32[24,256]{1,0:T(8,128)S(1)} %get-tuple-element.21), channel_id=1, source_target_pairs={{0,5},{1,4},{2,7},{3,6},{4,1},{5,0},{6,3},{7,2},{8,13},{9,12},{10,... | collective-permute-start | bytes 73736 | tf_op jit(solution)/shard_map/ppermute | solution.py:479
  23.7 0.5 collective-permute-start.3
  24.3 0.1 pad_maximum_fusion.3
  24.4 3.1 %shard_map.98 = (bf16[4096,128]{1,0:T(8,128)(2,1)S(1)}, bf16[4096,128]{1,0:T(8,128)(2,1)S(1)}) custom-call(s32[39]{0:T(128)S(1)} %shard_map.95.place_ref.list_ref, s32[5]{0:T(128)S(1)} %stack.41.place_ref, bf16[8,128,256]{2,1,0:T(8,128)(2,1)S(1)} %copy-done, bf16[8,128,256]{2,1,0:T(8,128)(2,1)S(1)} %copy-done.1, ...), custom_call_target="tpu_custom_call" | custom-call | flops 1 | bytes 1 | tf_op jit(solution)/shard_map/pallas_call | solution.py:231
  27.5 0.3 collective-permute-done.3.refs_1_
  27.8 1.2 %shard_map.99 = (bf16[24,512]{1,0:T(8,128)(2,1)}, bf16[48,256]{1,0:T(8,128)(2,1)S(1)}) custom-call(s32[5]{0:T(128)S(1)} %stack.41.place_ref, f32[24,512]{1,0:T(8,128)S(1)} %get-tuple-element.18.refs_1_.refs_0_, f32[24,512]{1,0:T(8,128)S(1)} %collective-permute-done.3.refs_1_, f32[24,256]{1,0:T(8,128)S(1)} %collective-permute-done.4.refs_2_, ...), custom_call_target="tpu_custom_call" | custom-call | flops 1 | bytes 1 | tf_op jit(solution)/shard_map/pallas_call | solution.py:166
  29.0 5.2 %shard_map.100 = (bf16[400,128]{1,0:T(8,128)(2,1)S(1)}, bf16[400,128]{1,0:T(8,128)(2,1)S(1)}) custom-call(s32[39]{0:T(128)S(1)} %shard_map.95.place_ref.list_ref, s32[2,8]{1,0:T(2,128)S(1)} %copy-done.3, s32[5]{0:T(128)S(1)} %stack.41.place_ref, bf16[48,1024]{1,0:T(8,128)(2,1)S(1)} %collective-permute-done.1.refs_4_.refs_0_, ...), custom_call_target="tpu_custom_call" | custom-call | flops 1610612736 | bytes 1572864 | tf_op jit(solution)/shard_map/pallas_call | solution.py:341
  34.2 2.9 %collective-permute-start.10 = (bf16[400,128]{1,0:T(8,128)(2,1)S(1)}, bf16[400,128]{1,0:T(8,128)(2,1)S(1)}, u32[]{:S(2)}, u32[]{:S(2)}) collective-permute-start(bf16[400,128]{1,0:T(8,128)(2,1)S(1)} %get-tuple-element.25), channel_id=1, source_target_pairs={{0,24},{2,26},{4,28},{6,30},{8,16},{10,18},{12,20},{14,22},{16,8},... | collective-permute-start | bytes 307208 | tf_op jit(solution)/shard_map/ppermute | solution.py:467
  37.1 5.2 %shard_map.101 = (bf16[400,128]{1,0:T(8,128)(2,1)S(1)}, bf16[400,128]{1,0:T(8,128)(2,1)S(1)}) custom-call(s32[39]{0:T(128)S(1)} %shard_map.95.place_ref.list_ref, s32[2,8]{1,0:T(2,128)S(1)} %copy-done.3, s32[5]{0:T(128)S(1)} %stack.41.place_ref, bf16[48,1024]{1,0:T(8,128)(2,1)S(1)} %collective-permute-done.8.refs_2_.refs_0_, ...), custom_call_target="tpu_custom_call" | custom-call | flops 1610612736 | bytes 1572864 | tf_op jit(solution)/shard_map/pallas_call | solution.py:341
  42.3 0.8 %collective-permute-start.12 = (bf16[400,128]{1,0:T(8,128)(2,1)S(1)}, bf16[400,128]{1,0:T(8,128)(2,1)S(1)}, u32[]{:S(2)}, u32[]{:S(2)}) collective-permute-start(bf16[400,128]{1,0:T(8,128)(2,1)S(1)} %get-tuple-element.27), channel_id=1, source_target_pairs={{0,8},{2,10},{4,12},{6,14},{8,0},{10,2},{12,4},{14,6},{16,24},{18,... | collective-permute-start | bytes 307208 | tf_op jit(solution)/shard_map/ppermute | solution.py:467
  43.2 3.9 %shard_map.102.refs_4_ = bf16[1024,4096]{1,0:T(8,128)(2,1)S(1)} custom-call(s32[5]{0:T(128)S(1)} %stack.41.place_ref, bf16[2048,4096]{1,0:T(8,128)(2,1)} %weight_ref.3, bf16[400,128]{1,0:T(8,128)(2,1)S(1)} %get-tuple-element.28.after_ref.refs_3_), custom_call_target="tpu_custom_call" | custom-call | bytes 16777216 | tf_op jit(solution)/shard_map/pallas_call | solution.py:369
  47.1 0.5 collective-permute-done.12.refs_2_
  47.7 2.3 %shard_map.103 = (f32[24,2048]{1,0:T(8,128)S(1)}, bf16[24,2048]{1,0:T(8,128)(2,1)S(1)}, bf16[24,2048]{1,0:T(8,128)(2,1)S(1)}, bf16[24,2048]{1,0:T(8,128)(2,1)S(1)}) custom-call(s32[5]{0:T(128)S(1)} %stack.41.place_ref, bf16[400,128]{1,0:T(8,128)(2,1)S(1)} %collective-permute-done.10.refs_0_, bf16[400,128]{1,0:T(8,128)(2,1)S(1)} %collective-permute-done.11.refs_1_, ...), custom_call_target="tpu_custom_call" | custom-call | flops 402653184 | bytes 4194304 | tf_op jit(solution)/shard_map/pallas_call | solution.py:423
  50.0 1.8 %collective-permute-start.13 = (bf16[24,2048]{1,0:T(8,128)(2,1)S(1)}, bf16[24,2048]{1,0:T(8,128)(2,1)S(1)}, u32[]{:S(2)}, u32[]{:S(2)}) collective-permute-start(bf16[24,2048]{1,0:T(8,128)(2,1)S(1)} %get-tuple-element.30), channel_id=1, source_target_pairs={{0,5},{1,4},{2,7},{3,6},{4,1},{5,0},{6,3},{7,2},{8,13},{9,12},{10,... | collective-permute-start | bytes 294920 | tf_op jit(solution)/shard_map/ppermute | solution.py:479
  51.7 0.5 collective-permute-start.14
  52.2 1.3 %collective-permute-start.15 = (bf16[24,2048]{1,0:T(8,128)(2,1)S(1)}, bf16[24,2048]{1,0:T(8,128)(2,1)S(1)}, u32[]{:S(2)}, u32[]{:S(2)}) collective-permute-start(bf16[24,2048]{1,0:T(8,128)(2,1)S(1)} %get-tuple-element.32), channel_id=1, source_target_pairs={{0,4},{1,5},{2,6},{3,7},{4,0},{5,1},{6,2},{7,3},{8,12},{9,13},{10,... | collective-permute-start | bytes 294920 | tf_op jit(solution)/shard_map/ppermute | solution.py:479
  53.5 3.0 %collective-permute-done.13 = bf16[24,2048]{1,0:T(8,128)(2,1)S(1)} collective-permute-done((bf16[24,2048]{1,0:T(8,128)(2,1)S(1)}, bf16[24,2048]{1,0:T(8,128)(2,1)S(1)}, u32[]{:S(2)}, u32[]{:S(2)}) %collective-permute-start.13) | collective-permute-done | bytes 98336 | tf_op jit(solution)/shard_map/ppermute | solution.py:479
  56.5 0.4 collective-permute-done.14
  56.9 0.4 collective-permute-done.15
  57.3 0.7 %add_convert_fusion = bf16[24,2048]{1,0:T(8,128)(2,1)} fusion(bf16[24,2048]{1,0:T(8,128)(2,1)S(1)} %collective-permute-done.15, bf16[24,2048]{1,0:T(8,128)(2,1)S(1)} %collective-permute-done.14, f32[24,2048]{1,0:T(8,128)S(1)} %get-tuple-element.29, bf16[24,2048]{1,0:T(8,128)(2,1)S(1)} %collective-permute-done.13), kind=kLoop, calls=%fused_computation.6 | loop fusion | flops 344064 | bytes 589824 | tf_op jit(solution)/shard_map/convert_element_type | solution.py:543
  (19 shorter events, 0.1 us)
Async XLA Ops:
  0.6 23.7 %copy-start.1 = (bf16[8,128,256]{2,1,0:T(8,128)(2,1)S(1)}, bf16[8,128,256]{2,1,0:T(8,128)(2,1)}, u32[]{:S(2)}) copy-start(bf16[8,128,256]{2,1,0:T(8,128)(2,1)} %refs_1_.1) | copy-start | bytes 1572868
  0.6 23.7 %copy-start = (bf16[8,128,256]{2,1,0:T(8,128)(2,1)S(1)}, bf16[8,128,256]{2,1,0:T(8,128)(2,1)}, u32[]{:S(2)}) copy-start(bf16[8,128,256]{2,1,0:T(8,128)(2,1)} %refs_0_.1) | copy-start | bytes 1572868
  1.6 5.7 %collective-permute-start = (bf16[24,1024]{1,0:T(8,128)(2,1)S(1)}, bf16[24,1024]{1,0:T(8,128)(2,1)S(1)}, u32[]{:S(2)}, u32[]{:S(2)}) collective-permute-start(bf16[24,1024]{1,0:T(8,128)(2,1)S(1)} %get-tuple-element.39), channel_id=1, source_target_pairs={{0,4},{2,6},{4,0},{6,2},{8,12},{10,14},{12,8},{14,10},{16,20},{18,... | collective-permute-start | bytes 147464 | tf_op jit(solution)/shard_map/ppermute | solution.py:467
  5.9 23.1 %copy-start.3 = (s32[2,8]{1,0:T(2,128)S(1)}, s32[2,8]{1,0:T(2,128)}, u32[]{:S(2)}) copy-start(s32[2,8]{1,0:T(2,128)} %len_ref.3) | copy-start | bytes 196
  6.0 18.4 %collective-permute-start.6 = (bf16[2,8,128,128]{3,2,1,0:T(8,128)(2,1)S(1)}, bf16[2,8,128,128]{3,2,1,0:T(8,128)(2,1)S(1)}, u32[]{:S(2)}, u32[]{:S(2)}) collective-permute-start(bf16[2,8,128,128]{3,2,1,0:T(8,128)(2,1)S(1)} %pad_maximum_fusion), channel_id=1, source_target_pairs={{0,2},{2,0},{4,6},{6,4},{8,10},{10,8},{12,14},{14,12},{16,18},{18,... | collective-permute-start | bytes 1572872 | tf_op jit(solution)/shard_map/ppermute | solution.py:467
  6.1 14.4 %collective-permute-start.7 = (bf16[2,8,128,128]{3,2,1,0:T(8,128)(2,1)S(1)}, bf16[2,8,128,128]{3,2,1,0:T(8,128)(2,1)S(1)}, u32[]{:S(2)}, u32[]{:S(2)}) collective-permute-start(bf16[2,8,128,128]{3,2,1,0:T(8,128)(2,1)S(1)} %pad_maximum_fusion.1), channel_id=1, source_target_pairs={{0,4},{2,6},{4,0},{6,2},{8,12},{10,14},{12,8},{14,10},{16,20},{18,... | collective-permute-start | bytes 1572872 | tf_op jit(solution)/shard_map/ppermute | solution.py:467
  7.3 12.0 %collective-permute-start.8 = (bf16[48,1024]{1,0:T(8,128)(2,1)S(1)}, bf16[48,1024]{1,0:T(8,128)(2,1)S(1)}, u32[]{:S(2)}, u32[]{:S(2)}) collective-permute-start(bf16[48,1024]{1,0:T(8,128)(2,1)S(1)} %pad_maximum_fusion.2.awaited_ref.refs_1_), channel_id=1, source_target_pairs={{0,8},{2,10},{4,12},{6,14},{8,0},{10,2},{12,4},{14,6},{16,24},{18,... | collective-permute-start | bytes 294920 | tf_op jit(solution)/shard_map/ppermute | solution.py:467
  9.4 10.6 %collective-permute-start.2 = (bf16[48,1024]{1,0:T(8,128)(2,1)S(1)}, bf16[48,1024]{1,0:T(8,128)(2,1)S(1)}, u32[]{:S(2)}, u32[]{:S(2)}) collective-permute-start(bf16[48,1024]{1,0:T(8,128)(2,1)S(1)} %pad_maximum_fusion.2.awaited_ref.refs_1_), channel_id=1, source_target_pairs={{0,16},{2,18},{4,20},{6,22},{8,24},{10,26},{12,28},{14,30},{16,0},... | collective-permute-start | bytes 294920 | tf_op jit(solution)/shard_map/ppermute | solution.py:467
  12.0 8.0 %collective-permute-start.1 = (bf16[48,1024]{1,0:T(8,128)(2,1)S(1)}, bf16[48,1024]{1,0:T(8,128)(2,1)S(1)}, u32[]{:S(2)}, u32[]{:S(2)}) collective-permute-start(bf16[48,1024]{1,0:T(8,128)(2,1)S(1)} %pad_maximum_fusion.2.awaited_ref.refs_1_), channel_id=1, source_target_pairs={{0,24},{2,26},{4,28},{6,30},{8,16},{10,18},{12,20},{14,22},{16,8},... | collective-permute-start | bytes 294920 | tf_op jit(solution)/shard_map/ppermute | solution.py:467
  12.0 0.7 %copy-start.4 = (s32[128]{0:T(128)S(1)}, s32[128]{0:T(128)}, u32[]{:S(2)}) copy-start(s32[128]{0:T(128)} %table.1) | copy-start | bytes 1540
  14.1 0.9 %copy-start.2 = (bf16[24,4096]{1,0:T(8,128)(2,1)S(1)}, bf16[24,4096]{1,0:T(8,128)(2,1)}, u32[]{:S(2)}) copy-start(bf16[24,4096]{1,0:T(8,128)(2,1)} %hidden_ref.1) | copy-start | bytes 589828
  20.5 3.8 %collective-permute-start.9 = (bf16[2,8,128,128]{3,2,1,0:T(8,128)(2,1)S(1)}, bf16[2,8,128,128]{3,2,1,0:T(8,128)(2,1)S(1)}, u32[]{:S(2)}, u32[]{:S(2)}) collective-permute-start(bf16[2,8,128,128]{3,2,1,0:T(8,128)(2,1)S(1)} %shard_map.97.refs_3_), channel_id=1, source_target_pairs={{0,2},{2,0},{4,6},{6,4},{8,10},{10,8},{12,14},{14,12},{16,18},{18,... | collective-permute-start | bytes 1572872 | tf_op jit(solution)/shard_map/ppermute | solution.py:467
  20.7 6.8 %collective-permute-start.4 = (f32[24,256]{1,0:T(8,128)S(1)}, f32[24,256]{1,0:T(8,128)S(1)}, u32[]{:S(2)}, u32[]{:S(2)}) collective-permute-start(f32[24,256]{1,0:T(8,128)S(1)} %get-tuple-element.20), channel_id=1, source_target_pairs={{0,4},{1,5},{2,6},{3,7},{4,0},{5,1},{6,2},{7,3},{8,12},{9,13},{10,... | collective-permute-start | bytes 73736 | tf_op jit(solution)/shard_map/ppermute | solution.py:479
  21.9 5.6 %collective-permute-start.5 = (f32[24,256]{1,0:T(8,128)S(1)}, f32[24,256]{1,0:T(8,128)S(1)}, u32[]{:S(2)}, u32[]{:S(2)}) collective-permute-start(f32[24,256]{1,0:T(8,128)S(1)} %get-tuple-element.21), channel_id=1, source_target_pairs={{0,5},{1,4},{2,7},{3,6},{4,1},{5,0},{6,3},{7,2},{8,13},{9,12},{10,... | collective-permute-start | bytes 73736 | tf_op jit(solution)/shard_map/ppermute | solution.py:479
  23.7 4.1 %collective-permute-start.3 = (f32[24,512]{1,0:T(8,128)S(1)}, f32[24,512]{1,0:T(8,128)S(1)}, u32[]{:S(2)}, u32[]{:S(2)}) collective-permute-start(f32[24,512]{1,0:T(8,128)S(1)} %get-tuple-element.19), channel_id=1, source_target_pairs={{0,1},{1,0},{2,3},{3,2},{4,5},{5,4},{6,7},{7,6},{8,9},{9,8},{10,11... | collective-permute-start | bytes 147464 | tf_op jit(solution)/shard_map/ppermute | solution.py:479
  34.2 12.9 %collective-permute-start.10 = (bf16[400,128]{1,0:T(8,128)(2,1)S(1)}, bf16[400,128]{1,0:T(8,128)(2,1)S(1)}, u32[]{:S(2)}, u32[]{:S(2)}) collective-permute-start(bf16[400,128]{1,0:T(8,128)(2,1)S(1)} %get-tuple-element.25), channel_id=1, source_target_pairs={{0,24},{2,26},{4,28},{6,30},{8,16},{10,18},{12,20},{14,22},{16,8},... | collective-permute-start | bytes 307208 | tf_op jit(solution)/shard_map/ppermute | solution.py:467
  37.1 10.0 %collective-permute-start.11 = (bf16[400,128]{1,0:T(8,128)(2,1)S(1)}, bf16[400,128]{1,0:T(8,128)(2,1)S(1)}, u32[]{:S(2)}, u32[]{:S(2)}) collective-permute-start(bf16[400,128]{1,0:T(8,128)(2,1)S(1)} %get-tuple-element.26), channel_id=1, source_target_pairs={{0,16},{2,18},{4,20},{6,22},{8,24},{10,26},{12,28},{14,30},{16,0},... | collective-permute-start | bytes 307208 | tf_op jit(solution)/shard_map/ppermute | solution.py:467
  42.3 5.3 %collective-permute-start.12 = (bf16[400,128]{1,0:T(8,128)(2,1)S(1)}, bf16[400,128]{1,0:T(8,128)(2,1)S(1)}, u32[]{:S(2)}, u32[]{:S(2)}) collective-permute-start(bf16[400,128]{1,0:T(8,128)(2,1)S(1)} %get-tuple-element.27), channel_id=1, source_target_pairs={{0,8},{2,10},{4,12},{6,14},{8,0},{10,2},{12,4},{14,6},{16,24},{18,... | collective-permute-start | bytes 307208 | tf_op jit(solution)/shard_map/ppermute | solution.py:467
  50.0 6.5 %collective-permute-start.13 = (bf16[24,2048]{1,0:T(8,128)(2,1)S(1)}, bf16[24,2048]{1,0:T(8,128)(2,1)S(1)}, u32[]{:S(2)}, u32[]{:S(2)}) collective-permute-start(bf16[24,2048]{1,0:T(8,128)(2,1)S(1)} %get-tuple-element.30), channel_id=1, source_target_pairs={{0,5},{1,4},{2,7},{3,6},{4,1},{5,0},{6,3},{7,2},{8,13},{9,12},{10,... | collective-permute-start | bytes 294920 | tf_op jit(solution)/shard_map/ppermute | solution.py:479
  51.7 5.2 %collective-permute-start.14 = (bf16[24,2048]{1,0:T(8,128)(2,1)S(1)}, bf16[24,2048]{1,0:T(8,128)(2,1)S(1)}, u32[]{:S(2)}, u32[]{:S(2)}) collective-permute-start(bf16[24,2048]{1,0:T(8,128)(2,1)S(1)} %get-tuple-element.31), channel_id=1, source_target_pairs={{0,1},{1,0},{2,3},{3,2},{4,5},{5,4},{6,7},{7,6},{8,9},{9,8},{10,11... | collective-permute-start | bytes 294920 | tf_op jit(solution)/shard_map/ppermute | solution.py:479
  52.2 5.0 %collective-permute-start.15 = (bf16[24,2048]{1,0:T(8,128)(2,1)S(1)}, bf16[24,2048]{1,0:T(8,128)(2,1)S(1)}, u32[]{:S(2)}, u32[]{:S(2)}) collective-permute-start(bf16[24,2048]{1,0:T(8,128)(2,1)S(1)} %get-tuple-element.32), channel_id=1, source_target_pairs={{0,4},{1,5},{2,6},{3,7},{4,0},{5,1},{6,2},{7,3},{8,12},{9,13},{10,... | collective-permute-start | bytes 294920 | tf_op jit(solution)/shard_map/ppermute | solution.py:479

commit v3 on v2

v3 whole, which is shorter than its diff:
```python
import functools
import math

import jax
import jax.numpy as jnp
from jax import lax
from jax.experimental import pallas as pl
from jax.experimental.pallas import tpu as pltpu
from jax.sharding import PartitionSpec as P

HD = 128
PAGE = 128
GROUPS = 2
REQS = 8
PLACE = 5
CHUNK = 4
BLOCKS = 2
AHEAD = 8
LOW = -1e30
EXP2_SCALE = math.log2(math.e) / math.sqrt(HD)
F32 = jnp.float32
BF16 = jnp.bfloat16
MIB = 1 << 20

NT = (((1,), (1,)), ((), ()))

VMEM = pl.BlockSpec(memory_space=pltpu.VMEM)
SMEM = pl.BlockSpec(memory_space=pltpu.SMEM)
ANY = pl.BlockSpec(memory_space=pl.ANY)
HBM = pl.BlockSpec(memory_space=pltpu.HBM)


TINY = pl.CostEstimate(flops=1, bytes_accessed=1, transcendentals=0)


def params(mib):
    return pltpu.CompilerParams(vmem_limit_bytes=mib * MIB)


def array_after(array, *awaited):
    def body(*refs):
        pass

    return pl.pallas_call(
        body,
        in_specs=[ANY] * (1 + len(awaited)),
        out_specs=ANY,
        out_shape=jax.ShapeDtypeStruct(array.shape, array.dtype),
        input_output_aliases={0: 0},
        compiler_params=params(2),
        cost_estimate=TINY,
    )(array, *awaited)


def project_kv(hidden_in, weight, table, ranks, slots, awaited):
    group_pages = (table.shape[0] - PLACE) // GROUPS
    rows, deep = hidden_in.shape
    width = weight.shape[1] // ranks
    steps = 8
    part = deep // steps

    def body(place_ref, hidden_ref, weight_ref, _, *refs):
        outs, (listed, buffer, sums, sem) = refs[:ranks], refs[ranks:]
        copies = [
            pltpu.make_async_copy(weight_ref.at[pl.ds(i * part, part)], buffer.at[i], sem.at[i])
            for i in range(steps)
        ]
        for copy in copies[:AHEAD]:
            copy.start()
        group, first = place_ref[0], place_ref[2]

        def look(i, number):
            slot = place_ref[PLACE + group * group_pages + i] - first
            here = jnp.logical_and(slot >= 0, slot < slots)
            listed[number + 1] = slot
            return number + here.astype(jnp.int32)

        listed[0] = lax.fori_loop(0, group_pages, look, jnp.int32(0), unroll=8)
        for i, copy in enumerate(copies):
            copy.wait()
            if i + AHEAD < steps:
                copies[i + AHEAD].start()
            product = jnp.dot(
                hidden_ref[:, i * part : (i + 1) * part],
                buffer[i],
                preferred_element_type=F32,
            )
            sums[...] = product if i == 0 else sums[...] + product
        for rank, out in enumerate(outs):
            start = pl.multiple_of(jnp.bitwise_xor(place_ref[4], rank) * width, width)
            out[...] = sums[:, pl.ds(start, width)]

    return pl.pallas_call(
        body,
        in_specs=[SMEM, VMEM, HBM, ANY],
        out_specs=[VMEM] * ranks + [SMEM],
        out_shape=[jax.ShapeDtypeStruct((rows, width), F32)] * ranks
        + [jax.ShapeDtypeStruct((slots + 2,), jnp.int32)],
        scratch_shapes=[
            pltpu.VMEM((steps, part, weight.shape[1]), BF16),
            pltpu.VMEM((rows, weight.shape[1]), F32),
            pltpu.SemaphoreType.DMA((steps,)),
        ],
        compiler_params=params(48),
        cost_estimate=TINY,
    )(table, hidden_in, weight, awaited)


def finish_kv(place, mine, others, cosine, sine, heads):
    rows = mine.shape[0]

    def body(place_ref, *refs):
        count = 1 + len(others)
        out, pieces = refs[count + 2], refs[count + 3 :]
        total = refs[0][...]
        for other in refs[1:count]:
            total = total + other[...]
        cos, sin = refs[count][...], refs[count + 1][...]
        for head in range(heads):
            key = total[:, head * 2 * HD : (head * 2 + 1) * HD]
            key = (key * cos + pltpu.roll(key, HD // 2, 1) * sin).astype(BF16)
            value = total[:, (head * 2 + 1) * HD : (head * 2 + 2) * HD].astype(BF16)
            out[:, head * 2 * HD : (head * 2 + 1) * HD] = key
            out[:, (head * 2 + 1) * HD : (head * 2 + 2) * HD] = value
            for step in range(heads):

                @pl.when(jnp.bitwise_xor(place_ref[1], step) == head)
                def _():
                    pieces[step][:, :HD] = key
                    pieces[step][:, HD:] = value

    return pl.pallas_call(
        body,
        in_specs=[SMEM] + [VMEM] * (3 + len(others)),
        out_specs=[VMEM] * (1 + heads),
        out_shape=[jax.ShapeDtypeStruct((rows, heads * 2 * HD), BF16)]
        + [jax.ShapeDtypeStruct((rows, 2 * HD), BF16)] * heads,
        compiler_params=params(4),
        cost_estimate=TINY,
    )(place, mine, *others, cosine, sine)


def collect_pages(listed, place, sources, pages, splits):
    slots = pages * splits * GROUPS

    def body(list_ref, place_ref, *refs):
        own_keys, own_values, *others = refs[: len(sources)]
        keys_out, values_out = refs[len(sources) :]
        here = place_ref[1] * GROUPS + place_ref[0]
        number = list_ref[0]

        def rows(i):
            return pl.ds(pl.multiple_of(i * PAGE, PAGE), PAGE)

        def collect(i, carry):
            slot = list_ref[1 + i]
            device = slot // pages
            page = slot - device * pages
            kind = jnp.bitwise_xor(device, here)

            @pl.when(kind == 0)
            def _():
                column = pl.ds(pl.multiple_of(place_ref[1] * HD, HD), HD)
                keys_out[rows(i), :] = own_keys[page, :, column]
                values_out[rows(i), :] = own_values[page, :, column]

            for which, other in enumerate(others):

                @pl.when(kind == which + 1)
                def _():
                    keys_out[rows(i), :] = other[0, page]
                    values_out[rows(i), :] = other[1, page]

            return carry

        lax.fori_loop(0, number, collect, 0)

        def clear(i, carry):
            values_out[rows(i), :] = jnp.zeros((PAGE, HD), BF16)
            return carry

        lax.fori_loop(number, jnp.minimum(number + CHUNK - 1, slots), clear, 0)

    return pl.pallas_call(
        body,
        in_specs=[SMEM, SMEM] + [VMEM] * len(sources),
        out_specs=[VMEM, VMEM],
        out_shape=[
            jax.ShapeDtypeStruct((slots * PAGE, HD), BF16),
            jax.ShapeDtypeStruct((slots * PAGE, HD), BF16),
        ],
        compiler_params=params(16),
        cost_estimate=TINY,
    )(listed, place, *sources)


def attend(listed, lengths, place, fars, queries, suffix, keys, values, rows_each, weight=None):
    fetched = [] if weight is None else [weight]
    tokens = queries[0].shape[0]
    splits = tokens // rows_each
    heads = queries[0].shape[1] // HD
    rows = tokens * heads
    slots = keys.shape[0] // PAGE
    wide = CHUNK * PAGE
    parts = -(-rows // HD)
    stat_rows = -(-3 * parts // 16) * 16
    blocks = len(queries)

    def body(list_ref, len_ref, place_ref, *refs):
        if fetched:
            weight_ref, rows_out, weight_sem = refs[0], refs[-8], refs[-1]
            refs = (*refs[1:-8], *refs[-7:-1])
            start = pl.multiple_of(place_ref[1] * heads * HD, heads * HD)
            copy = pltpu.make_async_copy(
                weight_ref.at[pl.ds(start, heads * HD)], rows_out, weight_sem
            )
            copy.start()
        query_refs, refs = refs[:blocks], refs[blocks:]
        suffix_refs, refs = refs[:splits], refs[splits:]
        keys_ref, values_ref, refs = refs[0], refs[1], refs[2:]
        outs, (stacked, scores, top, total, column, stats) = refs[:blocks], refs[blocks:]
        count = list_ref[0]
        turns = lax.div(count + (CHUNK - 1), CHUNK)
        group, split, z_here = place_ref[0], place_ref[1], place_ref[3]

        def places(z, axis):
            index = lax.broadcasted_iota(jnp.int32, (tokens, tokens), axis)
            result = jnp.zeros((tokens, tokens), jnp.int32)
            for sub in range(splits):
                block = z * splits + jnp.bitwise_xor(split, sub)
                result = jnp.where(
                    index >= sub * rows_each, (block - sub) * rows_each + index, result
                )
            return result

        own_kv = jnp.concatenate([ref[...].astype(F32) for ref in suffix_refs], axis=0).astype(BF16)
        own_keys = own_kv[:, :HD]
        own_values = jnp.concatenate([own_kv[:, HD:], jnp.ones((tokens, HD), BF16)], axis=1)
        key_place = places(z_here, 1)
        for b in range(blocks):
            q = jnp.concatenate(
                [query_refs[b][:, h * HD : (h + 1) * HD].astype(F32) for h in range(heads)], axis=0
            ).astype(BF16)
            stacked[b] = q
            query_place = places(jnp.bitwise_xor(z_here, fars[b]), 0)
            begins = jnp.zeros((tokens, tokens), jnp.int32)
            edge = jnp.int32(0)
            for r in range(REQS):
                edge = edge + len_ref[group, r]
                begins = jnp.where(query_place >= edge, edge, begins)
            seen = jnp.logical_and(key_place <= query_place, key_place >= begins)
            seen = jnp.concatenate([seen.astype(F32)] * heads, axis=0)
            own = lax.dot_general(q, own_keys, NT, preferred_element_type=F32)
            own = jnp.where(seen > 0.0, own, LOW)
            highest = jnp.max(own, axis=1, keepdims=True)
            weights = jnp.exp2((own - highest) * EXP2_SCALE) * seen
            total[b] = jnp.dot(weights.astype(BF16), own_values, preferred_element_type=F32)
            top[b] = jnp.broadcast_to(highest, (rows, HD))

        def score(b, c):
            span = pl.ds(pl.multiple_of(c * wide, wide), wide)
            scores[b] = lax.dot_general(
                stacked[b], keys_ref[span, :], NT, preferred_element_type=F32
            )

        def turn(c, carry):
            span = pl.ds(pl.multiple_of(c * wide, wide), wide)
            chunk_values = jnp.concatenate(
                [values_ref[span, :], jnp.ones((wide, HD), BF16)], axis=1
            )
            for b in range(blocks):
                pieces = [
                    jnp.where(c * CHUNK + j < count, scores[b, :, j * PAGE : (j + 1) * PAGE], LOW)
                    for j in range(CHUNK)
                ]
                best = functools.reduce(jnp.maximum, pieces)
                before = top[b]
                highest = jnp.maximum(before, jnp.max(best, axis=1, keepdims=True))
                weights = jnp.concatenate(
                    [jnp.exp2((piece - highest) * EXP2_SCALE).astype(BF16) for piece in pieces],
                    axis=1,
                )
                factor = jnp.exp2((before - highest) * EXP2_SCALE)
                added = jnp.dot(weights, chunk_values, preferred_element_type=F32)
                total[b] = total[b] * jnp.concatenate([factor, factor], axis=1) + added
                top[b] = highest
                score(b, jnp.minimum(c + 1, slots // CHUNK - 1))
            return carry

        for b in range(blocks):
            score(b, 0)
        lax.fori_loop(0, turns, turn, 0)
        for b in range(blocks):
            sums = total[b, :, HD:]
            some = sums > 0.0
            safe = jnp.where(some, sums, 1.0)
            outs[b][0:rows, :] = (total[b, :, :HD] / safe).astype(BF16)
            column[0:rows, :] = jnp.where(some, top[b] * EXP2_SCALE + jnp.log2(safe), LOW)
            stats[...] = jnp.zeros((stat_rows, HD), F32)
            for part in range(parts):
                line = column[part * HD : (part + 1) * HD, :].T[0:1, :]
                for piece in range(3):
                    rounded = line.astype(BF16).astype(F32)
                    stats[3 * part + piece : 3 * part + piece + 1, :] = rounded
                    line = line - rounded
            outs[b][rows : rows + stat_rows, :] = stats[...].astype(BF16)
        if fetched:
            copy.wait()

    return pl.pallas_call(
        body,
        in_specs=[SMEM, SMEM, SMEM] + [HBM] * len(fetched) + [VMEM] * (blocks + splits + 2),
        out_specs=[VMEM] * blocks + [ANY] * len(fetched),
        out_shape=[jax.ShapeDtypeStruct((rows + stat_rows, HD), BF16)] * blocks
        + [jax.ShapeDtypeStruct((heads * HD, array.shape[1]), BF16) for array in fetched],
        scratch_shapes=[
            pltpu.VMEM((blocks, rows, HD), BF16),
            pltpu.VMEM((blocks, rows, wide), F32),
            pltpu.VMEM((blocks, rows, HD), F32),
            pltpu.VMEM((blocks, rows, 2 * HD), F32),
            pltpu.VMEM((parts * HD, HD), F32),
            pltpu.VMEM((stat_rows, HD), F32),
        ]
        + [pltpu.SemaphoreType.DMA] * len(fetched),
        compiler_params=params(40 if fetched else 16),
        cost_estimate=pl.CostEstimate(
            flops=4 * blocks * rows * slots * PAGE * HD,
            bytes_accessed=slots * PAGE * HD * 3,
            transcendentals=blocks * rows * slots * PAGE // 2,
        ),
    )(listed, lengths, place, *fetched, *queries, *suffix, keys, values)


def project(place, partials, weight, rows_each, splits, ranks, heads):
    tokens = rows_each * splits
    rows = tokens * heads
    parts = -(-rows // HD)
    width = weight.shape[1] // ranks

    def body(place_ref, *refs):
        count = len(partials)
        partial_refs, weight_ref, outs = refs[:count], refs[count], refs[count + 1 : -2]
        merged, attended = refs[-2:]
        for part in range(parts):
            length = min(HD, rows - part * HD)
            lines = []
            for ref in partial_refs:
                stat = ref[rows:, :].astype(F32)
                lines.append(
                    stat[3 * part : 3 * part + 1]
                    + stat[3 * part + 1 : 3 * part + 2]
                    + stat[3 * part + 2 : 3 * part + 3]
                )
            best = functools.reduce(jnp.maximum, lines)
            shares = [jnp.exp2(line - best) for line in lines]
            whole = functools.reduce(jnp.add, shares)
            mixed = jnp.zeros((length, HD), F32)
            for share, ref in zip(shares, partial_refs):
                factor = jnp.broadcast_to(share / whole, (HD, HD)).T[:length]
                mixed = mixed + factor * ref[part * HD : part * HD + length, :].astype(F32)
            merged[part * HD : part * HD + length, :] = mixed
        for h in range(heads):
            attended[:, h * HD : (h + 1) * HD] = merged[h * tokens : (h + 1) * tokens, :].astype(
                BF16
            )
        for rank in range(ranks):
            start = pl.multiple_of(jnp.bitwise_xor(place_ref[4], rank) * width, width)
            product = jnp.dot(
                attended[...], weight_ref[:, pl.ds(start, width)], preferred_element_type=F32
            )
            for sub in range(splits):
                out = outs[rank * splits + sub]
                out[...] = product[sub * rows_each : (sub + 1) * rows_each].astype(out.dtype)

    return pl.pallas_call(
        body,
        in_specs=[SMEM] + [VMEM] * (len(partials) + 1),
        out_specs=[VMEM] * (ranks * splits),
        out_shape=[
            jax.ShapeDtypeStruct((rows_each, width), BF16 if i else F32)
            for i in range(ranks * splits)
        ],
        scratch_shapes=[pltpu.VMEM((rows, HD), F32), pltpu.VMEM((tokens, heads * HD), BF16)],
        compiler_params=params(16),
        cost_estimate=pl.CostEstimate(
            flops=2 * tokens * weight.size, bytes_accessed=weight.size, transcendentals=0
        ),
    )(place, *partials, weight)


def local(
    hidden_in,
    kv_weight,
    queries,
    prefix_keys,
    prefix_values,
    page_table,
    suffix_lengths,
    out_weight,
):
    rows = hidden_in.shape[0]
    seq_count, ranks = lax.axis_size("seq"), lax.axis_size("tp")
    seq_rank, tp_rank = lax.axis_index("seq"), lax.axis_index("tp")
    pages = prefix_keys.shape[0]
    splits = prefix_keys.shape[2] // HD
    heads = queries.shape[1] // HD // splits
    prefix_len = pages * seq_count // GROUPS * PAGE
    blocks = seq_count // GROUPS
    depth = blocks // splits
    group = seq_rank % GROUPS
    block = seq_rank // GROUPS
    split = block % splits
    place = jnp.stack(
        [group, split, (block - split) * GROUPS * pages, block // splits, tp_rank]
    ).astype(jnp.int32)
    place = jnp.concatenate([place, page_table])

    def across(array, far=0, side=0, core=0):
        step = (far * splits + side) * GROUPS + core
        return lax.ppermute(array, "seq", [(i, i ^ step) for i in range(seq_count)])

    def columns(array, index, width):
        return lax.dynamic_slice_in_dim(array, index * width, width, 1)

    def quad(array, rank, side):
        step = side * GROUPS
        route = [
            (i * ranks + j, (i ^ step) * ranks + (j ^ rank))
            for i in range(seq_count)
            for j in range(ranks)
        ]
        return lax.ppermute(array, ("seq", "tp"), route)

    def columns(array, index, width):
        return lax.dynamic_slice_in_dim(array, index * width, width, array.ndim - 1)

    parts = [columns(queries, split, heads * HD)]
    for side in range(1, splits):
        parts.append(across(columns(queries, split ^ side, heads * HD), side=side))
    my_query = jnp.concatenate(parts, axis=0)
    far_queries = [my_query] + [across(my_query, far=far) for far in range(1, depth)]
    sent = [
        jnp.stack([columns(array, split ^ side, HD) for array in (prefix_keys, prefix_values)])
        for side in range(splits)
    ]
    arrived = [across(sent[side], side=side) for side in range(1, splits)]
    sources = [prefix_keys, prefix_values, across(sent[0], core=1)]

    *projected, listed = project_kv(
        hidden_in, kv_weight, place, ranks, pages * splits * GROUPS, my_query
    )
    others = [
        lax.ppermute(projected[rank], "tp", [(i, i ^ rank) for i in range(ranks)])
        for rank in range(1, ranks)
    ]
    lengths = jnp.sum(
        jnp.where(jnp.arange(GROUPS)[:, None] == group, suffix_lengths, 0), axis=0
    )
    ends = jnp.sum(
        jnp.where(jnp.arange(REQS)[None, :] <= jnp.arange(REQS)[:, None], lengths[None, :], 0),
        axis=1,
    )
    within = block * rows + jnp.arange(rows, dtype=jnp.int32)
    begins = jnp.max(jnp.where(within[:, None] >= ends[None, :], ends[None, :], 0), axis=1)
    positions = prefix_len + within - begins
    half = HD // 2
    frequency = jnp.power(500000.0, -(jnp.arange(half, dtype=F32) * 2.0 / HD))
    angles = positions.astype(F32)[:, None] * frequency[None, :]
    cosine, sine = jnp.cos(angles), jnp.sin(angles)
    cosine = jnp.concatenate([cosine, cosine], axis=1)
    sine = jnp.concatenate([-sine, sine], axis=1)
    new_pages, *suffix = finish_kv(place, projected[0], others, cosine, sine, splits)
    suffix = suffix[:1] + [across(suffix[side], side=side) for side in range(1, splits)]

    for array in arrived:
        array = array_after(array, *others, *far_queries[1:])
        sources += [array, across(array, core=1)]
    keys, values = collect_pages(listed, place, sources, pages, splits)

    returned = []
    order = list(range(depth - 1, -1, -1))
    calls = [order[i : i + BLOCKS] for i in range(0, depth - BLOCKS, BLOCKS)]
    calls += [[far] for far in order[len(calls) * BLOCKS :]]
    for i, fars in enumerate(calls):
        sums = attend(
            listed, suffix_lengths, place, fars, [far_queries[far] for far in fars],
            suffix, keys, values, rows, None if i else out_weight,
        )
        if not i:
            weight = sums[-1]
        returned += [across(part, far=far) if far else part for far, part in zip(fars, sums)]

    products = project(place, returned, weight, rows, splits, ranks, heads)
    hidden = products[0]
    for rank in range(ranks - 1, -1, -1):
        for side in range(splits - 1, -1, -1):
            if rank or side:
                hidden = hidden + quad(products[rank * splits + side], rank, side).astype(F32)
    return (hidden.astype(BF16), new_pages)


def solution(mesh):
    return jax.shard_map(
        local,
        mesh=mesh,
        in_specs=(
            P("seq", "tp"),
            P("tp", None),
            P("seq", "tp"),
            P("seq", None, "tp"),
            P("seq", None, "tp"),
            P(),
            P(),
            P("tp", None),
        ),
        out_specs=(P("seq", "tp"), P("seq", "tp")),
        check_vma=False,
    )
```

time: 58.3 us -> 57.3 us (0.983)
  Pallas kernels: 26.6 us -> 21.2 us
  waiting for transfers between devices: 5.76 us -> 9.37 us
  starting transfers between devices: 18.7 us -> 19.9 us
    pallas_call x7 -> x6, Pallas kernels: 24.4 us -> 18.9 us  [the longest x3 11.7 us: attend(): pl.pallas_call(body, in_specs=[SMEM, SMEM, SMEM] + [HBM] * len(fetched) +...]
    ppermute x6 -> x3, starting transfers between devices: 7.11 us -> 3.55 us  [quad(): return lax.ppermute(array, ('seq', 'tp'), route)]
    ppermute x10 -> x11, starting transfers between devices: 11.6 us -> 14.6 us  [across(): return lax.ppermute(array, 'seq', [(i, i ^ step) for i in range(seq_count)])]
    ppermute x0 -> x1, waiting for transfers between devices: none -> 2.44 us  [local(): lax.ppermute(projected[rank], 'tp', [(i, i ^ rank) for i in range(ranks)])]
    ppermute x0 -> x1, starting transfers between devices: none -> 1.7 us  [local(): lax.ppermute(projected[rank], 'tp', [(i, i ^ rank) for i in range(ranks)])]
    ppermute x6 -> x3, waiting for transfers between devices: 4.08 us -> 5.03 us  [quad(): return lax.ppermute(array, ('seq', 'tp'), route)]
    concatenate x0 -> x1, local copies, waits for them, and re-layouts: none -> 0.73 us  [local(): place = jnp.concatenate([place, page_table])]
    unnamed x10 -> x8, local copies, waits for them, and re-layouts: 1.59 us -> 0.94 us
  transfers between devices with their start and end apart: 16 -> 15, of which waited for: 7 -> 7; matrix products, arithmetic and copies ran while one was open for 5% -> 6% of each run, Pallas kernels for 31% -> 24%
where the time goes in v3:
time: 57.3 us; the launch traced here: 57.1 us
  Pallas kernels  21.2 us (37%)
  starting transfers between devices  19.9 us (35%)
  waiting for transfers between devices  9.37 us (16%)
  local copies, waits for them, and re-layouts  3.86 us (7%)
  other arithmetic  2 us (3%)
  between operations  0.83 us (1%)
    ppermute x11, starting transfers between devices, across(): return lax.ppermute(array, 'seq', [(i, i ^ step) for i in range(seq_count)])  14.6 us
    pallas_call x3, Pallas kernels, attend(): pl.pallas_call(body, in_specs=[SMEM, SMEM, SMEM] + [HBM] * len(fetched) +...  11.7 us
    ppermute x3, waiting for transfers between devices, quad(): return lax.ppermute(array, ('seq', 'tp'), route)  5.03 us
    pallas_call x1, Pallas kernels, project_kv(): pl.pallas_call(body, in_specs=[SMEM, VMEM, HBM, ANY], out_specs=[VMEM] *...  4.61 us
    ppermute x3, starting transfers between devices, quad(): return lax.ppermute(array, ('seq', 'tp'), route)  3.55 us
    ppermute x1, waiting for transfers between devices, local(): lax.ppermute(projected[rank], 'tp', [(i, i ^ rank) for i in range(ranks)])  2.44 us
    pallas_call x1, Pallas kernels, project(): pl.pallas_call(body, in_specs=[SMEM] + [VMEM] * (len(partials) + 1), out_...  2.31 us
    ppermute x11, waiting for transfers between devices, across(): return lax.ppermute(array, 'seq', [(i, i ^ step) for i in range(seq_count)])  1.9 us
  transfers between devices with their start and end apart: 15, of which 7 were waited for; matrix products, arithmetic and copies ran while one was open for 6% of the time, Pallas kernels for 24%

profile of v3, /device:TPU:0, one launch (start us, length us, event | category | flops | bytes accessed | tf_op | source)
XLA Modules:
  0.0 57.1 jit_solution(13642610701842547122)
XLA Ops:
  0.6 0.0 copy-start
  0.6 0.0 copy-start.1
  0.7 0.9 %constant_dynamic-slice_fusion.1 = (bf16[24,1024]{1,0:T(8,128)(2,1)S(1)}, bf16[24,1024]{1,0:T(8,128)(2,1)S(1)}) fusion(bf16[24,2048]{1,0:T(8,128)(2,1)} %param.10, s32[]{:T(128)S(6)} %select_n.48, s32[]{:T(128)S(6)} %select_n.49), kind=kLoop, calls=%fused_computation.17 | loop fusion | bytes 196616 | tf_op jit(solution)/shard_map/dynamic_slice | solution.py:435
  1.6 3.0 %collective-permute-start = (bf16[24,1024]{1,0:T(8,128)(2,1)S(1)}, bf16[24,1024]{1,0:T(8,128)(2,1)S(1)}, u32[]{:S(2)}, u32[]{:S(2)}) collective-permute-start(bf16[24,1024]{1,0:T(8,128)(2,1)S(1)} %get-tuple-element.37), channel_id=1, source_target_pairs={{0,4},{2,6},{4,0},{6,2},{8,12},{10,14},{12,8},{14,10},{16,20},{18,... | collective-permute-start | bytes 147464 | tf_op jit(solution)/shard_map/ppermute | solution.py:420
  4.6 1.3 %dynamic-slice_bitcast_fusion = (bf16[1,8,128,128]{3,2,1,0:T(8,128)(2,1)S(1)}, bf16[1,8,128,128]{3,2,1,0:T(8,128)(2,1)S(1)}, bf16[1,8,128,128]{3,2,1,0:T(8,128)(2,1)S(1)}, bf16[1,8,128,128]{3,2,1,0:T(8,128)(2,1)S(1)}) fusion(bf16[8,128,256]{2,1,0:T(8,128)(2,1)} %refs_1_.1, s32[]{:T(128)S(6)} %select_n.54, s32[]{:T(128)S(6)} %select_n.53, ...), kind=kLoop, calls=%fused_computation.2 | loop fusion | bytes 2097160 | tf_op jit(solution)/shard_map/stack | solution.py:443
  5.9 0.1 pad_maximum_fusion.1
  6.0 0.1 collective-permute-start.6
  6.1 0.8 %select_reduce_fusion.2 = s32[8]{0:T(128)S(1)} fusion(s32[2,8]{1,0:T(2,128)} %len_ref.5, pred[2]{0:T(512)(128)(4,1)S(1)} %iota_compare_fusion.1), kind=kLoop, calls=%fused_computation.18 | loop fusion | flops 24 | bytes 98 | tf_op jit(solution)/shard_map/reduce_sum | solution.py:456
  6.8 0.1 select_reduce_fusion.1
  7.0 0.1 pad_maximum_fusion
  7.0 0.1 select_reduce_fusion
  7.1 0.7 %concatenate.12.place_ref = s32[133]{0:T(256)S(1)} concatenate(s32[1]{0:T(128)} %bitcast, s32[1]{0:T(128)} %bitcast.1, s32[1]{0:T(128)} %bitcast.2, s32[1]{0:T(128)} %bitcast.3, s32[1]{0:T(128)} %bitcast.4, s32[128]{0:T(128)} %param.13), dimensions={0} | concatenate | bytes 1064 | tf_op jit(solution)/shard_map/concatenate | solution.py:416
  7.8 0.0 collective-permute-done
  7.9 4.1 %collective-permute-start.1 = (bf16[48,1024]{1,0:T(8,128)(2,1)S(1)}, bf16[48,1024]{1,0:T(8,128)(2,1)S(1)}, u32[]{:S(2)}, u32[]{:S(2)}) collective-permute-start(bf16[48,1024]{1,0:T(8,128)(2,1)S(1)} %pad_maximum_fusion.2._.refs_0_), channel_id=1, source_target_pairs={{0,24},{2,26},{4,28},{6,30},{8,16},{10,18},{12,20},{14,22},{16,8},... | collective-permute-start | bytes 294920 | tf_op jit(solution)/shard_map/ppermute | solution.py:420
  12.0 0.0 collective-permute-start.2
  12.0 0.6 %collective-permute-start.7 = (bf16[48,1024]{1,0:T(8,128)(2,1)S(1)}, bf16[48,1024]{1,0:T(8,128)(2,1)S(1)}, u32[]{:S(2)}, u32[]{:S(2)}) collective-permute-start(bf16[48,1024]{1,0:T(8,128)(2,1)S(1)} %pad_maximum_fusion.2._.refs_0_), channel_id=1, source_target_pairs={{0,8},{2,10},{4,12},{6,14},{8,0},{10,2},{12,4},{14,6},{16,24},{18,... | collective-permute-start | bytes 294920 | tf_op jit(solution)/shard_map/ppermute | solution.py:420
  12.6 0.9 %copy-done.2 = bf16[24,4096]{1,0:T(8,128)(2,1)S(1)} copy-done((bf16[24,4096]{1,0:T(8,128)(2,1)S(1)}, bf16[24,4096]{1,0:T(8,128)(2,1)}, u32[]{:S(2)}) %copy-start.2) | copy-done | bytes 196632
  13.6 4.6 %shard_map.95 = (f32[24,512]{1,0:T(8,128)S(1)}, f32[24,512]{1,0:T(8,128)S(1)}, s32[34]{0:T(128)S(1)}) custom-call(s32[133]{0:T(256)S(1)} %concatenate.12.place_ref, bf16[24,4096]{1,0:T(8,128)(2,1)S(1)} %copy-done.2, bf16[4096,1024]{1,0:T(8,128)(2,1)} %weight_ref.1, bf16[48,1024]{1,0:T(8,128)(2,1)S(1)} %pad_maximum_fusion.2._.refs_0_), custom_call_target="tpu_custom_call" | custom-call | flops 1 | bytes 1 | tf_op jit(solution)/shard_map/pallas_call | solution.py:93
  18.2 1.7 %collective-permute-start.3 = (f32[24,512]{1,0:T(8,128)S(1)}, f32[24,512]{1,0:T(8,128)S(1)}, u32[]{:S(2)}, u32[]{:S(2)}) collective-permute-start(f32[24,512]{1,0:T(8,128)S(1)} %get-tuple-element.19), channel_id=1, source_target_pairs={{0,1},{1,0},{2,3},{3,2},{4,5},{5,4},{6,7},{7,6},{8,9},{9,8},{10,11... | collective-permute-start | bytes 147464 | tf_op jit(solution)/shard_map/ppermute | solution.py:453
  19.9 2.4 %collective-permute-done.3.refs_1_ = f32[24,512]{1,0:T(8,128)S(1)} collective-permute-done((f32[24,512]{1,0:T(8,128)S(1)}, f32[24,512]{1,0:T(8,128)S(1)}, u32[]{:S(2)}, u32[]{:S(2)}) %collective-permute-start.3) | collective-permute-done | bytes 49184 | tf_op jit(solution)/shard_map/ppermute | solution.py:453
  22.3 0.0 collective-permute-start.5
  22.3 0.0 collective-permute-done.1.refs_4_.refs_1_
  22.4 0.0 collective-permute-done.7.refs_2_.refs_0_
  22.4 0.6 collective-permute-start.8
  23.0 0.1 fusion
  23.1 0.1 pad_maximum_fusion.3
  23.2 1.3 %shard_map.96 = (bf16[24,512]{1,0:T(8,128)(2,1)}, bf16[24,256]{1,0:T(8,128)(2,1)S(1)}, bf16[24,256]{1,0:T(8,128)(2,1)S(1)}) custom-call(s32[133]{0:T(256)S(1)} %concatenate.12.place_ref, f32[24,512]{1,0:T(8,128)S(1)} %get-tuple-element.18.refs_0_, f32[24,512]{1,0:T(8,128)S(1)} %collective-permute-done.3.refs_1_, f32[24,128]{1,0:T(8,128)S(1)} %get-tuple-element.41.refs_2_, ...), custom_call_target="tpu_custom_call" | custom-call | flops 1 | bytes 1 | tf_op jit(solution)/shard_map/pallas_call | solution.py:132
  24.5 1.7 %collective-permute-start.4 = (bf16[24,256]{1,0:T(8,128)(2,1)S(1)}, bf16[24,256]{1,0:T(8,128)(2,1)S(1)}, u32[]{:S(2)}, u32[]{:S(2)}) collective-permute-start(bf16[24,256]{1,0:T(8,128)(2,1)S(1)} %get-tuple-element.21), channel_id=1, source_target_pairs={{0,4},{2,6},{4,0},{6,2},{8,12},{10,14},{12,8},{14,10},{16,20},{18,... | collective-permute-start | bytes 36872 | tf_op jit(solution)/shard_map/ppermute | solution.py:420
  26.1 0.0 collective-permute-done.5.refs_2_
  26.2 0.0 collective-permute-done.8.refs_4_
  26.2 1.3 %shard_map.98 = (bf16[4096,128]{1,0:T(8,128)(2,1)S(1)}, bf16[4096,128]{1,0:T(8,128)(2,1)S(1)}) custom-call(s32[34]{0:T(128)S(1)} %get-tuple-element.17.list_ref, s32[133]{0:T(256)S(1)} %concatenate.12.place_ref, bf16[8,128,256]{2,1,0:T(8,128)(2,1)S(1)} %copy-done, bf16[8,128,256]{2,1,0:T(8,128)(2,1)S(1)} %copy-done.1, ...), custom_call_target="tpu_custom_call" | custom-call | flops 1 | bytes 1 | tf_op jit(solution)/shard_map/pallas_call | solution.py:184
  27.5 0.7 %collective-permute-done.4.refs_4_.refs_2_ = bf16[24,256]{1,0:T(8,128)(2,1)S(1)} collective-permute-done((bf16[24,256]{1,0:T(8,128)(2,1)S(1)}, bf16[24,256]{1,0:T(8,128)(2,1)S(1)}, u32[]{:S(2)}, u32[]{:S(2)}) %collective-permute-start.4) | collective-permute-done | bytes 12320 | tf_op jit(solution)/shard_map/ppermute | solution.py:420
  28.2 5.0 %shard_map.99 = (bf16[400,128]{1,0:T(8,128)(2,1)S(1)}, bf16[400,128]{1,0:T(8,128)(2,1)S(1)}, bf16[1024,4096]{1,0:T(8,128)(2,1)S(1)}) custom-call(s32[34]{0:T(128)S(1)} %get-tuple-element.17.list_ref, s32[2,8]{1,0:T(2,128)S(1)} %copy-done.3, s32[133]{0:T(256)S(1)} %concatenate.12.place_ref, bf16[2048,4096]{1,0:T(8,128)(2,1)} %refs_0_.3, ...), custom_call_target="tpu_custom_call" | custom-call | flops 1610612736 | bytes 1572864 | tf_op jit(solution)/shard_map/pallas_call | solution.py:310
  33.1 3.2 %collective-permute-start.9 = (bf16[400,128]{1,0:T(8,128)(2,1)S(1)}, bf16[400,128]{1,0:T(8,128)(2,1)S(1)}, u32[]{:S(2)}, u32[]{:S(2)}) collective-permute-start(bf16[400,128]{1,0:T(8,128)(2,1)S(1)} %get-tuple-element.24), channel_id=1, source_target_pairs={{0,24},{2,26},{4,28},{6,30},{8,16},{10,18},{12,20},{14,22},{16,8},... | collective-permute-start | bytes 307208 | tf_op jit(solution)/shard_map/ppermute | solution.py:420
  36.3 3.3 %shard_map.100 = bf16[400,128]{1,0:T(8,128)(2,1)S(1)} custom-call(s32[34]{0:T(128)S(1)} %get-tuple-element.17.list_ref, s32[2,8]{1,0:T(2,128)S(1)} %copy-done.3, s32[133]{0:T(256)S(1)} %concatenate.12.place_ref, bf16[48,1024]{1,0:T(8,128)(2,1)S(1)} %collective-permute-done.7.refs_2_.refs_0_, bf16[24,256]{1,0:T(8,128)(2,1)S(1)} %get-tuple-element.20.refs_3_.refs_1_, ...), custom_call_target="tpu_custom_call" | custom-call | flops 805306368 | bytes 1572864 | tf_op jit(solution)/shard_map/pallas_call | solution.py:310
  39.7 1.3 %collective-permute-start.11 = (bf16[400,128]{1,0:T(8,128)(2,1)S(1)}, bf16[400,128]{1,0:T(8,128)(2,1)S(1)}, u32[]{:S(2)}, u32[]{:S(2)}) collective-permute-start(bf16[400,128]{1,0:T(8,128)(2,1)S(1)} %shard_map.100), channel_id=1, source_target_pairs={{0,8},{2,10},{4,12},{6,14},{8,0},{10,2},{12,4},{14,6},{16,24},{18,... | collective-permute-start | bytes 307208 | tf_op jit(solution)/shard_map/ppermute | solution.py:420
  41.0 3.4 %shard_map.101.refs_3_ = bf16[400,128]{1,0:T(8,128)(2,1)S(1)} custom-call(s32[34]{0:T(128)S(1)} %get-tuple-element.17.list_ref, s32[2,8]{1,0:T(2,128)S(1)} %copy-done.3, s32[133]{0:T(256)S(1)} %concatenate.12.place_ref, bf16[48,1024]{1,0:T(8,128)(2,1)S(1)} %pad_maximum_fusion.2._.refs_0_, bf16[24,256]{1,0:T(8,128)(2,1)S(1)} %get-tuple-element.20.refs_3_.refs_1_, ...), custom_call_target="tpu_custom_call" | custom-call | flops 805306368 | bytes 1572864 | tf_op jit(solution)/shard_map/pallas_call | solution.py:310
  44.4 0.0 collective-permute-done.9.refs_0_
  44.4 0.1 collective-permute-done.10.refs_1_
  44.5 1.0 %collective-permute-done.11.refs_2_ = bf16[400,128]{1,0:T(8,128)(2,1)S(1)} collective-permute-done((bf16[400,128]{1,0:T(8,128)(2,1)S(1)}, bf16[400,128]{1,0:T(8,128)(2,1)S(1)}, u32[]{:S(2)}, u32[]{:S(2)}) %collective-permute-start.11) | collective-permute-done | bytes 102432 | tf_op jit(solution)/shard_map/ppermute | solution.py:420
  45.5 2.3 %shard_map.102 = (f32[24,2048]{1,0:T(8,128)S(1)}, bf16[24,2048]{1,0:T(8,128)(2,1)S(1)}, bf16[24,2048]{1,0:T(8,128)(2,1)S(1)}, bf16[24,2048]{1,0:T(8,128)(2,1)S(1)}) custom-call(s32[133]{0:T(256)S(1)} %concatenate.12.place_ref, bf16[400,128]{1,0:T(8,128)(2,1)S(1)} %collective-permute-done.9.refs_0_, bf16[400,128]{1,0:T(8,128)(2,1)S(1)} %collective-permute-done.10.refs_1_, ...), custom_call_target="tpu_custom_call" | custom-call | flops 402653184 | bytes 4194304 | tf_op jit(solution)/shard_map/pallas_call | solution.py:375
  47.8 1.6 %collective-permute-start.14 = (bf16[24,2048]{1,0:T(8,128)(2,1)S(1)}, bf16[24,2048]{1,0:T(8,128)(2,1)S(1)}, u32[]{:S(2)}, u32[]{:S(2)}) collective-permute-start(bf16[24,2048]{1,0:T(8,128)(2,1)S(1)} %get-tuple-element.30), channel_id=1, source_target_pairs={{0,4},{1,5},{2,6},{3,7},{4,0},{5,1},{6,2},{7,3},{8,12},{9,13},{10,... | collective-permute-start | bytes 294920 | tf_op jit(solution)/shard_map/ppermute | solution.py:432
  49.4 1.5 %collective-permute-start.13 = (bf16[24,2048]{1,0:T(8,128)(2,1)S(1)}, bf16[24,2048]{1,0:T(8,128)(2,1)S(1)}, u32[]{:S(2)}, u32[]{:S(2)}) collective-permute-start(bf16[24,2048]{1,0:T(8,128)(2,1)S(1)} %get-tuple-element.29), channel_id=1, source_target_pairs={{0,1},{1,0},{2,3},{3,2},{4,5},{5,4},{6,7},{7,6},{8,9},{9,8},{10,11... | collective-permute-start | bytes 294920 | tf_op jit(solution)/shard_map/ppermute | solution.py:432
  50.9 0.5 collective-permute-start.12
  51.4 2.2 %collective-permute-done.14 = bf16[24,2048]{1,0:T(8,128)(2,1)S(1)} collective-permute-done((bf16[24,2048]{1,0:T(8,128)(2,1)S(1)}, bf16[24,2048]{1,0:T(8,128)(2,1)S(1)}, u32[]{:S(2)}, u32[]{:S(2)}) %collective-permute-start.14) | collective-permute-done | bytes 98336 | tf_op jit(solution)/shard_map/ppermute | solution.py:432
  53.6 0.5 collective-permute-done.13
  54.0 2.4 %collective-permute-done.12 = bf16[24,2048]{1,0:T(8,128)(2,1)S(1)} collective-permute-done((bf16[24,2048]{1,0:T(8,128)(2,1)S(1)}, bf16[24,2048]{1,0:T(8,128)(2,1)S(1)}, u32[]{:S(2)}, u32[]{:S(2)}) %collective-permute-start.12) | collective-permute-done | bytes 98336 | tf_op jit(solution)/shard_map/ppermute | solution.py:432
  56.4 0.7 %add_convert_fusion = bf16[24,2048]{1,0:T(8,128)(2,1)} fusion(bf16[24,2048]{1,0:T(8,128)(2,1)S(1)} %collective-permute-done.14, bf16[24,2048]{1,0:T(8,128)(2,1)S(1)} %collective-permute-done.13, f32[24,2048]{1,0:T(8,128)S(1)} %get-tuple-element.27, bf16[24,2048]{1,0:T(8,128)(2,1)S(1)} %collective-permute-done.12), kind=kLoop, calls=%fused_computation.6 | loop fusion | flops 344064 | bytes 589824 | tf_op jit(solution)/shard_map/convert_element_type | solution.py:499
  (14 shorter events, 0.1 us)
Async XLA Ops:
  0.6 25.5 %copy-start = (bf16[8,128,256]{2,1,0:T(8,128)(2,1)S(1)}, bf16[8,128,256]{2,1,0:T(8,128)(2,1)}, u32[]{:S(2)}) copy-start(bf16[8,128,256]{2,1,0:T(8,128)(2,1)} %refs_0_.2) | copy-start | bytes 1572868
  0.6 25.5 %copy-start.1 = (bf16[8,128,256]{2,1,0:T(8,128)(2,1)S(1)}, bf16[8,128,256]{2,1,0:T(8,128)(2,1)}, u32[]{:S(2)}) copy-start(bf16[8,128,256]{2,1,0:T(8,128)(2,1)} %refs_1_.1) | copy-start | bytes 1572868
  1.6 6.2 %collective-permute-start = (bf16[24,1024]{1,0:T(8,128)(2,1)S(1)}, bf16[24,1024]{1,0:T(8,128)(2,1)S(1)}, u32[]{:S(2)}, u32[]{:S(2)}) collective-permute-start(bf16[24,1024]{1,0:T(8,128)(2,1)S(1)} %get-tuple-element.37), channel_id=1, source_target_pairs={{0,4},{2,6},{4,0},{6,2},{8,12},{10,14},{12,8},{14,10},{16,20},{18,... | collective-permute-start | bytes 147464 | tf_op jit(solution)/shard_map/ppermute | solution.py:420
  4.6 23.6 %copy-start.3 = (s32[2,8]{1,0:T(2,128)S(1)}, s32[2,8]{1,0:T(2,128)}, u32[]{:S(2)}) copy-start(s32[2,8]{1,0:T(2,128)} %len_ref.5) | copy-start | bytes 196
  6.0 16.4 %collective-permute-start.6 = (bf16[2,8,128,128]{3,2,1,0:T(8,128)(2,1)S(1)}, bf16[2,8,128,128]{3,2,1,0:T(8,128)(2,1)S(1)}, u32[]{:S(2)}, u32[]{:S(2)}) collective-permute-start(bf16[2,8,128,128]{3,2,1,0:T(8,128)(2,1)S(1)} %pad_maximum_fusion.1), channel_id=1, source_target_pairs={{0,4},{2,6},{4,0},{6,2},{8,12},{10,14},{12,8},{14,10},{16,20},{18,... | collective-permute-start | bytes 1572872 | tf_op jit(solution)/shard_map/ppermute | solution.py:420
  7.9 14.5 %collective-permute-start.1 = (bf16[48,1024]{1,0:T(8,128)(2,1)S(1)}, bf16[48,1024]{1,0:T(8,128)(2,1)S(1)}, u32[]{:S(2)}, u32[]{:S(2)}) collective-permute-start(bf16[48,1024]{1,0:T(8,128)(2,1)S(1)} %pad_maximum_fusion.2._.refs_0_), channel_id=1, source_target_pairs={{0,24},{2,26},{4,28},{6,30},{8,16},{10,18},{12,20},{14,22},{16,8},... | collective-permute-start | bytes 294920 | tf_op jit(solution)/shard_map/ppermute | solution.py:420
  12.0 10.4 %collective-permute-start.2 = (bf16[48,1024]{1,0:T(8,128)(2,1)S(1)}, bf16[48,1024]{1,0:T(8,128)(2,1)S(1)}, u32[]{:S(2)}, u32[]{:S(2)}) collective-permute-start(bf16[48,1024]{1,0:T(8,128)(2,1)S(1)} %pad_maximum_fusion.2._.refs_0_), channel_id=1, source_target_pairs={{0,16},{2,18},{4,20},{6,22},{8,24},{10,26},{12,28},{14,30},{16,0},... | collective-permute-start | bytes 294920 | tf_op jit(solution)/shard_map/ppermute | solution.py:420
  12.0 10.4 %collective-permute-start.7 = (bf16[48,1024]{1,0:T(8,128)(2,1)S(1)}, bf16[48,1024]{1,0:T(8,128)(2,1)S(1)}, u32[]{:S(2)}, u32[]{:S(2)}) collective-permute-start(bf16[48,1024]{1,0:T(8,128)(2,1)S(1)} %pad_maximum_fusion.2._.refs_0_), channel_id=1, source_target_pairs={{0,8},{2,10},{4,12},{6,14},{8,0},{10,2},{12,4},{14,6},{16,24},{18,... | collective-permute-start | bytes 294920 | tf_op jit(solution)/shard_map/ppermute | solution.py:420
  12.6 0.9 %copy-start.2 = (bf16[24,4096]{1,0:T(8,128)(2,1)S(1)}, bf16[24,4096]{1,0:T(8,128)(2,1)}, u32[]{:S(2)}) copy-start(bf16[24,4096]{1,0:T(8,128)(2,1)} %hidden_ref.1) | copy-start | bytes 589828
  18.2 4.2 %collective-permute-start.3 = (f32[24,512]{1,0:T(8,128)S(1)}, f32[24,512]{1,0:T(8,128)S(1)}, u32[]{:S(2)}, u32[]{:S(2)}) collective-permute-start(f32[24,512]{1,0:T(8,128)S(1)} %get-tuple-element.19), channel_id=1, source_target_pairs={{0,1},{1,0},{2,3},{3,2},{4,5},{5,4},{6,7},{7,6},{8,9},{9,8},{10,11... | collective-permute-start | bytes 147464 | tf_op jit(solution)/shard_map/ppermute | solution.py:453
  22.3 3.8 %collective-permute-start.5 = (bf16[2,8,128,128]{3,2,1,0:T(8,128)(2,1)S(1)}, bf16[2,8,128,128]{3,2,1,0:T(8,128)(2,1)S(1)}, u32[]{:S(2)}, u32[]{:S(2)}) collective-permute-start(bf16[2,8,128,128]{3,2,1,0:T(8,128)(2,1)S(1)} %pad_maximum_fusion), channel_id=1, source_target_pairs={{0,2},{2,0},{4,6},{6,4},{8,10},{10,8},{12,14},{14,12},{16,18},{18,... | collective-permute-start | bytes 1572872 | tf_op jit(solution)/shard_map/ppermute | solution.py:420
  22.4 3.8 %collective-permute-start.8 = (bf16[2,8,128,128]{3,2,1,0:T(8,128)(2,1)S(1)}, bf16[2,8,128,128]{3,2,1,0:T(8,128)(2,1)S(1)}, u32[]{:S(2)}, u32[]{:S(2)}) collective-permute-start(bf16[2,8,128,128]{3,2,1,0:T(8,128)(2,1)S(1)} %shard_map.97.refs_3_), channel_id=1, source_target_pairs={{0,2},{2,0},{4,6},{6,4},{8,10},{10,8},{12,14},{14,12},{16,18},{18,... | collective-permute-start | bytes 1572872 | tf_op jit(solution)/shard_map/ppermute | solution.py:420
  24.5 3.7 %collective-permute-start.4 = (bf16[24,256]{1,0:T(8,128)(2,1)S(1)}, bf16[24,256]{1,0:T(8,128)(2,1)S(1)}, u32[]{:S(2)}, u32[]{:S(2)}) collective-permute-start(bf16[24,256]{1,0:T(8,128)(2,1)S(1)} %get-tuple-element.21), channel_id=1, source_target_pairs={{0,4},{2,6},{4,0},{6,2},{8,12},{10,14},{12,8},{14,10},{16,20},{18,... | collective-permute-start | bytes 36872 | tf_op jit(solution)/shard_map/ppermute | solution.py:420
  33.1 11.2 %collective-permute-start.9 = (bf16[400,128]{1,0:T(8,128)(2,1)S(1)}, bf16[400,128]{1,0:T(8,128)(2,1)S(1)}, u32[]{:S(2)}, u32[]{:S(2)}) collective-permute-start(bf16[400,128]{1,0:T(8,128)(2,1)S(1)} %get-tuple-element.24), channel_id=1, source_target_pairs={{0,24},{2,26},{4,28},{6,30},{8,16},{10,18},{12,20},{14,22},{16,8},... | collective-permute-start | bytes 307208 | tf_op jit(solution)/shard_map/ppermute | solution.py:420
  36.3 8.2 %collective-permute-start.10 = (bf16[400,128]{1,0:T(8,128)(2,1)S(1)}, bf16[400,128]{1,0:T(8,128)(2,1)S(1)}, u32[]{:S(2)}, u32[]{:S(2)}) collective-permute-start(bf16[400,128]{1,0:T(8,128)(2,1)S(1)} %get-tuple-element.25), channel_id=1, source_target_pairs={{0,16},{2,18},{4,20},{6,22},{8,24},{10,26},{12,28},{14,30},{16,0},... | collective-permute-start | bytes 307208 | tf_op jit(solution)/shard_map/ppermute | solution.py:420
  39.7 5.9 %collective-permute-start.11 = (bf16[400,128]{1,0:T(8,128)(2,1)S(1)}, bf16[400,128]{1,0:T(8,128)(2,1)S(1)}, u32[]{:S(2)}, u32[]{:S(2)}) collective-permute-start(bf16[400,128]{1,0:T(8,128)(2,1)S(1)} %shard_map.100), channel_id=1, source_target_pairs={{0,8},{2,10},{4,12},{6,14},{8,0},{10,2},{12,4},{14,6},{16,24},{18,... | collective-permute-start | bytes 307208 | tf_op jit(solution)/shard_map/ppermute | solution.py:420
  47.8 5.7 %collective-permute-start.14 = (bf16[24,2048]{1,0:T(8,128)(2,1)S(1)}, bf16[24,2048]{1,0:T(8,128)(2,1)S(1)}, u32[]{:S(2)}, u32[]{:S(2)}) collective-permute-start(bf16[24,2048]{1,0:T(8,128)(2,1)S(1)} %get-tuple-element.30), channel_id=1, source_target_pairs={{0,4},{1,5},{2,6},{3,7},{4,0},{5,1},{6,2},{7,3},{8,12},{9,13},{10,... | collective-permute-start | bytes 294920 | tf_op jit(solution)/shard_map/ppermute | solution.py:432
  49.4 4.6 %collective-permute-start.13 = (bf16[24,2048]{1,0:T(8,128)(2,1)S(1)}, bf16[24,2048]{1,0:T(8,128)(2,1)S(1)}, u32[]{:S(2)}, u32[]{:S(2)}) collective-permute-start(bf16[24,2048]{1,0:T(8,128)(2,1)S(1)} %get-tuple-element.29), channel_id=1, source_target_pairs={{0,1},{1,0},{2,3},{3,2},{4,5},{5,4},{6,7},{7,6},{8,9},{9,8},{10,11... | collective-permute-start | bytes 294920 | tf_op jit(solution)/shard_map/ppermute | solution.py:432
  50.9 5.5 %collective-permute-start.12 = (bf16[24,2048]{1,0:T(8,128)(2,1)S(1)}, bf16[24,2048]{1,0:T(8,128)(2,1)S(1)}, u32[]{:S(2)}, u32[]{:S(2)}) collective-permute-start(bf16[24,2048]{1,0:T(8,128)(2,1)S(1)} %get-tuple-element.28), channel_id=1, source_target_pairs={{0,5},{1,4},{2,7},{3,6},{4,1},{5,0},{6,3},{7,2},{8,13},{9,12},{10,... | collective-permute-start | bytes 294920 | tf_op jit(solution)/shard_map/ppermute | solution.py:432

commit v4 on v3

--- a/solution.py
+++ b/solution.py
@@ -453,8 +453,9 @@
         lax.ppermute(projected[rank], "tp", [(i, i ^ rank) for i in range(ranks)])
         for rank in range(1, ranks)
     ]
+    late = (projected[0][0, 0] * 0).astype(jnp.int32)
     lengths = jnp.sum(
-        jnp.where(jnp.arange(GROUPS)[:, None] == group, suffix_lengths, 0), axis=0
+        jnp.where(jnp.arange(GROUPS)[:, None] == group, suffix_lengths + late, 0), axis=0
     )
     ends = jnp.sum(
         jnp.where(jnp.arange(REQS)[None, :] <= jnp.arange(REQS)[:, None], lengths[None, :], 0),
@@ -492,8 +493,8 @@
 
     products = project(place, returned, weight, rows, splits, ranks, heads)
     hidden = products[0]
-    for rank in range(ranks - 1, -1, -1):
-        for side in range(splits - 1, -1, -1):
+    for rank in range(ranks):
+        for side in range(splits):
             if rank or side:
                 hidden = hidden + quad(products[rank * splits + side], rank, side).astype(F32)
     return (hidden.astype(BF16), new_pages)

time: 57.3 us -> 55.7 us (0.972)
  Pallas kernels: 21.2 us -> 19.6 us
  waiting for transfers between devices: 9.37 us -> 8.34 us
  between operations: 0.83 us -> 1.54 us
  other arithmetic: 2 us -> 1.32 us
    pallas_call x3, Pallas kernels: 11.7 us -> 10.1 us  [attend(): pl.pallas_call(body, in_specs=[SMEM, SMEM, SMEM] + [HBM] * len(fetched) +...]
    ppermute x1, waiting for transfers between devices: 2.44 us -> 0.98 us  [local(): lax.ppermute(projected[rank], 'tp', [(i, i ^ rank) for i in range(ranks)])]
    ppermute x11, waiting for transfers between devices: 1.9 us -> 3.25 us  [across(): return lax.ppermute(array, 'seq', [(i, i ^ step) for i in range(seq_count)])]
    ppermute x3, waiting for transfers between devices: 5.03 us -> 4.1 us  [quad(): return lax.ppermute(array, ('seq', 'tp'), route)]
    reduce_sum x1, other arithmetic: 0.76 us -> 0.09 us  [local(): jnp.sum(jnp.where(jnp.arange(GROUPS)[:, None] == group, suffix_lengths +...]
  transfers between devices with their start and end apart: 15 -> 15, of which waited for: 7 -> 7; matrix products, arithmetic and copies ran while one was open for 6% -> 6% of each run, Pallas kernels for 24% -> 23%
where the time goes in v4:
time: 55.7 us; the launch traced here: 55.5 us
  starting transfers between devices  20.4 us (37%)
  Pallas kernels  19.6 us (35%)
  waiting for transfers between devices  8.34 us (15%)
  local copies, waits for them, and re-layouts  4.36 us (8%)
  between operations  1.54 us (3%)
  other arithmetic  1.32 us (2%)
    ppermute x11, starting transfers between devices, across(): return lax.ppermute(array, 'seq', [(i, i ^ step) for i in range(seq_count)])  15.1 us
    pallas_call x3, Pallas kernels, attend(): pl.pallas_call(body, in_specs=[SMEM, SMEM, SMEM] + [HBM] * len(fetched) +...  10.1 us
    pallas_call x1, Pallas kernels, project_kv(): pl.pallas_call(body, in_specs=[SMEM, VMEM, HBM, ANY], out_specs=[VMEM] *...  4.61 us
    ppermute x3, waiting for transfers between devices, quad(): return lax.ppermute(array, ('seq', 'tp'), route)  4.1 us
    ppermute x3, starting transfers between devices, quad(): return lax.ppermute(array, ('seq', 'tp'), route)  3.55 us
    ppermute x11, waiting for transfers between devices, across(): return lax.ppermute(array, 'seq', [(i, i ^ step) for i in range(seq_count)])  3.25 us
    pallas_call x1, Pallas kernels, project(): pl.pallas_call(body, in_specs=[SMEM] + [VMEM] * (len(partials) + 1), out_...  2.3 us
    ppermute x1, starting transfers between devices, local(): lax.ppermute(projected[rank], 'tp', [(i, i ^ rank) for i in range(ranks)])  1.7 us
  transfers between devices with their start and end apart: 15, of which 7 were waited for; matrix products, arithmetic and copies ran while one was open for 6% of the time, Pallas kernels for 23%

profile of v4, /device:TPU:0, one launch (start us, length us, event | category | flops | bytes accessed | tf_op | source)
XLA Modules:
  0.0 55.5 jit_solution(80185422970961291)
XLA Ops:
  0.6 0.0 copy-start
  0.6 0.0 copy-start.1
  0.7 0.9 %constant_dynamic-slice_fusion.1 = (bf16[24,1024]{1,0:T(8,128)(2,1)S(1)}, bf16[24,1024]{1,0:T(8,128)(2,1)S(1)}) fusion(bf16[24,2048]{1,0:T(8,128)(2,1)} %param.10, s32[]{:T(128)S(6)} %select_n.48, s32[]{:T(128)S(6)} %select_n.49), kind=kLoop, calls=%fused_computation.17 | loop fusion | bytes 196616 | tf_op jit(solution)/shard_map/dynamic_slice | solution.py:435
  1.6 3.0 %collective-permute-start = (bf16[24,1024]{1,0:T(8,128)(2,1)S(1)}, bf16[24,1024]{1,0:T(8,128)(2,1)S(1)}, u32[]{:S(2)}, u32[]{:S(2)}) collective-permute-start(bf16[24,1024]{1,0:T(8,128)(2,1)S(1)} %get-tuple-element.37), channel_id=1, source_target_pairs={{0,4},{2,6},{4,0},{6,2},{8,12},{10,14},{12,8},{14,10},{16,20},{18,... | collective-permute-start | bytes 147464 | tf_op jit(solution)/shard_map/ppermute | solution.py:420
  4.6 1.3 %dynamic-slice_bitcast_fusion = (bf16[1,8,128,128]{3,2,1,0:T(8,128)(2,1)S(1)}, bf16[1,8,128,128]{3,2,1,0:T(8,128)(2,1)S(1)}, bf16[1,8,128,128]{3,2,1,0:T(8,128)(2,1)S(1)}, bf16[1,8,128,128]{3,2,1,0:T(8,128)(2,1)S(1)}) fusion(bf16[8,128,256]{2,1,0:T(8,128)(2,1)} %refs_1_.1, s32[]{:T(128)S(6)} %select_n.54, s32[]{:T(128)S(6)} %select_n.53, ...), kind=kLoop, calls=%fused_computation.2 | loop fusion | bytes 2097160 | tf_op jit(solution)/shard_map/stack | solution.py:443
  5.9 0.1 pad_maximum_fusion.1
  6.0 0.1 collective-permute-start.6
  6.1 0.1 pad_maximum_fusion
  6.2 0.7 %concatenate.12.place_ref = s32[133]{0:T(256)S(1)} concatenate(s32[1]{0:T(128)} %bitcast, s32[1]{0:T(128)} %bitcast.1, s32[1]{0:T(128)} %bitcast.2, s32[1]{0:T(128)} %bitcast.3, s32[1]{0:T(128)} %bitcast.4, s32[128]{0:T(128)} %param.13), dimensions={0} | concatenate | bytes 1064 | tf_op jit(solution)/shard_map/concatenate | solution.py:416
  6.9 4.1 %collective-permute-start.1 = (bf16[48,1024]{1,0:T(8,128)(2,1)S(1)}, bf16[48,1024]{1,0:T(8,128)(2,1)S(1)}, u32[]{:S(2)}, u32[]{:S(2)}) collective-permute-start(bf16[48,1024]{1,0:T(8,128)(2,1)S(1)} %pad_maximum_fusion.2._.refs_0_), channel_id=1, source_target_pairs={{0,24},{2,26},{4,28},{6,30},{8,16},{10,18},{12,20},{14,22},{16,8},... | collective-permute-start | bytes 294920 | tf_op jit(solution)/shard_map/ppermute | solution.py:420
  11.1 0.0 collective-permute-start.2
  11.1 0.6 %collective-permute-start.7 = (bf16[48,1024]{1,0:T(8,128)(2,1)S(1)}, bf16[48,1024]{1,0:T(8,128)(2,1)S(1)}, u32[]{:S(2)}, u32[]{:S(2)}) collective-permute-start(bf16[48,1024]{1,0:T(8,128)(2,1)S(1)} %pad_maximum_fusion.2._.refs_0_), channel_id=1, source_target_pairs={{0,8},{2,10},{4,12},{6,14},{8,0},{10,2},{12,4},{14,6},{16,24},{18,... | collective-permute-start | bytes 294920 | tf_op jit(solution)/shard_map/ppermute | solution.py:420
  11.7 0.9 %copy-done.2 = bf16[24,4096]{1,0:T(8,128)(2,1)S(1)} copy-done((bf16[24,4096]{1,0:T(8,128)(2,1)S(1)}, bf16[24,4096]{1,0:T(8,128)(2,1)}, u32[]{:S(2)}) %copy-start.2) | copy-done | bytes 196632
  12.6 4.6 %shard_map.95 = (f32[24,512]{1,0:T(8,128)S(1)}, f32[24,512]{1,0:T(8,128)S(1)}, s32[34]{0:T(128)S(1)}) custom-call(s32[133]{0:T(256)S(1)} %concatenate.12.place_ref, bf16[24,4096]{1,0:T(8,128)(2,1)S(1)} %copy-done.2, bf16[4096,1024]{1,0:T(8,128)(2,1)} %weight_ref.1, bf16[48,1024]{1,0:T(8,128)(2,1)S(1)} %pad_maximum_fusion.2._.refs_0_), custom_call_target="tpu_custom_call" | custom-call | flops 1 | bytes 1 | tf_op jit(solution)/shard_map/pallas_call | solution.py:93
  17.3 1.7 %collective-permute-start.3 = (f32[24,512]{1,0:T(8,128)S(1)}, f32[24,512]{1,0:T(8,128)S(1)}, u32[]{:S(2)}, u32[]{:S(2)}) collective-permute-start(f32[24,512]{1,0:T(8,128)S(1)} %get-tuple-element.19), channel_id=1, source_target_pairs={{0,1},{1,0},{2,3},{3,2},{4,5},{5,4},{6,7},{7,6},{8,9},{9,8},{10,11... | collective-permute-start | bytes 147464 | tf_op jit(solution)/shard_map/ppermute | solution.py:453
  19.0 0.5 slice.3
  20.1 0.1 select_reduce_fusion.2
  20.2 0.1 select_reduce_fusion.1
  20.3 0.1 select_reduce_fusion
  20.4 1.0 %collective-permute-done.3.refs_1_ = f32[24,512]{1,0:T(8,128)S(1)} collective-permute-done((f32[24,512]{1,0:T(8,128)S(1)}, f32[24,512]{1,0:T(8,128)S(1)}, u32[]{:S(2)}, u32[]{:S(2)}) %collective-permute-start.3) | collective-permute-done | bytes 49184 | tf_op jit(solution)/shard_map/ppermute | solution.py:453
  21.4 0.0 collective-permute-done.1.refs_4_.refs_1_
  21.4 0.0 collective-permute-done.2.refs_3_.refs_2_
  21.4 0.0 collective-permute-done.7.refs_2_.refs_0_
  21.4 0.0 collective-permute-done.6.refs_0_
  21.5 0.6 %collective-permute-start.8 = (bf16[2,8,128,128]{3,2,1,0:T(8,128)(2,1)S(1)}, bf16[2,8,128,128]{3,2,1,0:T(8,128)(2,1)S(1)}, u32[]{:S(2)}, u32[]{:S(2)}) collective-permute-start(bf16[2,8,128,128]{3,2,1,0:T(8,128)(2,1)S(1)} %shard_map.97.refs_3_), channel_id=1, source_target_pairs={{0,2},{2,0},{4,6},{6,4},{8,10},{10,8},{12,14},{14,12},{16,18},{18,... | collective-permute-start | bytes 1572872 | tf_op jit(solution)/shard_map/ppermute | solution.py:420
  22.0 0.1 fusion
  22.2 0.1 pad_maximum_fusion.3
  22.2 1.3 %shard_map.96 = (bf16[24,512]{1,0:T(8,128)(2,1)}, bf16[24,256]{1,0:T(8,128)(2,1)S(1)}, bf16[24,256]{1,0:T(8,128)(2,1)S(1)}) custom-call(s32[133]{0:T(256)S(1)} %concatenate.12.place_ref, f32[24,512]{1,0:T(8,128)S(1)} %get-tuple-element.18.refs_0_, f32[24,512]{1,0:T(8,128)S(1)} %collective-permute-done.3.refs_1_, f32[24,128]{1,0:T(8,128)S(1)} %get-tuple-element.41.refs_2_, ...), custom_call_target="tpu_custom_call" | custom-call | flops 1 | bytes 1 | tf_op jit(solution)/shard_map/pallas_call | solution.py:132
  23.6 1.7 %collective-permute-start.4 = (bf16[24,256]{1,0:T(8,128)(2,1)S(1)}, bf16[24,256]{1,0:T(8,128)(2,1)S(1)}, u32[]{:S(2)}, u32[]{:S(2)}) collective-permute-start(bf16[24,256]{1,0:T(8,128)(2,1)S(1)} %get-tuple-element.21), channel_id=1, source_target_pairs={{0,4},{2,6},{4,0},{6,2},{8,12},{10,14},{12,8},{14,10},{16,20},{18,... | collective-permute-start | bytes 36872 | tf_op jit(solution)/shard_map/ppermute | solution.py:420
  25.3 0.0 collective-permute-done.5.refs_2_
  25.3 1.2 %shard_map.98 = (bf16[4096,128]{1,0:T(8,128)(2,1)S(1)}, bf16[4096,128]{1,0:T(8,128)(2,1)S(1)}) custom-call(s32[34]{0:T(128)S(1)} %get-tuple-element.17.list_ref, s32[133]{0:T(256)S(1)} %concatenate.12.place_ref, bf16[8,128,256]{2,1,0:T(8,128)(2,1)S(1)} %copy-done, bf16[8,128,256]{2,1,0:T(8,128)(2,1)S(1)} %copy-done.1, ...), custom_call_target="tpu_custom_call" | custom-call | flops 1 | bytes 1 | tf_op jit(solution)/shard_map/pallas_call | solution.py:184
  26.5 0.8 %collective-permute-done.4.refs_4_.refs_2_ = bf16[24,256]{1,0:T(8,128)(2,1)S(1)} collective-permute-done((bf16[24,256]{1,0:T(8,128)(2,1)S(1)}, bf16[24,256]{1,0:T(8,128)(2,1)S(1)}, u32[]{:S(2)}, u32[]{:S(2)}) %collective-permute-start.4) | collective-permute-done | bytes 12320 | tf_op jit(solution)/shard_map/ppermute | solution.py:420
  27.3 4.3 %shard_map.99 = (bf16[400,128]{1,0:T(8,128)(2,1)S(1)}, bf16[400,128]{1,0:T(8,128)(2,1)S(1)}, bf16[1024,4096]{1,0:T(8,128)(2,1)S(1)}) custom-call(s32[34]{0:T(128)S(1)} %get-tuple-element.17.list_ref, s32[2,8]{1,0:T(2,128)S(1)} %copy-done.3, s32[133]{0:T(256)S(1)} %concatenate.12.place_ref, bf16[2048,4096]{1,0:T(8,128)(2,1)} %refs_0_.3, ...), custom_call_target="tpu_custom_call" | custom-call | flops 1610612736 | bytes 1572864 | tf_op jit(solution)/shard_map/pallas_call | solution.py:310
  31.6 3.8 %collective-permute-start.9 = (bf16[400,128]{1,0:T(8,128)(2,1)S(1)}, bf16[400,128]{1,0:T(8,128)(2,1)S(1)}, u32[]{:S(2)}, u32[]{:S(2)}) collective-permute-start(bf16[400,128]{1,0:T(8,128)(2,1)S(1)} %get-tuple-element.24), channel_id=1, source_target_pairs={{0,24},{2,26},{4,28},{6,30},{8,16},{10,18},{12,20},{14,22},{16,8},... | collective-permute-start | bytes 307208 | tf_op jit(solution)/shard_map/ppermute | solution.py:420
  35.4 2.9 %shard_map.100 = bf16[400,128]{1,0:T(8,128)(2,1)S(1)} custom-call(s32[34]{0:T(128)S(1)} %get-tuple-element.17.list_ref, s32[2,8]{1,0:T(2,128)S(1)} %copy-done.3, s32[133]{0:T(256)S(1)} %concatenate.12.place_ref, bf16[48,1024]{1,0:T(8,128)(2,1)S(1)} %collective-permute-done.7.refs_2_.refs_0_, bf16[24,256]{1,0:T(8,128)(2,1)S(1)} %get-tuple-element.20.refs_3_.refs_1_, ...), custom_call_target="tpu_custom_call" | custom-call | flops 805306368 | bytes 1572864 | tf_op jit(solution)/shard_map/pallas_call | solution.py:310
  38.3 1.1 %collective-permute-start.11 = (bf16[400,128]{1,0:T(8,128)(2,1)S(1)}, bf16[400,128]{1,0:T(8,128)(2,1)S(1)}, u32[]{:S(2)}, u32[]{:S(2)}) collective-permute-start(bf16[400,128]{1,0:T(8,128)(2,1)S(1)} %shard_map.100), channel_id=1, source_target_pairs={{0,8},{2,10},{4,12},{6,14},{8,0},{10,2},{12,4},{14,6},{16,24},{18,... | collective-permute-start | bytes 307208 | tf_op jit(solution)/shard_map/ppermute | solution.py:420
  39.4 2.9 %shard_map.101.refs_3_ = bf16[400,128]{1,0:T(8,128)(2,1)S(1)} custom-call(s32[34]{0:T(128)S(1)} %get-tuple-element.17.list_ref, s32[2,8]{1,0:T(2,128)S(1)} %copy-done.3, s32[133]{0:T(256)S(1)} %concatenate.12.place_ref, bf16[48,1024]{1,0:T(8,128)(2,1)S(1)} %pad_maximum_fusion.2._.refs_0_, bf16[24,256]{1,0:T(8,128)(2,1)S(1)} %get-tuple-element.20.refs_3_.refs_1_, ...), custom_call_target="tpu_custom_call" | custom-call | flops 805306368 | bytes 1572864 | tf_op jit(solution)/shard_map/pallas_call | solution.py:310
  42.3 0.0 collective-permute-done.9.refs_0_
  42.4 1.2 %collective-permute-done.10.refs_1_ = bf16[400,128]{1,0:T(8,128)(2,1)S(1)} collective-permute-done((bf16[400,128]{1,0:T(8,128)(2,1)S(1)}, bf16[400,128]{1,0:T(8,128)(2,1)S(1)}, u32[]{:S(2)}, u32[]{:S(2)}) %collective-permute-start.10) | collective-permute-done | bytes 102432 | tf_op jit(solution)/shard_map/ppermute | solution.py:420
  43.6 1.3 %collective-permute-done.11.refs_2_ = bf16[400,128]{1,0:T(8,128)(2,1)S(1)} collective-permute-done((bf16[400,128]{1,0:T(8,128)(2,1)S(1)}, bf16[400,128]{1,0:T(8,128)(2,1)S(1)}, u32[]{:S(2)}, u32[]{:S(2)}) %collective-permute-start.11) | collective-permute-done | bytes 102432 | tf_op jit(solution)/shard_map/ppermute | solution.py:420
  44.8 2.3 %shard_map.102 = (f32[24,2048]{1,0:T(8,128)S(1)}, bf16[24,2048]{1,0:T(8,128)(2,1)S(1)}, bf16[24,2048]{1,0:T(8,128)(2,1)S(1)}, bf16[24,2048]{1,0:T(8,128)(2,1)S(1)}) custom-call(s32[133]{0:T(256)S(1)} %concatenate.12.place_ref, bf16[400,128]{1,0:T(8,128)(2,1)S(1)} %collective-permute-done.9.refs_0_, bf16[400,128]{1,0:T(8,128)(2,1)S(1)} %collective-permute-done.10.refs_1_, ...), custom_call_target="tpu_custom_call" | custom-call | flops 402653184 | bytes 4194304 | tf_op jit(solution)/shard_map/pallas_call | solution.py:375
  47.1 2.5 %collective-permute-start.14 = (bf16[24,2048]{1,0:T(8,128)(2,1)S(1)}, bf16[24,2048]{1,0:T(8,128)(2,1)S(1)}, u32[]{:S(2)}, u32[]{:S(2)}) collective-permute-start(bf16[24,2048]{1,0:T(8,128)(2,1)S(1)} %get-tuple-element.30), channel_id=1, source_target_pairs={{0,5},{1,4},{2,7},{3,6},{4,1},{5,0},{6,3},{7,2},{8,13},{9,12},{10,... | collective-permute-start | bytes 294920 | tf_op jit(solution)/shard_map/ppermute | solution.py:432
  49.7 0.5 collective-permute-start.13
  50.2 0.5 collective-permute-start.12
  50.7 2.8 %collective-permute-done.14 = bf16[24,2048]{1,0:T(8,128)(2,1)S(1)} collective-permute-done((bf16[24,2048]{1,0:T(8,128)(2,1)S(1)}, bf16[24,2048]{1,0:T(8,128)(2,1)S(1)}, u32[]{:S(2)}, u32[]{:S(2)}) %collective-permute-start.14) | collective-permute-done | bytes 98336 | tf_op jit(solution)/shard_map/ppermute | solution.py:432
  53.5 1.1 %collective-permute-done.13 = bf16[24,2048]{1,0:T(8,128)(2,1)S(1)} collective-permute-done((bf16[24,2048]{1,0:T(8,128)(2,1)S(1)}, bf16[24,2048]{1,0:T(8,128)(2,1)S(1)}, u32[]{:S(2)}, u32[]{:S(2)}) %collective-permute-start.13) | collective-permute-done | bytes 98336 | tf_op jit(solution)/shard_map/ppermute | solution.py:432
  54.6 0.2 collective-permute-done.12
  54.8 0.7 %add_convert_fusion = bf16[24,2048]{1,0:T(8,128)(2,1)} fusion(bf16[24,2048]{1,0:T(8,128)(2,1)S(1)} %collective-permute-done.14, bf16[24,2048]{1,0:T(8,128)(2,1)S(1)} %collective-permute-done.13, f32[24,2048]{1,0:T(8,128)S(1)} %get-tuple-element.27, bf16[24,2048]{1,0:T(8,128)(2,1)S(1)} %collective-permute-done.12), kind=kLoop, calls=%fused_computation.6 | loop fusion | flops 344064 | bytes 589824 | tf_op jit(solution)/shard_map/convert_element_type | solution.py:500
  (15 shorter events, 0.1 us)
Async XLA Ops:
  0.6 24.6 %copy-start = (bf16[8,128,256]{2,1,0:T(8,128)(2,1)S(1)}, bf16[8,128,256]{2,1,0:T(8,128)(2,1)}, u32[]{:S(2)}) copy-start(bf16[8,128,256]{2,1,0:T(8,128)(2,1)} %refs_0_.2) | copy-start | bytes 1572868
  0.6 24.6 %copy-start.1 = (bf16[8,128,256]{2,1,0:T(8,128)(2,1)S(1)}, bf16[8,128,256]{2,1,0:T(8,128)(2,1)}, u32[]{:S(2)}) copy-start(bf16[8,128,256]{2,1,0:T(8,128)(2,1)} %refs_1_.1) | copy-start | bytes 1572868
  0.7 19.5 %copy-start.3 = (s32[2,8]{1,0:T(2,128)S(1)}, s32[2,8]{1,0:T(2,128)}, u32[]{:S(2)}) copy-start(s32[2,8]{1,0:T(2,128)} %len_ref.5) | copy-start | bytes 196
  1.6 5.3 %collective-permute-start = (bf16[24,1024]{1,0:T(8,128)(2,1)S(1)}, bf16[24,1024]{1,0:T(8,128)(2,1)S(1)}, u32[]{:S(2)}, u32[]{:S(2)}) collective-permute-start(bf16[24,1024]{1,0:T(8,128)(2,1)S(1)} %get-tuple-element.37), channel_id=1, source_target_pairs={{0,4},{2,6},{4,0},{6,2},{8,12},{10,14},{12,8},{14,10},{16,20},{18,... | collective-permute-start | bytes 147464 | tf_op jit(solution)/shard_map/ppermute | solution.py:420
  6.0 15.5 %collective-permute-start.6 = (bf16[2,8,128,128]{3,2,1,0:T(8,128)(2,1)S(1)}, bf16[2,8,128,128]{3,2,1,0:T(8,128)(2,1)S(1)}, u32[]{:S(2)}, u32[]{:S(2)}) collective-permute-start(bf16[2,8,128,128]{3,2,1,0:T(8,128)(2,1)S(1)} %pad_maximum_fusion.1), channel_id=1, source_target_pairs={{0,4},{2,6},{4,0},{6,2},{8,12},{10,14},{12,8},{14,10},{16,20},{18,... | collective-permute-start | bytes 1572872 | tf_op jit(solution)/shard_map/ppermute | solution.py:420
  6.9 14.5 %collective-permute-start.1 = (bf16[48,1024]{1,0:T(8,128)(2,1)S(1)}, bf16[48,1024]{1,0:T(8,128)(2,1)S(1)}, u32[]{:S(2)}, u32[]{:S(2)}) collective-permute-start(bf16[48,1024]{1,0:T(8,128)(2,1)S(1)} %pad_maximum_fusion.2._.refs_0_), channel_id=1, source_target_pairs={{0,24},{2,26},{4,28},{6,30},{8,16},{10,18},{12,20},{14,22},{16,8},... | collective-permute-start | bytes 294920 | tf_op jit(solution)/shard_map/ppermute | solution.py:420
  11.1 10.4 %collective-permute-start.2 = (bf16[48,1024]{1,0:T(8,128)(2,1)S(1)}, bf16[48,1024]{1,0:T(8,128)(2,1)S(1)}, u32[]{:S(2)}, u32[]{:S(2)}) collective-permute-start(bf16[48,1024]{1,0:T(8,128)(2,1)S(1)} %pad_maximum_fusion.2._.refs_0_), channel_id=1, source_target_pairs={{0,16},{2,18},{4,20},{6,22},{8,24},{10,26},{12,28},{14,30},{16,0},... | collective-permute-start | bytes 294920 | tf_op jit(solution)/shard_map/ppermute | solution.py:420
  11.1 10.4 %collective-permute-start.7 = (bf16[48,1024]{1,0:T(8,128)(2,1)S(1)}, bf16[48,1024]{1,0:T(8,128)(2,1)S(1)}, u32[]{:S(2)}, u32[]{:S(2)}) collective-permute-start(bf16[48,1024]{1,0:T(8,128)(2,1)S(1)} %pad_maximum_fusion.2._.refs_0_), channel_id=1, source_target_pairs={{0,8},{2,10},{4,12},{6,14},{8,0},{10,2},{12,4},{14,6},{16,24},{18,... | collective-permute-start | bytes 294920 | tf_op jit(solution)/shard_map/ppermute | solution.py:420
  11.7 0.9 %copy-start.2 = (bf16[24,4096]{1,0:T(8,128)(2,1)S(1)}, bf16[24,4096]{1,0:T(8,128)(2,1)}, u32[]{:S(2)}) copy-start(bf16[24,4096]{1,0:T(8,128)(2,1)} %hidden_ref.1) | copy-start | bytes 589828
  17.3 4.2 %collective-permute-start.3 = (f32[24,512]{1,0:T(8,128)S(1)}, f32[24,512]{1,0:T(8,128)S(1)}, u32[]{:S(2)}, u32[]{:S(2)}) collective-permute-start(f32[24,512]{1,0:T(8,128)S(1)} %get-tuple-element.19), channel_id=1, source_target_pairs={{0,1},{1,0},{2,3},{3,2},{4,5},{5,4},{6,7},{7,6},{8,9},{9,8},{10,11... | collective-permute-start | bytes 147464 | tf_op jit(solution)/shard_map/ppermute | solution.py:453
  21.4 3.8 %collective-permute-start.5 = (bf16[2,8,128,128]{3,2,1,0:T(8,128)(2,1)S(1)}, bf16[2,8,128,128]{3,2,1,0:T(8,128)(2,1)S(1)}, u32[]{:S(2)}, u32[]{:S(2)}) collective-permute-start(bf16[2,8,128,128]{3,2,1,0:T(8,128)(2,1)S(1)} %pad_maximum_fusion), channel_id=1, source_target_pairs={{0,2},{2,0},{4,6},{6,4},{8,10},{10,8},{12,14},{14,12},{16,18},{18,... | collective-permute-start | bytes 1572872 | tf_op jit(solution)/shard_map/ppermute | solution.py:420
  21.5 3.8 %collective-permute-start.8 = (bf16[2,8,128,128]{3,2,1,0:T(8,128)(2,1)S(1)}, bf16[2,8,128,128]{3,2,1,0:T(8,128)(2,1)S(1)}, u32[]{:S(2)}, u32[]{:S(2)}) collective-permute-start(bf16[2,8,128,128]{3,2,1,0:T(8,128)(2,1)S(1)} %shard_map.97.refs_3_), channel_id=1, source_target_pairs={{0,2},{2,0},{4,6},{6,4},{8,10},{10,8},{12,14},{14,12},{16,18},{18,... | collective-permute-start | bytes 1572872 | tf_op jit(solution)/shard_map/ppermute | solution.py:420
  23.6 3.7 %collective-permute-start.4 = (bf16[24,256]{1,0:T(8,128)(2,1)S(1)}, bf16[24,256]{1,0:T(8,128)(2,1)S(1)}, u32[]{:S(2)}, u32[]{:S(2)}) collective-permute-start(bf16[24,256]{1,0:T(8,128)(2,1)S(1)} %get-tuple-element.21), channel_id=1, source_target_pairs={{0,4},{2,6},{4,0},{6,2},{8,12},{10,14},{12,8},{14,10},{16,20},{18,... | collective-permute-start | bytes 36872 | tf_op jit(solution)/shard_map/ppermute | solution.py:420
  31.6 10.8 %collective-permute-start.9 = (bf16[400,128]{1,0:T(8,128)(2,1)S(1)}, bf16[400,128]{1,0:T(8,128)(2,1)S(1)}, u32[]{:S(2)}, u32[]{:S(2)}) collective-permute-start(bf16[400,128]{1,0:T(8,128)(2,1)S(1)} %get-tuple-element.24), channel_id=1, source_target_pairs={{0,24},{2,26},{4,28},{6,30},{8,16},{10,18},{12,20},{14,22},{16,8},... | collective-permute-start | bytes 307208 | tf_op jit(solution)/shard_map/ppermute | solution.py:420
  35.4 8.2 %collective-permute-start.10 = (bf16[400,128]{1,0:T(8,128)(2,1)S(1)}, bf16[400,128]{1,0:T(8,128)(2,1)S(1)}, u32[]{:S(2)}, u32[]{:S(2)}) collective-permute-start(bf16[400,128]{1,0:T(8,128)(2,1)S(1)} %get-tuple-element.25), channel_id=1, source_target_pairs={{0,16},{2,18},{4,20},{6,22},{8,24},{10,26},{12,28},{14,30},{16,0},... | collective-permute-start | bytes 307208 | tf_op jit(solution)/shard_map/ppermute | solution.py:420
  38.3 6.5 %collective-permute-start.11 = (bf16[400,128]{1,0:T(8,128)(2,1)S(1)}, bf16[400,128]{1,0:T(8,128)(2,1)S(1)}, u32[]{:S(2)}, u32[]{:S(2)}) collective-permute-start(bf16[400,128]{1,0:T(8,128)(2,1)S(1)} %shard_map.100), channel_id=1, source_target_pairs={{0,8},{2,10},{4,12},{6,14},{8,0},{10,2},{12,4},{14,6},{16,24},{18,... | collective-permute-start | bytes 307208 | tf_op jit(solution)/shard_map/ppermute | solution.py:420
  47.1 6.3 %collective-permute-start.14 = (bf16[24,2048]{1,0:T(8,128)(2,1)S(1)}, bf16[24,2048]{1,0:T(8,128)(2,1)S(1)}, u32[]{:S(2)}, u32[]{:S(2)}) collective-permute-start(bf16[24,2048]{1,0:T(8,128)(2,1)S(1)} %get-tuple-element.30), channel_id=1, source_target_pairs={{0,5},{1,4},{2,7},{3,6},{4,1},{5,0},{6,3},{7,2},{8,13},{9,12},{10,... | collective-permute-start | bytes 294920 | tf_op jit(solution)/shard_map/ppermute | solution.py:432
  49.7 4.9 %collective-permute-start.13 = (bf16[24,2048]{1,0:T(8,128)(2,1)S(1)}, bf16[24,2048]{1,0:T(8,128)(2,1)S(1)}, u32[]{:S(2)}, u32[]{:S(2)}) collective-permute-start(bf16[24,2048]{1,0:T(8,128)(2,1)S(1)} %get-tuple-element.29), channel_id=1, source_target_pairs={{0,1},{1,0},{2,3},{3,2},{4,5},{5,4},{6,7},{7,6},{8,9},{9,8},{10,11... | collective-permute-start | bytes 294920 | tf_op jit(solution)/shard_map/ppermute | solution.py:432
  50.2 4.6 %collective-permute-start.12 = (bf16[24,2048]{1,0:T(8,128)(2,1)S(1)}, bf16[24,2048]{1,0:T(8,128)(2,1)S(1)}, u32[]{:S(2)}, u32[]{:S(2)}) collective-permute-start(bf16[24,2048]{1,0:T(8,128)(2,1)S(1)} %get-tuple-element.28), channel_id=1, source_target_pairs={{0,4},{1,5},{2,6},{3,7},{4,0},{5,1},{6,2},{7,3},{8,12},{9,13},{10,... | collective-permute-start | bytes 294920 | tf_op jit(solution)/shard_map/ppermute | solution.py:432

commit v5 on v4

--- a/solution.py
+++ b/solution.py
@@ -453,7 +453,7 @@
         lax.ppermute(projected[rank], "tp", [(i, i ^ rank) for i in range(ranks)])
         for rank in range(1, ranks)
     ]
-    late = (projected[0][0, 0] * 0).astype(jnp.int32)
+    late = (far_queries[-1][0, 0] * 0).astype(jnp.int32)
     lengths = jnp.sum(
         jnp.where(jnp.arange(GROUPS)[:, None] == group, suffix_lengths + late, 0), axis=0
     )
@@ -474,7 +474,7 @@
     suffix = suffix[:1] + [across(suffix[side], side=side) for side in range(1, splits)]
 
     for array in arrived:
-        array = array_after(array, *others, *far_queries[1:])
+        array = array_after(array, projected[0], *far_queries[1:])
         sources += [array, across(array, core=1)]
     keys, values = collect_pages(listed, place, sources, pages, splits)
 

time: 55.7 us -> 55.3 us (level)
  Pallas kernels: 19.6 us -> 21.2 us
  starting transfers between devices: 20.4 us -> 18.9 us
  waiting for transfers between devices: 8.34 us -> 6.86 us
  other arithmetic: 1.32 us -> 2.12 us
    pallas_call x3, Pallas kernels: 10.1 us -> 11.6 us  [attend(): pl.pallas_call(body, in_specs=[SMEM, SMEM, SMEM] + [HBM] * len(fetched) +...]
    ppermute x11, starting transfers between devices: 15.1 us -> 13.7 us  [across(): return lax.ppermute(array, 'seq', [(i, i ^ step) for i in range(seq_count)])]
    ppermute x11, waiting for transfers between devices: 3.25 us -> 2.42 us  [across(): return lax.ppermute(array, 'seq', [(i, i ^ step) for i in range(seq_count)])]
    another operation x2, other arithmetic: 0.1 us -> 0.9 us  [local(): jnp.stack([columns(array, split ^ side, HD) for array in (prefix_keys, pr...]
  transfers between devices with their start and end apart: 15 -> 15, of which waited for: 7 -> 8; matrix products, arithmetic and copies ran while one was open for 6% -> 7% of each run, Pallas kernels for 23% -> 25%
where the time goes in v5:
time: 55.3 us; the launch traced here: 54.9 us
  Pallas kernels  21.2 us (38%)
  starting transfers between devices  18.9 us (34%)
  waiting for transfers between devices  6.86 us (12%)
  local copies, waits for them, and re-layouts  4.36 us (8%)
  other arithmetic  2.12 us (4%)
  between operations  1.52 us (3%)
    ppermute x11, starting transfers between devices, across(): return lax.ppermute(array, 'seq', [(i, i ^ step) for i in range(seq_count)])  13.7 us
    pallas_call x3, Pallas kernels, attend(): pl.pallas_call(body, in_specs=[SMEM, SMEM, SMEM] + [HBM] * len(fetched) +...  11.6 us
    pallas_call x1, Pallas kernels, project_kv(): pl.pallas_call(body, in_specs=[SMEM, VMEM, HBM, ANY], out_specs=[VMEM] *...  4.61 us
    ppermute x3, waiting for transfers between devices, quad(): return lax.ppermute(array, ('seq', 'tp'), route)  3.86 us
    ppermute x3, starting transfers between devices, quad(): return lax.ppermute(array, ('seq', 'tp'), route)  3.55 us
    ppermute x11, waiting for transfers between devices, across(): return lax.ppermute(array, 'seq', [(i, i ^ step) for i in range(seq_count)])  2.42 us
    pallas_call x1, Pallas kernels, project(): pl.pallas_call(body, in_specs=[SMEM] + [VMEM] * (len(partials) + 1), out_...  2.31 us
    ppermute x1, starting transfers between devices, local(): lax.ppermute(projected[rank], 'tp', [(i, i ^ rank) for i in range(ranks)])  1.69 us
  transfers between devices with their start and end apart: 15, of which 8 were waited for; matrix products, arithmetic and copies ran while one was open for 7% of the time, Pallas kernels for 25%

profile of v5, /device:TPU:0, one launch (start us, length us, event | category | flops | bytes accessed | tf_op | source)
XLA Modules:
  0.0 54.9 jit_solution(17063314699698534182)
XLA Ops:
  0.6 0.0 copy-start
  0.6 0.0 copy-start.1
  0.7 0.9 %constant_dynamic-slice_fusion.1 = (bf16[24,1024]{1,0:T(8,128)(2,1)S(1)}, bf16[24,1024]{1,0:T(8,128)(2,1)S(1)}) fusion(bf16[24,2048]{1,0:T(8,128)(2,1)} %param.10, s32[]{:T(128)S(6)} %select_n.48, s32[]{:T(128)S(6)} %select_n.49), kind=kLoop, calls=%fused_computation.17 | loop fusion | bytes 196616 | tf_op jit(solution)/shard_map/dynamic_slice | solution.py:435
  1.6 3.0 %collective-permute-start = (bf16[24,1024]{1,0:T(8,128)(2,1)S(1)}, bf16[24,1024]{1,0:T(8,128)(2,1)S(1)}, u32[]{:S(2)}, u32[]{:S(2)}) collective-permute-start(bf16[24,1024]{1,0:T(8,128)(2,1)S(1)} %get-tuple-element.37), channel_id=1, source_target_pairs={{0,4},{2,6},{4,0},{6,2},{8,12},{10,14},{12,8},{14,10},{16,20},{18,... | collective-permute-start | bytes 147464 | tf_op jit(solution)/shard_map/ppermute | solution.py:420
  4.6 1.3 %dynamic-slice_bitcast_fusion = (bf16[1,8,128,128]{3,2,1,0:T(8,128)(2,1)S(1)}, bf16[1,8,128,128]{3,2,1,0:T(8,128)(2,1)S(1)}, bf16[1,8,128,128]{3,2,1,0:T(8,128)(2,1)S(1)}, bf16[1,8,128,128]{3,2,1,0:T(8,128)(2,1)S(1)}) fusion(bf16[8,128,256]{2,1,0:T(8,128)(2,1)} %refs_1_.1, s32[]{:T(128)S(6)} %select_n.54, s32[]{:T(128)S(6)} %select_n.53, ...), kind=kLoop, calls=%fused_computation.2 | loop fusion | bytes 2097160 | tf_op jit(solution)/shard_map/stack | solution.py:443
  5.9 0.1 pad_maximum_fusion
  6.0 0.1 collective-permute-start.5
  6.0 0.8 %pad_maximum_fusion.1 = bf16[2,8,128,128]{3,2,1,0:T(8,128)(2,1)} fusion(bf16[1,8,128,128]{3,2,1,0:T(8,128)(2,1)S(1)} %get-tuple-element.34, bf16[1,8,128,128]{3,2,1,0:T(8,128)(2,1)S(1)} %get-tuple-element.44), kind=kLoop, calls=%fused_computation.1 | loop fusion | flops 262144 | bytes 1048576 | tf_op jit(solution)/shard_map/stack | solution.py:443
  6.9 0.0 collective-permute-start.6
  7.0 0.7 %concatenate.12.place_ref = s32[133]{0:T(256)S(1)} concatenate(s32[1]{0:T(128)} %bitcast, s32[1]{0:T(128)} %bitcast.1, s32[1]{0:T(128)} %bitcast.2, s32[1]{0:T(128)} %bitcast.3, s32[1]{0:T(128)} %bitcast.4, s32[128]{0:T(128)} %param.13), dimensions={0} | concatenate | bytes 1064 | tf_op jit(solution)/shard_map/concatenate | solution.py:416
  7.7 0.0 collective-permute-done
  7.7 4.1 %collective-permute-start.1 = (bf16[48,1024]{1,0:T(8,128)(2,1)S(1)}, bf16[48,1024]{1,0:T(8,128)(2,1)S(1)}, u32[]{:S(2)}, u32[]{:S(2)}) collective-permute-start(bf16[48,1024]{1,0:T(8,128)(2,1)S(1)} %pad_maximum_fusion.2._.refs_0_), channel_id=1, source_target_pairs={{0,24},{2,26},{4,28},{6,30},{8,16},{10,18},{12,20},{14,22},{16,8},... | collective-permute-start | bytes 294920 | tf_op jit(solution)/shard_map/ppermute | solution.py:420
  11.9 0.0 collective-permute-start.2
  11.9 0.7 %collective-permute-start.7 = (bf16[48,1024]{1,0:T(8,128)(2,1)S(1)}, bf16[48,1024]{1,0:T(8,128)(2,1)S(1)}, u32[]{:S(2)}, u32[]{:S(2)}) collective-permute-start(bf16[48,1024]{1,0:T(8,128)(2,1)S(1)} %pad_maximum_fusion.2._.refs_0_), channel_id=1, source_target_pairs={{0,8},{2,10},{4,12},{6,14},{8,0},{10,2},{12,4},{14,6},{16,24},{18,... | collective-permute-start | bytes 294920 | tf_op jit(solution)/shard_map/ppermute | solution.py:420
  12.5 0.9 %copy-done.2 = bf16[24,4096]{1,0:T(8,128)(2,1)S(1)} copy-done((bf16[24,4096]{1,0:T(8,128)(2,1)S(1)}, bf16[24,4096]{1,0:T(8,128)(2,1)}, u32[]{:S(2)}) %copy-start.2) | copy-done | bytes 196632
  13.4 4.6 %shard_map.95 = (f32[24,512]{1,0:T(8,128)S(1)}, f32[24,512]{1,0:T(8,128)S(1)}, s32[34]{0:T(128)S(1)}) custom-call(s32[133]{0:T(256)S(1)} %concatenate.12.place_ref, bf16[24,4096]{1,0:T(8,128)(2,1)S(1)} %copy-done.2, bf16[4096,1024]{1,0:T(8,128)(2,1)} %weight_ref.1, bf16[48,1024]{1,0:T(8,128)(2,1)S(1)} %pad_maximum_fusion.2._.refs_0_), custom_call_target="tpu_custom_call" | custom-call | flops 1 | bytes 1 | tf_op jit(solution)/shard_map/pallas_call | solution.py:93
  18.1 0.0 collective-permute-done.1.refs_4_.refs_1_
  18.1 1.7 %collective-permute-start.3 = (f32[24,512]{1,0:T(8,128)S(1)}, f32[24,512]{1,0:T(8,128)S(1)}, u32[]{:S(2)}, u32[]{:S(2)}) collective-permute-start(f32[24,512]{1,0:T(8,128)S(1)} %get-tuple-element.19), channel_id=1, source_target_pairs={{0,1},{1,0},{2,3},{3,2},{4,5},{5,4},{6,7},{7,6},{8,9},{9,8},{10,11... | collective-permute-start | bytes 147464 | tf_op jit(solution)/shard_map/ppermute | solution.py:453
  19.8 0.5 slice.4
  21.0 0.1 select_reduce_fusion.2
  21.0 0.1 select_reduce_fusion.1
  21.2 0.1 select_reduce_fusion
  21.2 0.0 collective-permute-done.2.refs_3_.refs_2_
  21.3 0.0 collective-permute-done.7.refs_2_.refs_0_
  21.3 0.2 collective-permute-done.6.refs_0_
  21.4 0.1 fusion
  21.6 0.1 pad_maximum_fusion.3
  21.6 0.6 %collective-permute-done.3.refs_1_ = f32[24,512]{1,0:T(8,128)S(1)} collective-permute-done((f32[24,512]{1,0:T(8,128)S(1)}, f32[24,512]{1,0:T(8,128)S(1)}, u32[]{:S(2)}, u32[]{:S(2)}) %collective-permute-start.3) | collective-permute-done | bytes 49184 | tf_op jit(solution)/shard_map/ppermute | solution.py:453
  22.2 1.3 %shard_map.96 = (bf16[24,512]{1,0:T(8,128)(2,1)}, bf16[24,256]{1,0:T(8,128)(2,1)S(1)}, bf16[24,256]{1,0:T(8,128)(2,1)S(1)}) custom-call(s32[133]{0:T(256)S(1)} %concatenate.12.place_ref, f32[24,512]{1,0:T(8,128)S(1)} %get-tuple-element.18.refs_0_.refs_1_, f32[24,512]{1,0:T(8,128)S(1)} %collective-permute-done.3.refs_1_, ...), custom_call_target="tpu_custom_call" | custom-call | flops 1 | bytes 1 | tf_op jit(solution)/shard_map/pallas_call | solution.py:132
  23.5 1.7 %collective-permute-start.4 = (bf16[24,256]{1,0:T(8,128)(2,1)S(1)}, bf16[24,256]{1,0:T(8,128)(2,1)S(1)}, u32[]{:S(2)}, u32[]{:S(2)}) collective-permute-start(bf16[24,256]{1,0:T(8,128)(2,1)S(1)} %get-tuple-element.21), channel_id=1, source_target_pairs={{0,4},{2,6},{4,0},{6,2},{8,12},{10,14},{12,8},{14,10},{16,20},{18,... | collective-permute-start | bytes 36872 | tf_op jit(solution)/shard_map/ppermute | solution.py:420
  25.2 1.3 %shard_map.98 = (bf16[4096,128]{1,0:T(8,128)(2,1)S(1)}, bf16[4096,128]{1,0:T(8,128)(2,1)S(1)}) custom-call(s32[34]{0:T(128)S(1)} %get-tuple-element.17.list_ref, s32[133]{0:T(256)S(1)} %concatenate.12.place_ref, bf16[8,128,256]{2,1,0:T(8,128)(2,1)S(1)} %copy-done, bf16[8,128,256]{2,1,0:T(8,128)(2,1)S(1)} %copy-done.1, ...), custom_call_target="tpu_custom_call" | custom-call | flops 1 | bytes 1 | tf_op jit(solution)/shard_map/pallas_call | solution.py:184
  26.5 0.7 %collective-permute-done.4.refs_4_.refs_2_ = bf16[24,256]{1,0:T(8,128)(2,1)S(1)} collective-permute-done((bf16[24,256]{1,0:T(8,128)(2,1)S(1)}, bf16[24,256]{1,0:T(8,128)(2,1)S(1)}, u32[]{:S(2)}, u32[]{:S(2)}) %collective-permute-start.4) | collective-permute-done | bytes 12320 | tf_op jit(solution)/shard_map/ppermute | solution.py:420
  27.2 5.0 %shard_map.99 = (bf16[400,128]{1,0:T(8,128)(2,1)S(1)}, bf16[400,128]{1,0:T(8,128)(2,1)S(1)}, bf16[1024,4096]{1,0:T(8,128)(2,1)S(1)}) custom-call(s32[34]{0:T(128)S(1)} %get-tuple-element.17.list_ref, s32[2,8]{1,0:T(2,128)S(1)} %copy-done.3, s32[133]{0:T(256)S(1)} %concatenate.12.place_ref, bf16[2048,4096]{1,0:T(8,128)(2,1)} %refs_0_.3, ...), custom_call_target="tpu_custom_call" | custom-call | flops 1610612736 | bytes 1572864 | tf_op jit(solution)/shard_map/pallas_call | solution.py:310
  32.2 3.8 %collective-permute-start.9 = (bf16[400,128]{1,0:T(8,128)(2,1)S(1)}, bf16[400,128]{1,0:T(8,128)(2,1)S(1)}, u32[]{:S(2)}, u32[]{:S(2)}) collective-permute-start(bf16[400,128]{1,0:T(8,128)(2,1)S(1)} %get-tuple-element.24), channel_id=1, source_target_pairs={{0,24},{2,26},{4,28},{6,30},{8,16},{10,18},{12,20},{14,22},{16,8},... | collective-permute-start | bytes 307208 | tf_op jit(solution)/shard_map/ppermute | solution.py:420
  36.0 3.3 %shard_map.100 = bf16[400,128]{1,0:T(8,128)(2,1)S(1)} custom-call(s32[34]{0:T(128)S(1)} %get-tuple-element.17.list_ref, s32[2,8]{1,0:T(2,128)S(1)} %copy-done.3, s32[133]{0:T(256)S(1)} %concatenate.12.place_ref, bf16[48,1024]{1,0:T(8,128)(2,1)S(1)} %collective-permute-done.7.refs_2_.refs_0_, bf16[24,256]{1,0:T(8,128)(2,1)S(1)} %get-tuple-element.20.refs_3_.refs_1_, ...), custom_call_target="tpu_custom_call" | custom-call | flops 805306368 | bytes 1572864 | tf_op jit(solution)/shard_map/pallas_call | solution.py:310
  39.3 0.3 collective-permute-start.11
  39.6 3.3 %shard_map.101.refs_3_ = bf16[400,128]{1,0:T(8,128)(2,1)S(1)} custom-call(s32[34]{0:T(128)S(1)} %get-tuple-element.17.list_ref, s32[2,8]{1,0:T(2,128)S(1)} %copy-done.3, s32[133]{0:T(256)S(1)} %concatenate.12.place_ref, bf16[48,1024]{1,0:T(8,128)(2,1)S(1)} %pad_maximum_fusion.2._.refs_0_, bf16[24,256]{1,0:T(8,128)(2,1)S(1)} %get-tuple-element.20.refs_3_.refs_1_, ...), custom_call_target="tpu_custom_call" | custom-call | flops 805306368 | bytes 1572864 | tf_op jit(solution)/shard_map/pallas_call | solution.py:310
  43.0 0.0 collective-permute-done.9.refs_0_
  43.0 0.5 collective-permute-done.10.refs_1_
  43.5 1.0 %collective-permute-done.11.refs_2_ = bf16[400,128]{1,0:T(8,128)(2,1)S(1)} collective-permute-done((bf16[400,128]{1,0:T(8,128)(2,1)S(1)}, bf16[400,128]{1,0:T(8,128)(2,1)S(1)}, u32[]{:S(2)}, u32[]{:S(2)}) %collective-permute-start.11) | collective-permute-done | bytes 102432 | tf_op jit(solution)/shard_map/ppermute | solution.py:420
  44.5 2.3 %shard_map.102 = (f32[24,2048]{1,0:T(8,128)S(1)}, bf16[24,2048]{1,0:T(8,128)(2,1)S(1)}, bf16[24,2048]{1,0:T(8,128)(2,1)S(1)}, bf16[24,2048]{1,0:T(8,128)(2,1)S(1)}) custom-call(s32[133]{0:T(256)S(1)} %concatenate.12.place_ref, bf16[400,128]{1,0:T(8,128)(2,1)S(1)} %collective-permute-done.9.refs_0_, bf16[400,128]{1,0:T(8,128)(2,1)S(1)} %collective-permute-done.10.refs_1_, ...), custom_call_target="tpu_custom_call" | custom-call | flops 402653184 | bytes 4194304 | tf_op jit(solution)/shard_map/pallas_call | solution.py:375
  46.8 2.1 %collective-permute-start.14 = (bf16[24,2048]{1,0:T(8,128)(2,1)S(1)}, bf16[24,2048]{1,0:T(8,128)(2,1)S(1)}, u32[]{:S(2)}, u32[]{:S(2)}) collective-permute-start(bf16[24,2048]{1,0:T(8,128)(2,1)S(1)} %get-tuple-element.30), channel_id=1, source_target_pairs={{0,5},{1,4},{2,7},{3,6},{4,1},{5,0},{6,3},{7,2},{8,13},{9,12},{10,... | collective-permute-start | bytes 294920 | tf_op jit(solution)/shard_map/ppermute | solution.py:432
  48.9 0.7 %collective-permute-start.13 = (bf16[24,2048]{1,0:T(8,128)(2,1)S(1)}, bf16[24,2048]{1,0:T(8,128)(2,1)S(1)}, u32[]{:S(2)}, u32[]{:S(2)}) collective-permute-start(bf16[24,2048]{1,0:T(8,128)(2,1)S(1)} %get-tuple-element.29), channel_id=1, source_target_pairs={{0,1},{1,0},{2,3},{3,2},{4,5},{5,4},{6,7},{7,6},{8,9},{9,8},{10,11... | collective-permute-start | bytes 294920 | tf_op jit(solution)/shard_map/ppermute | solution.py:432
  49.6 0.8 %collective-permute-start.12 = (bf16[24,2048]{1,0:T(8,128)(2,1)S(1)}, bf16[24,2048]{1,0:T(8,128)(2,1)S(1)}, u32[]{:S(2)}, u32[]{:S(2)}) collective-permute-start(bf16[24,2048]{1,0:T(8,128)(2,1)S(1)} %get-tuple-element.28), channel_id=1, source_target_pairs={{0,4},{1,5},{2,6},{3,7},{4,0},{5,1},{6,2},{7,3},{8,12},{9,13},{10,... | collective-permute-start | bytes 294920 | tf_op jit(solution)/shard_map/ppermute | solution.py:432
  50.4 2.0 %collective-permute-done.14 = bf16[24,2048]{1,0:T(8,128)(2,1)S(1)} collective-permute-done((bf16[24,2048]{1,0:T(8,128)(2,1)S(1)}, bf16[24,2048]{1,0:T(8,128)(2,1)S(1)}, u32[]{:S(2)}, u32[]{:S(2)}) %collective-permute-start.14) | collective-permute-done | bytes 98336 | tf_op jit(solution)/shard_map/ppermute | solution.py:432
  52.4 1.1 %collective-permute-done.13 = bf16[24,2048]{1,0:T(8,128)(2,1)S(1)} collective-permute-done((bf16[24,2048]{1,0:T(8,128)(2,1)S(1)}, bf16[24,2048]{1,0:T(8,128)(2,1)S(1)}, u32[]{:S(2)}, u32[]{:S(2)}) %collective-permute-start.13) | collective-permute-done | bytes 98336 | tf_op jit(solution)/shard_map/ppermute | solution.py:432
  53.5 0.7 %collective-permute-done.12 = bf16[24,2048]{1,0:T(8,128)(2,1)S(1)} collective-permute-done((bf16[24,2048]{1,0:T(8,128)(2,1)S(1)}, bf16[24,2048]{1,0:T(8,128)(2,1)S(1)}, u32[]{:S(2)}, u32[]{:S(2)}) %collective-permute-start.12) | collective-permute-done | bytes 98336 | tf_op jit(solution)/shard_map/ppermute | solution.py:432
  54.3 0.7 %add_convert_fusion = bf16[24,2048]{1,0:T(8,128)(2,1)} fusion(bf16[24,2048]{1,0:T(8,128)(2,1)S(1)} %collective-permute-done.14, bf16[24,2048]{1,0:T(8,128)(2,1)S(1)} %collective-permute-done.13, f32[24,2048]{1,0:T(8,128)S(1)} %get-tuple-element.27, bf16[24,2048]{1,0:T(8,128)(2,1)S(1)} %collective-permute-done.12), kind=kLoop, calls=%fused_computation.6 | loop fusion | flops 344064 | bytes 589824 | tf_op jit(solution)/shard_map/convert_element_type | solution.py:500
  (15 shorter events, 0.1 us)
Async XLA Ops:
  0.6 24.6 %copy-start = (bf16[8,128,256]{2,1,0:T(8,128)(2,1)S(1)}, bf16[8,128,256]{2,1,0:T(8,128)(2,1)}, u32[]{:S(2)}) copy-start(bf16[8,128,256]{2,1,0:T(8,128)(2,1)} %refs_0_.2) | copy-start | bytes 1572868
  0.6 24.6 %copy-start.1 = (bf16[8,128,256]{2,1,0:T(8,128)(2,1)S(1)}, bf16[8,128,256]{2,1,0:T(8,128)(2,1)}, u32[]{:S(2)}) copy-start(bf16[8,128,256]{2,1,0:T(8,128)(2,1)} %refs_1_.1) | copy-start | bytes 1572868
  0.7 20.3 %copy-start.3 = (s32[2,8]{1,0:T(2,128)S(1)}, s32[2,8]{1,0:T(2,128)}, u32[]{:S(2)}) copy-start(s32[2,8]{1,0:T(2,128)} %len_ref.5) | copy-start | bytes 196
  1.6 6.1 %collective-permute-start = (bf16[24,1024]{1,0:T(8,128)(2,1)S(1)}, bf16[24,1024]{1,0:T(8,128)(2,1)S(1)}, u32[]{:S(2)}, u32[]{:S(2)}) collective-permute-start(bf16[24,1024]{1,0:T(8,128)(2,1)S(1)} %get-tuple-element.37), channel_id=1, source_target_pairs={{0,4},{2,6},{4,0},{6,2},{8,12},{10,14},{12,8},{14,10},{16,20},{18,... | collective-permute-start | bytes 147464 | tf_op jit(solution)/shard_map/ppermute | solution.py:420
  6.0 19.2 %collective-permute-start.5 = (bf16[2,8,128,128]{3,2,1,0:T(8,128)(2,1)S(1)}, bf16[2,8,128,128]{3,2,1,0:T(8,128)(2,1)S(1)}, u32[]{:S(2)}, u32[]{:S(2)}) collective-permute-start(bf16[2,8,128,128]{3,2,1,0:T(8,128)(2,1)S(1)} %pad_maximum_fusion), channel_id=1, source_target_pairs={{0,2},{2,0},{4,6},{6,4},{8,10},{10,8},{12,14},{14,12},{16,18},{18,... | collective-permute-start | bytes 1572872 | tf_op jit(solution)/shard_map/ppermute | solution.py:420
  6.9 14.5 %collective-permute-start.6 = (bf16[2,8,128,128]{3,2,1,0:T(8,128)(2,1)}, bf16[2,8,128,128]{3,2,1,0:T(8,128)(2,1)S(1)}, u32[]{:S(2)}, u32[]{:S(2)}) collective-permute-start(bf16[2,8,128,128]{3,2,1,0:T(8,128)(2,1)} %pad_maximum_fusion.1), channel_id=1, source_target_pairs={{0,4},{2,6},{4,0},{6,2},{8,12},{10,14},{12,8},{14,10},{16,20},{18,... | collective-permute-start | bytes 1572872 | tf_op jit(solution)/shard_map/ppermute | solution.py:420
  7.7 10.3 %collective-permute-start.1 = (bf16[48,1024]{1,0:T(8,128)(2,1)S(1)}, bf16[48,1024]{1,0:T(8,128)(2,1)S(1)}, u32[]{:S(2)}, u32[]{:S(2)}) collective-permute-start(bf16[48,1024]{1,0:T(8,128)(2,1)S(1)} %pad_maximum_fusion.2._.refs_0_), channel_id=1, source_target_pairs={{0,24},{2,26},{4,28},{6,30},{8,16},{10,18},{12,20},{14,22},{16,8},... | collective-permute-start | bytes 294920 | tf_op jit(solution)/shard_map/ppermute | solution.py:420
  11.9 9.4 %collective-permute-start.2 = (bf16[48,1024]{1,0:T(8,128)(2,1)S(1)}, bf16[48,1024]{1,0:T(8,128)(2,1)S(1)}, u32[]{:S(2)}, u32[]{:S(2)}) collective-permute-start(bf16[48,1024]{1,0:T(8,128)(2,1)S(1)} %pad_maximum_fusion.2._.refs_0_), channel_id=1, source_target_pairs={{0,16},{2,18},{4,20},{6,22},{8,24},{10,26},{12,28},{14,30},{16,0},... | collective-permute-start | bytes 294920 | tf_op jit(solution)/shard_map/ppermute | solution.py:420
  11.9 9.4 %collective-permute-start.7 = (bf16[48,1024]{1,0:T(8,128)(2,1)S(1)}, bf16[48,1024]{1,0:T(8,128)(2,1)S(1)}, u32[]{:S(2)}, u32[]{:S(2)}) collective-permute-start(bf16[48,1024]{1,0:T(8,128)(2,1)S(1)} %pad_maximum_fusion.2._.refs_0_), channel_id=1, source_target_pairs={{0,8},{2,10},{4,12},{6,14},{8,0},{10,2},{12,4},{14,6},{16,24},{18,... | collective-permute-start | bytes 294920 | tf_op jit(solution)/shard_map/ppermute | solution.py:420
  12.5 0.9 %copy-start.2 = (bf16[24,4096]{1,0:T(8,128)(2,1)S(1)}, bf16[24,4096]{1,0:T(8,128)(2,1)}, u32[]{:S(2)}) copy-start(bf16[24,4096]{1,0:T(8,128)(2,1)} %hidden_ref.1) | copy-start | bytes 589828
  18.1 4.2 %collective-permute-start.3 = (f32[24,512]{1,0:T(8,128)S(1)}, f32[24,512]{1,0:T(8,128)S(1)}, u32[]{:S(2)}, u32[]{:S(2)}) collective-permute-start(f32[24,512]{1,0:T(8,128)S(1)} %get-tuple-element.19), channel_id=1, source_target_pairs={{0,1},{1,0},{2,3},{3,2},{4,5},{5,4},{6,7},{7,6},{8,9},{9,8},{10,11... | collective-permute-start | bytes 147464 | tf_op jit(solution)/shard_map/ppermute | solution.py:453
  21.4 3.8 %collective-permute-start.8 = (bf16[2,8,128,128]{3,2,1,0:T(8,128)(2,1)S(1)}, bf16[2,8,128,128]{3,2,1,0:T(8,128)(2,1)S(1)}, u32[]{:S(2)}, u32[]{:S(2)}) collective-permute-start(bf16[2,8,128,128]{3,2,1,0:T(8,128)(2,1)S(1)} %shard_map.97.refs_3_), channel_id=1, source_target_pairs={{0,2},{2,0},{4,6},{6,4},{8,10},{10,8},{12,14},{14,12},{16,18},{18,... | collective-permute-start | bytes 1572872 | tf_op jit(solution)/shard_map/ppermute | solution.py:420
  23.5 3.7 %collective-permute-start.4 = (bf16[24,256]{1,0:T(8,128)(2,1)S(1)}, bf16[24,256]{1,0:T(8,128)(2,1)S(1)}, u32[]{:S(2)}, u32[]{:S(2)}) collective-permute-start(bf16[24,256]{1,0:T(8,128)(2,1)S(1)} %get-tuple-element.21), channel_id=1, source_target_pairs={{0,4},{2,6},{4,0},{6,2},{8,12},{10,14},{12,8},{14,10},{16,20},{18,... | collective-permute-start | bytes 36872 | tf_op jit(solution)/shard_map/ppermute | solution.py:420
  32.2 10.8 %collective-permute-start.9 = (bf16[400,128]{1,0:T(8,128)(2,1)S(1)}, bf16[400,128]{1,0:T(8,128)(2,1)S(1)}, u32[]{:S(2)}, u32[]{:S(2)}) collective-permute-start(bf16[400,128]{1,0:T(8,128)(2,1)S(1)} %get-tuple-element.24), channel_id=1, source_target_pairs={{0,24},{2,26},{4,28},{6,30},{8,16},{10,18},{12,20},{14,22},{16,8},... | collective-permute-start | bytes 307208 | tf_op jit(solution)/shard_map/ppermute | solution.py:420
  36.0 7.5 %collective-permute-start.10 = (bf16[400,128]{1,0:T(8,128)(2,1)S(1)}, bf16[400,128]{1,0:T(8,128)(2,1)S(1)}, u32[]{:S(2)}, u32[]{:S(2)}) collective-permute-start(bf16[400,128]{1,0:T(8,128)(2,1)S(1)} %get-tuple-element.25), channel_id=1, source_target_pairs={{0,16},{2,18},{4,20},{6,22},{8,24},{10,26},{12,28},{14,30},{16,0},... | collective-permute-start | bytes 307208 | tf_op jit(solution)/shard_map/ppermute | solution.py:420
  39.3 5.2 %collective-permute-start.11 = (bf16[400,128]{1,0:T(8,128)(2,1)S(1)}, bf16[400,128]{1,0:T(8,128)(2,1)S(1)}, u32[]{:S(2)}, u32[]{:S(2)}) collective-permute-start(bf16[400,128]{1,0:T(8,128)(2,1)S(1)} %shard_map.100), channel_id=1, source_target_pairs={{0,8},{2,10},{4,12},{6,14},{8,0},{10,2},{12,4},{14,6},{16,24},{18,... | collective-permute-start | bytes 307208 | tf_op jit(solution)/shard_map/ppermute | solution.py:420
  46.8 5.6 %collective-permute-start.14 = (bf16[24,2048]{1,0:T(8,128)(2,1)S(1)}, bf16[24,2048]{1,0:T(8,128)(2,1)S(1)}, u32[]{:S(2)}, u32[]{:S(2)}) collective-permute-start(bf16[24,2048]{1,0:T(8,128)(2,1)S(1)} %get-tuple-element.30), channel_id=1, source_target_pairs={{0,5},{1,4},{2,7},{3,6},{4,1},{5,0},{6,3},{7,2},{8,13},{9,12},{10,... | collective-permute-start | bytes 294920 | tf_op jit(solution)/shard_map/ppermute | solution.py:432
  48.9 4.6 %collective-permute-start.13 = (bf16[24,2048]{1,0:T(8,128)(2,1)S(1)}, bf16[24,2048]{1,0:T(8,128)(2,1)S(1)}, u32[]{:S(2)}, u32[]{:S(2)}) collective-permute-start(bf16[24,2048]{1,0:T(8,128)(2,1)S(1)} %get-tuple-element.29), channel_id=1, source_target_pairs={{0,1},{1,0},{2,3},{3,2},{4,5},{5,4},{6,7},{7,6},{8,9},{9,8},{10,11... | collective-permute-start | bytes 294920 | tf_op jit(solution)/shard_map/ppermute | solution.py:432
  49.6 4.6 %collective-permute-start.12 = (bf16[24,2048]{1,0:T(8,128)(2,1)S(1)}, bf16[24,2048]{1,0:T(8,128)(2,1)S(1)}, u32[]{:S(2)}, u32[]{:S(2)}) collective-permute-start(bf16[24,2048]{1,0:T(8,128)(2,1)S(1)} %get-tuple-element.28), channel_id=1, source_target_pairs={{0,4},{1,5},{2,6},{3,7},{4,0},{5,1},{6,2},{7,3},{8,12},{9,13},{10,... | collective-permute-start | bytes 294920 | tf_op jit(solution)/shard_map/ppermute | solution.py:432

commit v6 on v4

--- a/solution.py
+++ b/solution.py
@@ -263,16 +263,18 @@
                 stacked[b], keys_ref[span, :], NT, preferred_element_type=F32
             )
 
-        def turn(c, carry):
+        def turn(c, last):
             span = pl.ds(pl.multiple_of(c * wide, wide), wide)
             chunk_values = jnp.concatenate(
                 [values_ref[span, :], jnp.ones((wide, HD), BF16)], axis=1
             )
             for b in range(blocks):
-                pieces = [
-                    jnp.where(c * CHUNK + j < count, scores[b, :, j * PAGE : (j + 1) * PAGE], LOW)
-                    for j in range(CHUNK)
-                ]
+                pieces = [scores[b, :, j * PAGE : (j + 1) * PAGE] for j in range(CHUNK)]
+                if last:
+                    pieces = [
+                        jnp.where(c * CHUNK + j < count, piece, LOW)
+                        for j, piece in enumerate(pieces)
+                    ]
                 best = functools.reduce(jnp.maximum, pieces)
                 before = top[b]
                 highest = jnp.maximum(before, jnp.max(best, axis=1, keepdims=True))
@@ -284,12 +286,21 @@
                 added = jnp.dot(weights, chunk_values, preferred_element_type=F32)
                 total[b] = total[b] * jnp.concatenate([factor, factor], axis=1) + added
                 top[b] = highest
-                score(b, jnp.minimum(c + 1, slots // CHUNK - 1))
+                if not last:
+                    score(b, c + 1)
+
+        def full_turn(c, carry):
+            turn(c, False)
             return carry
 
         for b in range(blocks):
             score(b, 0)
-        lax.fori_loop(0, turns, turn, 0)
+        lax.fori_loop(0, turns - 1, full_turn, 0)
+
+        @pl.when(turns > 0)
+        def _():
+            turn(turns - 1, True)
+
         for b in range(blocks):
             sums = total[b, :, HD:]
             some = sums > 0.0

time: 55.7 us -> 55.1 us (0.989)
  no operation moved by 1% of the time
where the time goes in v6:
time: 55.1 us; the launch traced here: 54.9 us
  starting transfers between devices  20.4 us (37%)
  Pallas kernels  19.4 us (35%)
  waiting for transfers between devices  7.93 us (14%)
  local copies, waits for them, and re-layouts  4.36 us (8%)
  between operations  1.54 us (3%)
  other arithmetic  1.32 us (2%)
    ppermute x11, starting transfers between devices, across(): return lax.ppermute(array, 'seq', [(i, i ^ step) for i in range(seq_count)])  15.1 us
    pallas_call x3, Pallas kernels, attend(): pl.pallas_call(body, in_specs=[SMEM, SMEM, SMEM] + [HBM] * len(fetched) +...  9.93 us
    pallas_call x1, Pallas kernels, project_kv(): pl.pallas_call(body, in_specs=[SMEM, VMEM, HBM, ANY], out_specs=[VMEM] *...  4.61 us
    ppermute x3, waiting for transfers between devices, quad(): return lax.ppermute(array, ('seq', 'tp'), route)  3.98 us
    ppermute x3, starting transfers between devices, quad(): return lax.ppermute(array, ('seq', 'tp'), route)  3.55 us
    ppermute x11, waiting for transfers between devices, across(): return lax.ppermute(array, 'seq', [(i, i ^ step) for i in range(seq_count)])  2.96 us
    pallas_call x1, Pallas kernels, project(): pl.pallas_call(body, in_specs=[SMEM] + [VMEM] * (len(partials) + 1), out_...  2.3 us
    ppermute x1, starting transfers between devices, local(): lax.ppermute(projected[rank], 'tp', [(i, i ^ rank) for i in range(ranks)])  1.7 us
  transfers between devices with their start and end apart: 15, of which 7 were waited for; matrix products, arithmetic and copies ran while one was open for 6% of the time, Pallas kernels for 23%

profile of v6, /device:TPU:0, one launch (start us, length us, event | category | flops | bytes accessed | tf_op | source)
XLA Modules:
  0.0 54.9 jit_solution(15516015009229794521)
XLA Ops:
  0.6 0.0 copy-start
  0.6 0.0 copy-start.1
  0.7 0.9 %constant_dynamic-slice_fusion.1 = (bf16[24,1024]{1,0:T(8,128)(2,1)S(1)}, bf16[24,1024]{1,0:T(8,128)(2,1)S(1)}) fusion(bf16[24,2048]{1,0:T(8,128)(2,1)} %param.10, s32[]{:T(128)S(6)} %select_n.48, s32[]{:T(128)S(6)} %select_n.49), kind=kLoop, calls=%fused_computation.17 | loop fusion | bytes 196616 | tf_op jit(solution)/shard_map/dynamic_slice | solution.py:446
  1.6 3.0 %collective-permute-start = (bf16[24,1024]{1,0:T(8,128)(2,1)S(1)}, bf16[24,1024]{1,0:T(8,128)(2,1)S(1)}, u32[]{:S(2)}, u32[]{:S(2)}) collective-permute-start(bf16[24,1024]{1,0:T(8,128)(2,1)S(1)} %get-tuple-element.37), channel_id=1, source_target_pairs={{0,4},{2,6},{4,0},{6,2},{8,12},{10,14},{12,8},{14,10},{16,20},{18,... | collective-permute-start | bytes 147464 | tf_op jit(solution)/shard_map/ppermute | solution.py:431
  4.6 1.3 %dynamic-slice_bitcast_fusion = (bf16[1,8,128,128]{3,2,1,0:T(8,128)(2,1)S(1)}, bf16[1,8,128,128]{3,2,1,0:T(8,128)(2,1)S(1)}, bf16[1,8,128,128]{3,2,1,0:T(8,128)(2,1)S(1)}, bf16[1,8,128,128]{3,2,1,0:T(8,128)(2,1)S(1)}) fusion(bf16[8,128,256]{2,1,0:T(8,128)(2,1)} %refs_1_.1, s32[]{:T(128)S(6)} %select_n.54, s32[]{:T(128)S(6)} %select_n.53, ...), kind=kLoop, calls=%fused_computation.2 | loop fusion | bytes 2097160 | tf_op jit(solution)/shard_map/stack | solution.py:454
  5.9 0.1 pad_maximum_fusion.1
  6.0 0.1 collective-permute-start.6
  6.1 0.1 pad_maximum_fusion
  6.2 0.7 %concatenate.12.place_ref = s32[133]{0:T(256)S(1)} concatenate(s32[1]{0:T(128)} %bitcast, s32[1]{0:T(128)} %bitcast.1, s32[1]{0:T(128)} %bitcast.2, s32[1]{0:T(128)} %bitcast.3, s32[1]{0:T(128)} %bitcast.4, s32[128]{0:T(128)} %param.13), dimensions={0} | concatenate | bytes 1064 | tf_op jit(solution)/shard_map/concatenate | solution.py:427
  6.9 4.1 %collective-permute-start.1 = (bf16[48,1024]{1,0:T(8,128)(2,1)S(1)}, bf16[48,1024]{1,0:T(8,128)(2,1)S(1)}, u32[]{:S(2)}, u32[]{:S(2)}) collective-permute-start(bf16[48,1024]{1,0:T(8,128)(2,1)S(1)} %pad_maximum_fusion.2._.refs_0_), channel_id=1, source_target_pairs={{0,24},{2,26},{4,28},{6,30},{8,16},{10,18},{12,20},{14,22},{16,8},... | collective-permute-start | bytes 294920 | tf_op jit(solution)/shard_map/ppermute | solution.py:431
  11.1 0.0 collective-permute-start.2
  11.1 0.6 %collective-permute-start.7 = (bf16[48,1024]{1,0:T(8,128)(2,1)S(1)}, bf16[48,1024]{1,0:T(8,128)(2,1)S(1)}, u32[]{:S(2)}, u32[]{:S(2)}) collective-permute-start(bf16[48,1024]{1,0:T(8,128)(2,1)S(1)} %pad_maximum_fusion.2._.refs_0_), channel_id=1, source_target_pairs={{0,8},{2,10},{4,12},{6,14},{8,0},{10,2},{12,4},{14,6},{16,24},{18,... | collective-permute-start | bytes 294920 | tf_op jit(solution)/shard_map/ppermute | solution.py:431
  11.7 0.9 %copy-done.2 = bf16[24,4096]{1,0:T(8,128)(2,1)S(1)} copy-done((bf16[24,4096]{1,0:T(8,128)(2,1)S(1)}, bf16[24,4096]{1,0:T(8,128)(2,1)}, u32[]{:S(2)}) %copy-start.2) | copy-done | bytes 196632
  12.6 4.6 %shard_map.95 = (f32[24,512]{1,0:T(8,128)S(1)}, f32[24,512]{1,0:T(8,128)S(1)}, s32[34]{0:T(128)S(1)}) custom-call(s32[133]{0:T(256)S(1)} %concatenate.12.place_ref, bf16[24,4096]{1,0:T(8,128)(2,1)S(1)} %copy-done.2, bf16[4096,1024]{1,0:T(8,128)(2,1)} %weight_ref.1, bf16[48,1024]{1,0:T(8,128)(2,1)S(1)} %pad_maximum_fusion.2._.refs_0_), custom_call_target="tpu_custom_call" | custom-call | flops 1 | bytes 1 | tf_op jit(solution)/shard_map/pallas_call | solution.py:93
  17.3 1.7 %collective-permute-start.3 = (f32[24,512]{1,0:T(8,128)S(1)}, f32[24,512]{1,0:T(8,128)S(1)}, u32[]{:S(2)}, u32[]{:S(2)}) collective-permute-start(f32[24,512]{1,0:T(8,128)S(1)} %get-tuple-element.19), channel_id=1, source_target_pairs={{0,1},{1,0},{2,3},{3,2},{4,5},{5,4},{6,7},{7,6},{8,9},{9,8},{10,11... | collective-permute-start | bytes 147464 | tf_op jit(solution)/shard_map/ppermute | solution.py:464
  19.0 0.5 slice.3
  20.1 0.1 select_reduce_fusion.2
  20.2 0.1 select_reduce_fusion.1
  20.3 0.1 select_reduce_fusion
  20.4 1.0 %collective-permute-done.3.refs_1_ = f32[24,512]{1,0:T(8,128)S(1)} collective-permute-done((f32[24,512]{1,0:T(8,128)S(1)}, f32[24,512]{1,0:T(8,128)S(1)}, u32[]{:S(2)}, u32[]{:S(2)}) %collective-permute-start.3) | collective-permute-done | bytes 49184 | tf_op jit(solution)/shard_map/ppermute | solution.py:464
  21.4 0.0 collective-permute-start.5
  21.4 0.0 collective-permute-done.1.refs_4_.refs_1_
  21.4 0.0 collective-permute-done.2.refs_3_.refs_2_
  21.4 0.0 collective-permute-done.7.refs_2_.refs_0_
  21.4 0.0 collective-permute-done.6.refs_0_
  21.5 0.6 %collective-permute-start.8 = (bf16[2,8,128,128]{3,2,1,0:T(8,128)(2,1)S(1)}, bf16[2,8,128,128]{3,2,1,0:T(8,128)(2,1)S(1)}, u32[]{:S(2)}, u32[]{:S(2)}) collective-permute-start(bf16[2,8,128,128]{3,2,1,0:T(8,128)(2,1)S(1)} %shard_map.97.refs_3_), channel_id=1, source_target_pairs={{0,2},{2,0},{4,6},{6,4},{8,10},{10,8},{12,14},{14,12},{16,18},{18,... | collective-permute-start | bytes 1572872 | tf_op jit(solution)/shard_map/ppermute | solution.py:431
  22.0 0.1 fusion
  22.2 0.1 pad_maximum_fusion.3
  22.2 1.3 %shard_map.96 = (bf16[24,512]{1,0:T(8,128)(2,1)}, bf16[24,256]{1,0:T(8,128)(2,1)S(1)}, bf16[24,256]{1,0:T(8,128)(2,1)S(1)}) custom-call(s32[133]{0:T(256)S(1)} %concatenate.12.place_ref, f32[24,512]{1,0:T(8,128)S(1)} %get-tuple-element.18.refs_0_, f32[24,512]{1,0:T(8,128)S(1)} %collective-permute-done.3.refs_1_, f32[24,128]{1,0:T(8,128)S(1)} %get-tuple-element.41.refs_2_, ...), custom_call_target="tpu_custom_call" | custom-call | flops 1 | bytes 1 | tf_op jit(solution)/shard_map/pallas_call | solution.py:132
  23.6 1.7 %collective-permute-start.4 = (bf16[24,256]{1,0:T(8,128)(2,1)S(1)}, bf16[24,256]{1,0:T(8,128)(2,1)S(1)}, u32[]{:S(2)}, u32[]{:S(2)}) collective-permute-start(bf16[24,256]{1,0:T(8,128)(2,1)S(1)} %get-tuple-element.21), channel_id=1, source_target_pairs={{0,4},{2,6},{4,0},{6,2},{8,12},{10,14},{12,8},{14,10},{16,20},{18,... | collective-permute-start | bytes 36872 | tf_op jit(solution)/shard_map/ppermute | solution.py:431
  25.3 1.2 %shard_map.98 = (bf16[4096,128]{1,0:T(8,128)(2,1)S(1)}, bf16[4096,128]{1,0:T(8,128)(2,1)S(1)}) custom-call(s32[34]{0:T(128)S(1)} %get-tuple-element.17.list_ref, s32[133]{0:T(256)S(1)} %concatenate.12.place_ref, bf16[8,128,256]{2,1,0:T(8,128)(2,1)S(1)} %copy-done, bf16[8,128,256]{2,1,0:T(8,128)(2,1)S(1)} %copy-done.1, ...), custom_call_target="tpu_custom_call" | custom-call | flops 1 | bytes 1 | tf_op jit(solution)/shard_map/pallas_call | solution.py:184
  26.5 0.7 %collective-permute-done.4.refs_4_.refs_2_ = bf16[24,256]{1,0:T(8,128)(2,1)S(1)} collective-permute-done((bf16[24,256]{1,0:T(8,128)(2,1)S(1)}, bf16[24,256]{1,0:T(8,128)(2,1)S(1)}, u32[]{:S(2)}, u32[]{:S(2)}) %collective-permute-start.4) | collective-permute-done | bytes 12320 | tf_op jit(solution)/shard_map/ppermute | solution.py:431
  27.3 4.3 %shard_map.99 = (bf16[400,128]{1,0:T(8,128)(2,1)S(1)}, bf16[400,128]{1,0:T(8,128)(2,1)S(1)}, bf16[1024,4096]{1,0:T(8,128)(2,1)S(1)}) custom-call(s32[34]{0:T(128)S(1)} %get-tuple-element.17.list_ref, s32[2,8]{1,0:T(2,128)S(1)} %copy-done.3, s32[133]{0:T(256)S(1)} %concatenate.12.place_ref, bf16[2048,4096]{1,0:T(8,128)(2,1)} %refs_0_.3, ...), custom_call_target="tpu_custom_call" | custom-call | flops 1610612736 | bytes 1572864 | tf_op jit(solution)/shard_map/pallas_call | solution.py:321
  31.6 3.8 %collective-permute-start.9 = (bf16[400,128]{1,0:T(8,128)(2,1)S(1)}, bf16[400,128]{1,0:T(8,128)(2,1)S(1)}, u32[]{:S(2)}, u32[]{:S(2)}) collective-permute-start(bf16[400,128]{1,0:T(8,128)(2,1)S(1)} %get-tuple-element.24), channel_id=1, source_target_pairs={{0,24},{2,26},{4,28},{6,30},{8,16},{10,18},{12,20},{14,22},{16,8},... | collective-permute-start | bytes 307208 | tf_op jit(solution)/shard_map/ppermute | solution.py:431
  35.4 2.8 %shard_map.100 = bf16[400,128]{1,0:T(8,128)(2,1)S(1)} custom-call(s32[34]{0:T(128)S(1)} %get-tuple-element.17.list_ref, s32[2,8]{1,0:T(2,128)S(1)} %copy-done.3, s32[133]{0:T(256)S(1)} %concatenate.12.place_ref, bf16[48,1024]{1,0:T(8,128)(2,1)S(1)} %collective-permute-done.7.refs_2_.refs_0_, bf16[24,256]{1,0:T(8,128)(2,1)S(1)} %get-tuple-element.20.refs_3_.refs_1_, ...), custom_call_target="tpu_custom_call" | custom-call | flops 805306368 | bytes 1572864 | tf_op jit(solution)/shard_map/pallas_call | solution.py:321
  38.2 1.1 %collective-permute-start.11 = (bf16[400,128]{1,0:T(8,128)(2,1)S(1)}, bf16[400,128]{1,0:T(8,128)(2,1)S(1)}, u32[]{:S(2)}, u32[]{:S(2)}) collective-permute-start(bf16[400,128]{1,0:T(8,128)(2,1)S(1)} %shard_map.100), channel_id=1, source_target_pairs={{0,8},{2,10},{4,12},{6,14},{8,0},{10,2},{12,4},{14,6},{16,24},{18,... | collective-permute-start | bytes 307208 | tf_op jit(solution)/shard_map/ppermute | solution.py:431
  39.3 2.8 %shard_map.101.refs_3_ = bf16[400,128]{1,0:T(8,128)(2,1)S(1)} custom-call(s32[34]{0:T(128)S(1)} %get-tuple-element.17.list_ref, s32[2,8]{1,0:T(2,128)S(1)} %copy-done.3, s32[133]{0:T(256)S(1)} %concatenate.12.place_ref, bf16[48,1024]{1,0:T(8,128)(2,1)S(1)} %pad_maximum_fusion.2._.refs_0_, bf16[24,256]{1,0:T(8,128)(2,1)S(1)} %get-tuple-element.20.refs_3_.refs_1_, ...), custom_call_target="tpu_custom_call" | custom-call | flops 805306368 | bytes 1572864 | tf_op jit(solution)/shard_map/pallas_call | solution.py:321
  42.1 0.0 collective-permute-done.9.refs_0_
  42.2 1.3 %collective-permute-done.10.refs_1_ = bf16[400,128]{1,0:T(8,128)(2,1)S(1)} collective-permute-done((bf16[400,128]{1,0:T(8,128)(2,1)S(1)}, bf16[400,128]{1,0:T(8,128)(2,1)S(1)}, u32[]{:S(2)}, u32[]{:S(2)}) %collective-permute-start.10) | collective-permute-done | bytes 102432 | tf_op jit(solution)/shard_map/ppermute | solution.py:431
  43.4 0.9 %collective-permute-done.11.refs_2_ = bf16[400,128]{1,0:T(8,128)(2,1)S(1)} collective-permute-done((bf16[400,128]{1,0:T(8,128)(2,1)S(1)}, bf16[400,128]{1,0:T(8,128)(2,1)S(1)}, u32[]{:S(2)}, u32[]{:S(2)}) %collective-permute-start.11) | collective-permute-done | bytes 102432 | tf_op jit(solution)/shard_map/ppermute | solution.py:431
  44.4 2.3 %shard_map.102 = (f32[24,2048]{1,0:T(8,128)S(1)}, bf16[24,2048]{1,0:T(8,128)(2,1)S(1)}, bf16[24,2048]{1,0:T(8,128)(2,1)S(1)}, bf16[24,2048]{1,0:T(8,128)(2,1)S(1)}) custom-call(s32[133]{0:T(256)S(1)} %concatenate.12.place_ref, bf16[400,128]{1,0:T(8,128)(2,1)S(1)} %collective-permute-done.9.refs_0_, bf16[400,128]{1,0:T(8,128)(2,1)S(1)} %collective-permute-done.10.refs_1_, ...), custom_call_target="tpu_custom_call" | custom-call | flops 402653184 | bytes 4194304 | tf_op jit(solution)/shard_map/pallas_call | solution.py:386
  46.7 2.4 %collective-permute-start.14 = (bf16[24,2048]{1,0:T(8,128)(2,1)S(1)}, bf16[24,2048]{1,0:T(8,128)(2,1)S(1)}, u32[]{:S(2)}, u32[]{:S(2)}) collective-permute-start(bf16[24,2048]{1,0:T(8,128)(2,1)S(1)} %get-tuple-element.30), channel_id=1, source_target_pairs={{0,5},{1,4},{2,7},{3,6},{4,1},{5,0},{6,3},{7,2},{8,13},{9,12},{10,... | collective-permute-start | bytes 294920 | tf_op jit(solution)/shard_map/ppermute | solution.py:443
  49.0 0.5 collective-permute-start.13
  49.6 0.6 %collective-permute-start.12 = (bf16[24,2048]{1,0:T(8,128)(2,1)S(1)}, bf16[24,2048]{1,0:T(8,128)(2,1)S(1)}, u32[]{:S(2)}, u32[]{:S(2)}) collective-permute-start(bf16[24,2048]{1,0:T(8,128)(2,1)S(1)} %get-tuple-element.28), channel_id=1, source_target_pairs={{0,4},{1,5},{2,6},{3,7},{4,0},{5,1},{6,2},{7,3},{8,12},{9,13},{10,... | collective-permute-start | bytes 294920 | tf_op jit(solution)/shard_map/ppermute | solution.py:443
  50.2 2.0 %collective-permute-done.14 = bf16[24,2048]{1,0:T(8,128)(2,1)S(1)} collective-permute-done((bf16[24,2048]{1,0:T(8,128)(2,1)S(1)}, bf16[24,2048]{1,0:T(8,128)(2,1)S(1)}, u32[]{:S(2)}, u32[]{:S(2)}) %collective-permute-start.14) | collective-permute-done | bytes 98336 | tf_op jit(solution)/shard_map/ppermute | solution.py:443
  52.3 1.4 %collective-permute-done.13 = bf16[24,2048]{1,0:T(8,128)(2,1)S(1)} collective-permute-done((bf16[24,2048]{1,0:T(8,128)(2,1)S(1)}, bf16[24,2048]{1,0:T(8,128)(2,1)S(1)}, u32[]{:S(2)}, u32[]{:S(2)}) %collective-permute-start.13) | collective-permute-done | bytes 98336 | tf_op jit(solution)/shard_map/ppermute | solution.py:443
  53.7 0.5 collective-permute-done.12
  54.2 0.7 %add_convert_fusion = bf16[24,2048]{1,0:T(8,128)(2,1)} fusion(bf16[24,2048]{1,0:T(8,128)(2,1)S(1)} %collective-permute-done.14, bf16[24,2048]{1,0:T(8,128)(2,1)S(1)} %collective-permute-done.13, f32[24,2048]{1,0:T(8,128)S(1)} %get-tuple-element.27, bf16[24,2048]{1,0:T(8,128)(2,1)S(1)} %collective-permute-done.12), kind=kLoop, calls=%fused_computation.6 | loop fusion | flops 344064 | bytes 589824 | tf_op jit(solution)/shard_map/convert_element_type | solution.py:511
  (15 shorter events, 0.1 us)
Async XLA Ops:
  0.6 24.6 %copy-start = (bf16[8,128,256]{2,1,0:T(8,128)(2,1)S(1)}, bf16[8,128,256]{2,1,0:T(8,128)(2,1)}, u32[]{:S(2)}) copy-start(bf16[8,128,256]{2,1,0:T(8,128)(2,1)} %refs_0_.2) | copy-start | bytes 1572868
  0.6 24.6 %copy-start.1 = (bf16[8,128,256]{2,1,0:T(8,128)(2,1)S(1)}, bf16[8,128,256]{2,1,0:T(8,128)(2,1)}, u32[]{:S(2)}) copy-start(bf16[8,128,256]{2,1,0:T(8,128)(2,1)} %refs_1_.1) | copy-start | bytes 1572868
  0.7 19.5 %copy-start.3 = (s32[2,8]{1,0:T(2,128)S(1)}, s32[2,8]{1,0:T(2,128)}, u32[]{:S(2)}) copy-start(s32[2,8]{1,0:T(2,128)} %len_ref.5) | copy-start | bytes 196
  1.6 5.3 %collective-permute-start = (bf16[24,1024]{1,0:T(8,128)(2,1)S(1)}, bf16[24,1024]{1,0:T(8,128)(2,1)S(1)}, u32[]{:S(2)}, u32[]{:S(2)}) collective-permute-start(bf16[24,1024]{1,0:T(8,128)(2,1)S(1)} %get-tuple-element.37), channel_id=1, source_target_pairs={{0,4},{2,6},{4,0},{6,2},{8,12},{10,14},{12,8},{14,10},{16,20},{18,... | collective-permute-start | bytes 147464 | tf_op jit(solution)/shard_map/ppermute | solution.py:431
  6.0 15.5 %collective-permute-start.6 = (bf16[2,8,128,128]{3,2,1,0:T(8,128)(2,1)S(1)}, bf16[2,8,128,128]{3,2,1,0:T(8,128)(2,1)S(1)}, u32[]{:S(2)}, u32[]{:S(2)}) collective-permute-start(bf16[2,8,128,128]{3,2,1,0:T(8,128)(2,1)S(1)} %pad_maximum_fusion.1), channel_id=1, source_target_pairs={{0,4},{2,6},{4,0},{6,2},{8,12},{10,14},{12,8},{14,10},{16,20},{18,... | collective-permute-start | bytes 1572872 | tf_op jit(solution)/shard_map/ppermute | solution.py:431
  6.9 14.5 %collective-permute-start.1 = (bf16[48,1024]{1,0:T(8,128)(2,1)S(1)}, bf16[48,1024]{1,0:T(8,128)(2,1)S(1)}, u32[]{:S(2)}, u32[]{:S(2)}) collective-permute-start(bf16[48,1024]{1,0:T(8,128)(2,1)S(1)} %pad_maximum_fusion.2._.refs_0_), channel_id=1, source_target_pairs={{0,24},{2,26},{4,28},{6,30},{8,16},{10,18},{12,20},{14,22},{16,8},... | collective-permute-start | bytes 294920 | tf_op jit(solution)/shard_map/ppermute | solution.py:431
  11.1 10.4 %collective-permute-start.2 = (bf16[48,1024]{1,0:T(8,128)(2,1)S(1)}, bf16[48,1024]{1,0:T(8,128)(2,1)S(1)}, u32[]{:S(2)}, u32[]{:S(2)}) collective-permute-start(bf16[48,1024]{1,0:T(8,128)(2,1)S(1)} %pad_maximum_fusion.2._.refs_0_), channel_id=1, source_target_pairs={{0,16},{2,18},{4,20},{6,22},{8,24},{10,26},{12,28},{14,30},{16,0},... | collective-permute-start | bytes 294920 | tf_op jit(solution)/shard_map/ppermute | solution.py:431
  11.1 10.4 %collective-permute-start.7 = (bf16[48,1024]{1,0:T(8,128)(2,1)S(1)}, bf16[48,1024]{1,0:T(8,128)(2,1)S(1)}, u32[]{:S(2)}, u32[]{:S(2)}) collective-permute-start(bf16[48,1024]{1,0:T(8,128)(2,1)S(1)} %pad_maximum_fusion.2._.refs_0_), channel_id=1, source_target_pairs={{0,8},{2,10},{4,12},{6,14},{8,0},{10,2},{12,4},{14,6},{16,24},{18,... | collective-permute-start | bytes 294920 | tf_op jit(solution)/shard_map/ppermute | solution.py:431
  11.7 0.9 %copy-start.2 = (bf16[24,4096]{1,0:T(8,128)(2,1)S(1)}, bf16[24,4096]{1,0:T(8,128)(2,1)}, u32[]{:S(2)}) copy-start(bf16[24,4096]{1,0:T(8,128)(2,1)} %hidden_ref.1) | copy-start | bytes 589828
  17.3 4.2 %collective-permute-start.3 = (f32[24,512]{1,0:T(8,128)S(1)}, f32[24,512]{1,0:T(8,128)S(1)}, u32[]{:S(2)}, u32[]{:S(2)}) collective-permute-start(f32[24,512]{1,0:T(8,128)S(1)} %get-tuple-element.19), channel_id=1, source_target_pairs={{0,1},{1,0},{2,3},{3,2},{4,5},{5,4},{6,7},{7,6},{8,9},{9,8},{10,11... | collective-permute-start | bytes 147464 | tf_op jit(solution)/shard_map/ppermute | solution.py:464
  21.4 3.8 %collective-permute-start.5 = (bf16[2,8,128,128]{3,2,1,0:T(8,128)(2,1)S(1)}, bf16[2,8,128,128]{3,2,1,0:T(8,128)(2,1)S(1)}, u32[]{:S(2)}, u32[]{:S(2)}) collective-permute-start(bf16[2,8,128,128]{3,2,1,0:T(8,128)(2,1)S(1)} %pad_maximum_fusion), channel_id=1, source_target_pairs={{0,2},{2,0},{4,6},{6,4},{8,10},{10,8},{12,14},{14,12},{16,18},{18,... | collective-permute-start | bytes 1572872 | tf_op jit(solution)/shard_map/ppermute | solution.py:431
  21.5 3.8 %collective-permute-start.8 = (bf16[2,8,128,128]{3,2,1,0:T(8,128)(2,1)S(1)}, bf16[2,8,128,128]{3,2,1,0:T(8,128)(2,1)S(1)}, u32[]{:S(2)}, u32[]{:S(2)}) collective-permute-start(bf16[2,8,128,128]{3,2,1,0:T(8,128)(2,1)S(1)} %shard_map.97.refs_3_), channel_id=1, source_target_pairs={{0,2},{2,0},{4,6},{6,4},{8,10},{10,8},{12,14},{14,12},{16,18},{18,... | collective-permute-start | bytes 1572872 | tf_op jit(solution)/shard_map/ppermute | solution.py:431
  23.6 3.7 %collective-permute-start.4 = (bf16[24,256]{1,0:T(8,128)(2,1)S(1)}, bf16[24,256]{1,0:T(8,128)(2,1)S(1)}, u32[]{:S(2)}, u32[]{:S(2)}) collective-permute-start(bf16[24,256]{1,0:T(8,128)(2,1)S(1)} %get-tuple-element.21), channel_id=1, source_target_pairs={{0,4},{2,6},{4,0},{6,2},{8,12},{10,14},{12,8},{14,10},{16,20},{18,... | collective-permute-start | bytes 36872 | tf_op jit(solution)/shard_map/ppermute | solution.py:431
  31.6 10.6 %collective-permute-start.9 = (bf16[400,128]{1,0:T(8,128)(2,1)S(1)}, bf16[400,128]{1,0:T(8,128)(2,1)S(1)}, u32[]{:S(2)}, u32[]{:S(2)}) collective-permute-start(bf16[400,128]{1,0:T(8,128)(2,1)S(1)} %get-tuple-element.24), channel_id=1, source_target_pairs={{0,24},{2,26},{4,28},{6,30},{8,16},{10,18},{12,20},{14,22},{16,8},... | collective-permute-start | bytes 307208 | tf_op jit(solution)/shard_map/ppermute | solution.py:431
  35.4 8.0 %collective-permute-start.10 = (bf16[400,128]{1,0:T(8,128)(2,1)S(1)}, bf16[400,128]{1,0:T(8,128)(2,1)S(1)}, u32[]{:S(2)}, u32[]{:S(2)}) collective-permute-start(bf16[400,128]{1,0:T(8,128)(2,1)S(1)} %get-tuple-element.25), channel_id=1, source_target_pairs={{0,16},{2,18},{4,20},{6,22},{8,24},{10,26},{12,28},{14,30},{16,0},... | collective-permute-start | bytes 307208 | tf_op jit(solution)/shard_map/ppermute | solution.py:431
  38.2 6.2 %collective-permute-start.11 = (bf16[400,128]{1,0:T(8,128)(2,1)S(1)}, bf16[400,128]{1,0:T(8,128)(2,1)S(1)}, u32[]{:S(2)}, u32[]{:S(2)}) collective-permute-start(bf16[400,128]{1,0:T(8,128)(2,1)S(1)} %shard_map.100), channel_id=1, source_target_pairs={{0,8},{2,10},{4,12},{6,14},{8,0},{10,2},{12,4},{14,6},{16,24},{18,... | collective-permute-start | bytes 307208 | tf_op jit(solution)/shard_map/ppermute | solution.py:431
  46.7 5.6 %collective-permute-start.14 = (bf16[24,2048]{1,0:T(8,128)(2,1)S(1)}, bf16[24,2048]{1,0:T(8,128)(2,1)S(1)}, u32[]{:S(2)}, u32[]{:S(2)}) collective-permute-start(bf16[24,2048]{1,0:T(8,128)(2,1)S(1)} %get-tuple-element.30), channel_id=1, source_target_pairs={{0,5},{1,4},{2,7},{3,6},{4,1},{5,0},{6,3},{7,2},{8,13},{9,12},{10,... | collective-permute-start | bytes 294920 | tf_op jit(solution)/shard_map/ppermute | solution.py:443
  49.0 4.6 %collective-permute-start.13 = (bf16[24,2048]{1,0:T(8,128)(2,1)S(1)}, bf16[24,2048]{1,0:T(8,128)(2,1)S(1)}, u32[]{:S(2)}, u32[]{:S(2)}) collective-permute-start(bf16[24,2048]{1,0:T(8,128)(2,1)S(1)} %get-tuple-element.29), channel_id=1, source_target_pairs={{0,1},{1,0},{2,3},{3,2},{4,5},{5,4},{6,7},{7,6},{8,9},{9,8},{10,11... | collective-permute-start | bytes 294920 | tf_op jit(solution)/shard_map/ppermute | solution.py:443
  49.6 4.6 %collective-permute-start.12 = (bf16[24,2048]{1,0:T(8,128)(2,1)S(1)}, bf16[24,2048]{1,0:T(8,128)(2,1)S(1)}, u32[]{:S(2)}, u32[]{:S(2)}) collective-permute-start(bf16[24,2048]{1,0:T(8,128)(2,1)S(1)} %get-tuple-element.28), channel_id=1, source_target_pairs={{0,4},{1,5},{2,6},{3,7},{4,0},{5,1},{6,2},{7,3},{8,12},{9,13},{10,... | collective-permute-start | bytes 294920 | tf_op jit(solution)/shard_map/ppermute | solution.py:443

commit v7 on v6

--- a/solution.py
+++ b/solution.py
@@ -464,7 +464,7 @@
         lax.ppermute(projected[rank], "tp", [(i, i ^ rank) for i in range(ranks)])
         for rank in range(1, ranks)
     ]
-    late = (projected[0][0, 0] * 0).astype(jnp.int32)
+    late = (far_queries[-1][0, 0] * 0).astype(jnp.int32)
     lengths = jnp.sum(
         jnp.where(jnp.arange(GROUPS)[:, None] == group, suffix_lengths + late, 0), axis=0
     )
@@ -485,7 +485,7 @@
     suffix = suffix[:1] + [across(suffix[side], side=side) for side in range(1, splits)]
 
     for array in arrived:
-        array = array_after(array, *others, *far_queries[1:])
+        array = array_after(array, projected[0], *far_queries[1:])
         sources += [array, across(array, core=1)]
     keys, values = collect_pages(listed, place, sources, pages, splits)
 

time: 55.1 us -> 54.9 us (level)
  other arithmetic: 1.32 us -> 2.12 us
  starting transfers between devices: 20.4 us -> 19.7 us
    another operation x2, other arithmetic: 0.1 us -> 0.9 us  [local(): jnp.stack([columns(array, split ^ side, HD) for array in (prefix_keys, pr...]
    ppermute x11, starting transfers between devices: 15.1 us -> 14.5 us  [across(): return lax.ppermute(array, 'seq', [(i, i ^ step) for i in range(seq_count)])]
  transfers between devices with their start and end apart: 15 -> 15, of which waited for: 7 -> 8; matrix products, arithmetic and copies ran while one was open for 6% -> 7% of each run, Pallas kernels for 23% -> 23%
where the time goes in v7:
time: 54.9 us; the launch traced here: 54.7 us
  starting transfers between devices  19.7 us (36%)
  Pallas kernels  19.4 us (35%)
  waiting for transfers between devices  7.55 us (14%)
  local copies, waits for them, and re-layouts  4.36 us (8%)
  other arithmetic  2.12 us (4%)
  between operations  1.52 us (3%)
    ppermute x11, starting transfers between devices, across(): return lax.ppermute(array, 'seq', [(i, i ^ step) for i in range(seq_count)])  14.5 us
    pallas_call x3, Pallas kernels, attend(): pl.pallas_call(body, in_specs=[SMEM, SMEM, SMEM] + [HBM] * len(fetched) +...  9.93 us
    pallas_call x1, Pallas kernels, project_kv(): pl.pallas_call(body, in_specs=[SMEM, VMEM, HBM, ANY], out_specs=[VMEM] *...  4.61 us
    ppermute x3, waiting for transfers between devices, quad(): return lax.ppermute(array, ('seq', 'tp'), route)  3.97 us
    ppermute x3, starting transfers between devices, quad(): return lax.ppermute(array, ('seq', 'tp'), route)  3.55 us
    ppermute x11, waiting for transfers between devices, across(): return lax.ppermute(array, 'seq', [(i, i ^ step) for i in range(seq_count)])  3 us
    pallas_call x1, Pallas kernels, project(): pl.pallas_call(body, in_specs=[SMEM] + [VMEM] * (len(partials) + 1), out_...  2.31 us
    ppermute x1, starting transfers between devices, local(): lax.ppermute(projected[rank], 'tp', [(i, i ^ rank) for i in range(ranks)])  1.69 us
  transfers between devices with their start and end apart: 15, of which 8 were waited for; matrix products, arithmetic and copies ran while one was open for 7% of the time, Pallas kernels for 23%

profile of v7, /device:TPU:0, one launch (start us, length us, event | category | flops | bytes accessed | tf_op | source)
XLA Modules:
  0.0 54.7 jit_solution(10738355825339253968)
XLA Ops:
  0.6 0.0 copy-start
  0.6 0.0 copy-start.1
  0.7 0.9 %constant_dynamic-slice_fusion.1 = (bf16[24,1024]{1,0:T(8,128)(2,1)S(1)}, bf16[24,1024]{1,0:T(8,128)(2,1)S(1)}) fusion(bf16[24,2048]{1,0:T(8,128)(2,1)} %param.10, s32[]{:T(128)S(6)} %select_n.48, s32[]{:T(128)S(6)} %select_n.49), kind=kLoop, calls=%fused_computation.17 | loop fusion | bytes 196616 | tf_op jit(solution)/shard_map/dynamic_slice | solution.py:446
  1.6 3.0 %collective-permute-start = (bf16[24,1024]{1,0:T(8,128)(2,1)S(1)}, bf16[24,1024]{1,0:T(8,128)(2,1)S(1)}, u32[]{:S(2)}, u32[]{:S(2)}) collective-permute-start(bf16[24,1024]{1,0:T(8,128)(2,1)S(1)} %get-tuple-element.37), channel_id=1, source_target_pairs={{0,4},{2,6},{4,0},{6,2},{8,12},{10,14},{12,8},{14,10},{16,20},{18,... | collective-permute-start | bytes 147464 | tf_op jit(solution)/shard_map/ppermute | solution.py:431
  4.6 1.3 %dynamic-slice_bitcast_fusion = (bf16[1,8,128,128]{3,2,1,0:T(8,128)(2,1)S(1)}, bf16[1,8,128,128]{3,2,1,0:T(8,128)(2,1)S(1)}, bf16[1,8,128,128]{3,2,1,0:T(8,128)(2,1)S(1)}, bf16[1,8,128,128]{3,2,1,0:T(8,128)(2,1)S(1)}) fusion(bf16[8,128,256]{2,1,0:T(8,128)(2,1)} %refs_1_.1, s32[]{:T(128)S(6)} %select_n.54, s32[]{:T(128)S(6)} %select_n.53, ...), kind=kLoop, calls=%fused_computation.2 | loop fusion | bytes 2097160 | tf_op jit(solution)/shard_map/stack | solution.py:454
  5.9 0.1 pad_maximum_fusion
  6.0 0.1 collective-permute-start.5
  6.0 0.8 %pad_maximum_fusion.1 = bf16[2,8,128,128]{3,2,1,0:T(8,128)(2,1)} fusion(bf16[1,8,128,128]{3,2,1,0:T(8,128)(2,1)S(1)} %get-tuple-element.34, bf16[1,8,128,128]{3,2,1,0:T(8,128)(2,1)S(1)} %get-tuple-element.44), kind=kLoop, calls=%fused_computation.1 | loop fusion | flops 262144 | bytes 1048576 | tf_op jit(solution)/shard_map/stack | solution.py:454
  6.9 0.0 collective-permute-start.6
  7.0 0.7 %concatenate.12.place_ref = s32[133]{0:T(256)S(1)} concatenate(s32[1]{0:T(128)} %bitcast, s32[1]{0:T(128)} %bitcast.1, s32[1]{0:T(128)} %bitcast.2, s32[1]{0:T(128)} %bitcast.3, s32[1]{0:T(128)} %bitcast.4, s32[128]{0:T(128)} %param.13), dimensions={0} | concatenate | bytes 1064 | tf_op jit(solution)/shard_map/concatenate | solution.py:427
  7.7 0.0 collective-permute-done
  7.7 4.1 %collective-permute-start.1 = (bf16[48,1024]{1,0:T(8,128)(2,1)S(1)}, bf16[48,1024]{1,0:T(8,128)(2,1)S(1)}, u32[]{:S(2)}, u32[]{:S(2)}) collective-permute-start(bf16[48,1024]{1,0:T(8,128)(2,1)S(1)} %pad_maximum_fusion.2._.refs_0_), channel_id=1, source_target_pairs={{0,24},{2,26},{4,28},{6,30},{8,16},{10,18},{12,20},{14,22},{16,8},... | collective-permute-start | bytes 294920 | tf_op jit(solution)/shard_map/ppermute | solution.py:431
  11.9 0.0 collective-permute-start.2
  11.9 0.7 %collective-permute-start.7 = (bf16[48,1024]{1,0:T(8,128)(2,1)S(1)}, bf16[48,1024]{1,0:T(8,128)(2,1)S(1)}, u32[]{:S(2)}, u32[]{:S(2)}) collective-permute-start(bf16[48,1024]{1,0:T(8,128)(2,1)S(1)} %pad_maximum_fusion.2._.refs_0_), channel_id=1, source_target_pairs={{0,8},{2,10},{4,12},{6,14},{8,0},{10,2},{12,4},{14,6},{16,24},{18,... | collective-permute-start | bytes 294920 | tf_op jit(solution)/shard_map/ppermute | solution.py:431
  12.5 0.9 %copy-done.2 = bf16[24,4096]{1,0:T(8,128)(2,1)S(1)} copy-done((bf16[24,4096]{1,0:T(8,128)(2,1)S(1)}, bf16[24,4096]{1,0:T(8,128)(2,1)}, u32[]{:S(2)}) %copy-start.2) | copy-done | bytes 196632
  13.4 4.6 %shard_map.95 = (f32[24,512]{1,0:T(8,128)S(1)}, f32[24,512]{1,0:T(8,128)S(1)}, s32[34]{0:T(128)S(1)}) custom-call(s32[133]{0:T(256)S(1)} %concatenate.12.place_ref, bf16[24,4096]{1,0:T(8,128)(2,1)S(1)} %copy-done.2, bf16[4096,1024]{1,0:T(8,128)(2,1)} %weight_ref.1, bf16[48,1024]{1,0:T(8,128)(2,1)S(1)} %pad_maximum_fusion.2._.refs_0_), custom_call_target="tpu_custom_call" | custom-call | flops 1 | bytes 1 | tf_op jit(solution)/shard_map/pallas_call | solution.py:93
  18.1 1.7 %collective-permute-start.3 = (f32[24,512]{1,0:T(8,128)S(1)}, f32[24,512]{1,0:T(8,128)S(1)}, u32[]{:S(2)}, u32[]{:S(2)}) collective-permute-start(f32[24,512]{1,0:T(8,128)S(1)} %get-tuple-element.19), channel_id=1, source_target_pairs={{0,1},{1,0},{2,3},{3,2},{4,5},{5,4},{6,7},{7,6},{8,9},{9,8},{10,11... | collective-permute-start | bytes 147464 | tf_op jit(solution)/shard_map/ppermute | solution.py:464
  19.8 0.5 slice.4
  21.0 0.1 select_reduce_fusion.2
  21.0 0.1 select_reduce_fusion.1
  21.2 0.1 select_reduce_fusion
  21.3 0.2 collective-permute-done.6.refs_0_
  21.4 0.0 collective-permute-start.8
  21.4 0.1 fusion
  21.6 0.1 pad_maximum_fusion.3
  21.6 0.6 %collective-permute-done.3.refs_1_ = f32[24,512]{1,0:T(8,128)S(1)} collective-permute-done((f32[24,512]{1,0:T(8,128)S(1)}, f32[24,512]{1,0:T(8,128)S(1)}, u32[]{:S(2)}, u32[]{:S(2)}) %collective-permute-start.3) | collective-permute-done | bytes 49184 | tf_op jit(solution)/shard_map/ppermute | solution.py:464
  22.2 1.3 %shard_map.96 = (bf16[24,512]{1,0:T(8,128)(2,1)}, bf16[24,256]{1,0:T(8,128)(2,1)S(1)}, bf16[24,256]{1,0:T(8,128)(2,1)S(1)}) custom-call(s32[133]{0:T(256)S(1)} %concatenate.12.place_ref, f32[24,512]{1,0:T(8,128)S(1)} %get-tuple-element.18.refs_0_.refs_1_, f32[24,512]{1,0:T(8,128)S(1)} %collective-permute-done.3.refs_1_, ...), custom_call_target="tpu_custom_call" | custom-call | flops 1 | bytes 1 | tf_op jit(solution)/shard_map/pallas_call | solution.py:132
  23.5 1.7 %collective-permute-start.4 = (bf16[24,256]{1,0:T(8,128)(2,1)S(1)}, bf16[24,256]{1,0:T(8,128)(2,1)S(1)}, u32[]{:S(2)}, u32[]{:S(2)}) collective-permute-start(bf16[24,256]{1,0:T(8,128)(2,1)S(1)} %get-tuple-element.21), channel_id=1, source_target_pairs={{0,4},{2,6},{4,0},{6,2},{8,12},{10,14},{12,8},{14,10},{16,20},{18,... | collective-permute-start | bytes 36872 | tf_op jit(solution)/shard_map/ppermute | solution.py:431
  25.2 0.0 collective-permute-done.5.refs_2_
  25.2 0.0 collective-permute-done.8.refs_4_
  25.2 1.2 %shard_map.98 = (bf16[4096,128]{1,0:T(8,128)(2,1)S(1)}, bf16[4096,128]{1,0:T(8,128)(2,1)S(1)}) custom-call(s32[34]{0:T(128)S(1)} %get-tuple-element.17.list_ref, s32[133]{0:T(256)S(1)} %concatenate.12.place_ref, bf16[8,128,256]{2,1,0:T(8,128)(2,1)S(1)} %copy-done, bf16[8,128,256]{2,1,0:T(8,128)(2,1)S(1)} %copy-done.1, ...), custom_call_target="tpu_custom_call" | custom-call | flops 1 | bytes 1 | tf_op jit(solution)/shard_map/pallas_call | solution.py:184
  26.4 0.8 %collective-permute-done.4.refs_4_.refs_2_ = bf16[24,256]{1,0:T(8,128)(2,1)S(1)} collective-permute-done((bf16[24,256]{1,0:T(8,128)(2,1)S(1)}, bf16[24,256]{1,0:T(8,128)(2,1)S(1)}, u32[]{:S(2)}, u32[]{:S(2)}) %collective-permute-start.4) | collective-permute-done | bytes 12320 | tf_op jit(solution)/shard_map/ppermute | solution.py:431
  27.2 4.3 %shard_map.99 = (bf16[400,128]{1,0:T(8,128)(2,1)S(1)}, bf16[400,128]{1,0:T(8,128)(2,1)S(1)}, bf16[1024,4096]{1,0:T(8,128)(2,1)S(1)}) custom-call(s32[34]{0:T(128)S(1)} %get-tuple-element.17.list_ref, s32[2,8]{1,0:T(2,128)S(1)} %copy-done.3, s32[133]{0:T(256)S(1)} %concatenate.12.place_ref, bf16[2048,4096]{1,0:T(8,128)(2,1)} %refs_0_.3, ...), custom_call_target="tpu_custom_call" | custom-call | flops 1610612736 | bytes 1572864 | tf_op jit(solution)/shard_map/pallas_call | solution.py:321
  31.6 3.8 %collective-permute-start.9 = (bf16[400,128]{1,0:T(8,128)(2,1)S(1)}, bf16[400,128]{1,0:T(8,128)(2,1)S(1)}, u32[]{:S(2)}, u32[]{:S(2)}) collective-permute-start(bf16[400,128]{1,0:T(8,128)(2,1)S(1)} %get-tuple-element.24), channel_id=1, source_target_pairs={{0,24},{2,26},{4,28},{6,30},{8,16},{10,18},{12,20},{14,22},{16,8},... | collective-permute-start | bytes 307208 | tf_op jit(solution)/shard_map/ppermute | solution.py:431
  35.4 2.8 %shard_map.100 = bf16[400,128]{1,0:T(8,128)(2,1)S(1)} custom-call(s32[34]{0:T(128)S(1)} %get-tuple-element.17.list_ref, s32[2,8]{1,0:T(2,128)S(1)} %copy-done.3, s32[133]{0:T(256)S(1)} %concatenate.12.place_ref, bf16[48,1024]{1,0:T(8,128)(2,1)S(1)} %collective-permute-done.7.refs_2_.refs_0_, bf16[24,256]{1,0:T(8,128)(2,1)S(1)} %get-tuple-element.20.refs_3_.refs_1_, ...), custom_call_target="tpu_custom_call" | custom-call | flops 805306368 | bytes 1572864 | tf_op jit(solution)/shard_map/pallas_call | solution.py:321
  38.2 1.1 %collective-permute-start.11 = (bf16[400,128]{1,0:T(8,128)(2,1)S(1)}, bf16[400,128]{1,0:T(8,128)(2,1)S(1)}, u32[]{:S(2)}, u32[]{:S(2)}) collective-permute-start(bf16[400,128]{1,0:T(8,128)(2,1)S(1)} %shard_map.100), channel_id=1, source_target_pairs={{0,8},{2,10},{4,12},{6,14},{8,0},{10,2},{12,4},{14,6},{16,24},{18,... | collective-permute-start | bytes 307208 | tf_op jit(solution)/shard_map/ppermute | solution.py:431
  39.3 2.8 %shard_map.101.refs_3_ = bf16[400,128]{1,0:T(8,128)(2,1)S(1)} custom-call(s32[34]{0:T(128)S(1)} %get-tuple-element.17.list_ref, s32[2,8]{1,0:T(2,128)S(1)} %copy-done.3, s32[133]{0:T(256)S(1)} %concatenate.12.place_ref, bf16[48,1024]{1,0:T(8,128)(2,1)S(1)} %pad_maximum_fusion.2._.refs_0_, bf16[24,256]{1,0:T(8,128)(2,1)S(1)} %get-tuple-element.20.refs_3_.refs_1_, ...), custom_call_target="tpu_custom_call" | custom-call | flops 805306368 | bytes 1572864 | tf_op jit(solution)/shard_map/pallas_call | solution.py:321
  42.1 0.0 collective-permute-done.9.refs_0_
  42.1 1.1 %collective-permute-done.10.refs_1_ = bf16[400,128]{1,0:T(8,128)(2,1)S(1)} collective-permute-done((bf16[400,128]{1,0:T(8,128)(2,1)S(1)}, bf16[400,128]{1,0:T(8,128)(2,1)S(1)}, u32[]{:S(2)}, u32[]{:S(2)}) %collective-permute-start.10) | collective-permute-done | bytes 102432 | tf_op jit(solution)/shard_map/ppermute | solution.py:431
  43.2 0.9 %collective-permute-done.11.refs_2_ = bf16[400,128]{1,0:T(8,128)(2,1)S(1)} collective-permute-done((bf16[400,128]{1,0:T(8,128)(2,1)S(1)}, bf16[400,128]{1,0:T(8,128)(2,1)S(1)}, u32[]{:S(2)}, u32[]{:S(2)}) %collective-permute-start.11) | collective-permute-done | bytes 102432 | tf_op jit(solution)/shard_map/ppermute | solution.py:431
  44.2 2.3 %shard_map.102 = (f32[24,2048]{1,0:T(8,128)S(1)}, bf16[24,2048]{1,0:T(8,128)(2,1)S(1)}, bf16[24,2048]{1,0:T(8,128)(2,1)S(1)}, bf16[24,2048]{1,0:T(8,128)(2,1)S(1)}) custom-call(s32[133]{0:T(256)S(1)} %concatenate.12.place_ref, bf16[400,128]{1,0:T(8,128)(2,1)S(1)} %collective-permute-done.9.refs_0_, bf16[400,128]{1,0:T(8,128)(2,1)S(1)} %collective-permute-done.10.refs_1_, ...), custom_call_target="tpu_custom_call" | custom-call | flops 402653184 | bytes 4194304 | tf_op jit(solution)/shard_map/pallas_call | solution.py:386
  46.5 1.6 %collective-permute-start.14 = (bf16[24,2048]{1,0:T(8,128)(2,1)S(1)}, bf16[24,2048]{1,0:T(8,128)(2,1)S(1)}, u32[]{:S(2)}, u32[]{:S(2)}) collective-permute-start(bf16[24,2048]{1,0:T(8,128)(2,1)S(1)} %get-tuple-element.30), channel_id=1, source_target_pairs={{0,5},{1,4},{2,7},{3,6},{4,1},{5,0},{6,3},{7,2},{8,13},{9,12},{10,... | collective-permute-start | bytes 294920 | tf_op jit(solution)/shard_map/ppermute | solution.py:443
  48.1 1.3 %collective-permute-start.13 = (bf16[24,2048]{1,0:T(8,128)(2,1)S(1)}, bf16[24,2048]{1,0:T(8,128)(2,1)S(1)}, u32[]{:S(2)}, u32[]{:S(2)}) collective-permute-start(bf16[24,2048]{1,0:T(8,128)(2,1)S(1)} %get-tuple-element.29), channel_id=1, source_target_pairs={{0,1},{1,0},{2,3},{3,2},{4,5},{5,4},{6,7},{7,6},{8,9},{9,8},{10,11... | collective-permute-start | bytes 294920 | tf_op jit(solution)/shard_map/ppermute | solution.py:443
  49.4 0.6 %collective-permute-start.12 = (bf16[24,2048]{1,0:T(8,128)(2,1)S(1)}, bf16[24,2048]{1,0:T(8,128)(2,1)S(1)}, u32[]{:S(2)}, u32[]{:S(2)}) collective-permute-start(bf16[24,2048]{1,0:T(8,128)(2,1)S(1)} %get-tuple-element.28), channel_id=1, source_target_pairs={{0,4},{1,5},{2,6},{3,7},{4,0},{5,1},{6,2},{7,3},{8,12},{9,13},{10,... | collective-permute-start | bytes 294920 | tf_op jit(solution)/shard_map/ppermute | solution.py:443
  50.0 2.0 %collective-permute-done.14 = bf16[24,2048]{1,0:T(8,128)(2,1)S(1)} collective-permute-done((bf16[24,2048]{1,0:T(8,128)(2,1)S(1)}, bf16[24,2048]{1,0:T(8,128)(2,1)S(1)}, u32[]{:S(2)}, u32[]{:S(2)}) %collective-permute-start.14) | collective-permute-done | bytes 98336 | tf_op jit(solution)/shard_map/ppermute | solution.py:443
  52.1 1.0 %collective-permute-done.13 = bf16[24,2048]{1,0:T(8,128)(2,1)S(1)} collective-permute-done((bf16[24,2048]{1,0:T(8,128)(2,1)S(1)}, bf16[24,2048]{1,0:T(8,128)(2,1)S(1)}, u32[]{:S(2)}, u32[]{:S(2)}) %collective-permute-start.13) | collective-permute-done | bytes 98336 | tf_op jit(solution)/shard_map/ppermute | solution.py:443
  53.0 1.0 %collective-permute-done.12 = bf16[24,2048]{1,0:T(8,128)(2,1)S(1)} collective-permute-done((bf16[24,2048]{1,0:T(8,128)(2,1)S(1)}, bf16[24,2048]{1,0:T(8,128)(2,1)S(1)}, u32[]{:S(2)}, u32[]{:S(2)}) %collective-permute-start.12) | collective-permute-done | bytes 98336 | tf_op jit(solution)/shard_map/ppermute | solution.py:443
  54.0 0.7 %add_convert_fusion = bf16[24,2048]{1,0:T(8,128)(2,1)} fusion(bf16[24,2048]{1,0:T(8,128)(2,1)S(1)} %collective-permute-done.14, bf16[24,2048]{1,0:T(8,128)(2,1)S(1)} %collective-permute-done.13, f32[24,2048]{1,0:T(8,128)S(1)} %get-tuple-element.27, bf16[24,2048]{1,0:T(8,128)(2,1)S(1)} %collective-permute-done.12), kind=kLoop, calls=%fused_computation.6 | loop fusion | flops 344064 | bytes 589824 | tf_op jit(solution)/shard_map/convert_element_type | solution.py:511
  (15 shorter events, 0.1 us)
Async XLA Ops:
  0.6 24.6 %copy-start = (bf16[8,128,256]{2,1,0:T(8,128)(2,1)S(1)}, bf16[8,128,256]{2,1,0:T(8,128)(2,1)}, u32[]{:S(2)}) copy-start(bf16[8,128,256]{2,1,0:T(8,128)(2,1)} %refs_0_.2) | copy-start | bytes 1572868
  0.6 24.6 %copy-start.1 = (bf16[8,128,256]{2,1,0:T(8,128)(2,1)S(1)}, bf16[8,128,256]{2,1,0:T(8,128)(2,1)}, u32[]{:S(2)}) copy-start(bf16[8,128,256]{2,1,0:T(8,128)(2,1)} %refs_1_.1) | copy-start | bytes 1572868
  0.7 20.3 %copy-start.3 = (s32[2,8]{1,0:T(2,128)S(1)}, s32[2,8]{1,0:T(2,128)}, u32[]{:S(2)}) copy-start(s32[2,8]{1,0:T(2,128)} %len_ref.5) | copy-start | bytes 196
  1.6 6.1 %collective-permute-start = (bf16[24,1024]{1,0:T(8,128)(2,1)S(1)}, bf16[24,1024]{1,0:T(8,128)(2,1)S(1)}, u32[]{:S(2)}, u32[]{:S(2)}) collective-permute-start(bf16[24,1024]{1,0:T(8,128)(2,1)S(1)} %get-tuple-element.37), channel_id=1, source_target_pairs={{0,4},{2,6},{4,0},{6,2},{8,12},{10,14},{12,8},{14,10},{16,20},{18,... | collective-permute-start | bytes 147464 | tf_op jit(solution)/shard_map/ppermute | solution.py:431
  6.0 19.2 %collective-permute-start.5 = (bf16[2,8,128,128]{3,2,1,0:T(8,128)(2,1)S(1)}, bf16[2,8,128,128]{3,2,1,0:T(8,128)(2,1)S(1)}, u32[]{:S(2)}, u32[]{:S(2)}) collective-permute-start(bf16[2,8,128,128]{3,2,1,0:T(8,128)(2,1)S(1)} %pad_maximum_fusion), channel_id=1, source_target_pairs={{0,2},{2,0},{4,6},{6,4},{8,10},{10,8},{12,14},{14,12},{16,18},{18,... | collective-permute-start | bytes 1572872 | tf_op jit(solution)/shard_map/ppermute | solution.py:431
  6.9 14.5 %collective-permute-start.6 = (bf16[2,8,128,128]{3,2,1,0:T(8,128)(2,1)}, bf16[2,8,128,128]{3,2,1,0:T(8,128)(2,1)S(1)}, u32[]{:S(2)}, u32[]{:S(2)}) collective-permute-start(bf16[2,8,128,128]{3,2,1,0:T(8,128)(2,1)} %pad_maximum_fusion.1), channel_id=1, source_target_pairs={{0,4},{2,6},{4,0},{6,2},{8,12},{10,14},{12,8},{14,10},{16,20},{18,... | collective-permute-start | bytes 1572872 | tf_op jit(solution)/shard_map/ppermute | solution.py:431
  7.7 10.3 %collective-permute-start.1 = (bf16[48,1024]{1,0:T(8,128)(2,1)S(1)}, bf16[48,1024]{1,0:T(8,128)(2,1)S(1)}, u32[]{:S(2)}, u32[]{:S(2)}) collective-permute-start(bf16[48,1024]{1,0:T(8,128)(2,1)S(1)} %pad_maximum_fusion.2._.refs_0_), channel_id=1, source_target_pairs={{0,24},{2,26},{4,28},{6,30},{8,16},{10,18},{12,20},{14,22},{16,8},... | collective-permute-start | bytes 294920 | tf_op jit(solution)/shard_map/ppermute | solution.py:431
  11.9 9.4 %collective-permute-start.2 = (bf16[48,1024]{1,0:T(8,128)(2,1)S(1)}, bf16[48,1024]{1,0:T(8,128)(2,1)S(1)}, u32[]{:S(2)}, u32[]{:S(2)}) collective-permute-start(bf16[48,1024]{1,0:T(8,128)(2,1)S(1)} %pad_maximum_fusion.2._.refs_0_), channel_id=1, source_target_pairs={{0,16},{2,18},{4,20},{6,22},{8,24},{10,26},{12,28},{14,30},{16,0},... | collective-permute-start | bytes 294920 | tf_op jit(solution)/shard_map/ppermute | solution.py:431
  11.9 9.4 %collective-permute-start.7 = (bf16[48,1024]{1,0:T(8,128)(2,1)S(1)}, bf16[48,1024]{1,0:T(8,128)(2,1)S(1)}, u32[]{:S(2)}, u32[]{:S(2)}) collective-permute-start(bf16[48,1024]{1,0:T(8,128)(2,1)S(1)} %pad_maximum_fusion.2._.refs_0_), channel_id=1, source_target_pairs={{0,8},{2,10},{4,12},{6,14},{8,0},{10,2},{12,4},{14,6},{16,24},{18,... | collective-permute-start | bytes 294920 | tf_op jit(solution)/shard_map/ppermute | solution.py:431
  12.5 0.9 %copy-start.2 = (bf16[24,4096]{1,0:T(8,128)(2,1)S(1)}, bf16[24,4096]{1,0:T(8,128)(2,1)}, u32[]{:S(2)}) copy-start(bf16[24,4096]{1,0:T(8,128)(2,1)} %hidden_ref.1) | copy-start | bytes 589828
  18.1 4.2 %collective-permute-start.3 = (f32[24,512]{1,0:T(8,128)S(1)}, f32[24,512]{1,0:T(8,128)S(1)}, u32[]{:S(2)}, u32[]{:S(2)}) collective-permute-start(f32[24,512]{1,0:T(8,128)S(1)} %get-tuple-element.19), channel_id=1, source_target_pairs={{0,1},{1,0},{2,3},{3,2},{4,5},{5,4},{6,7},{7,6},{8,9},{9,8},{10,11... | collective-permute-start | bytes 147464 | tf_op jit(solution)/shard_map/ppermute | solution.py:464
  21.4 3.8 %collective-permute-start.8 = (bf16[2,8,128,128]{3,2,1,0:T(8,128)(2,1)S(1)}, bf16[2,8,128,128]{3,2,1,0:T(8,128)(2,1)S(1)}, u32[]{:S(2)}, u32[]{:S(2)}) collective-permute-start(bf16[2,8,128,128]{3,2,1,0:T(8,128)(2,1)S(1)} %shard_map.97.refs_3_), channel_id=1, source_target_pairs={{0,2},{2,0},{4,6},{6,4},{8,10},{10,8},{12,14},{14,12},{16,18},{18,... | collective-permute-start | bytes 1572872 | tf_op jit(solution)/shard_map/ppermute | solution.py:431
  23.5 3.7 %collective-permute-start.4 = (bf16[24,256]{1,0:T(8,128)(2,1)S(1)}, bf16[24,256]{1,0:T(8,128)(2,1)S(1)}, u32[]{:S(2)}, u32[]{:S(2)}) collective-permute-start(bf16[24,256]{1,0:T(8,128)(2,1)S(1)} %get-tuple-element.21), channel_id=1, source_target_pairs={{0,4},{2,6},{4,0},{6,2},{8,12},{10,14},{12,8},{14,10},{16,20},{18,... | collective-permute-start | bytes 36872 | tf_op jit(solution)/shard_map/ppermute | solution.py:431
  31.6 10.6 %collective-permute-start.9 = (bf16[400,128]{1,0:T(8,128)(2,1)S(1)}, bf16[400,128]{1,0:T(8,128)(2,1)S(1)}, u32[]{:S(2)}, u32[]{:S(2)}) collective-permute-start(bf16[400,128]{1,0:T(8,128)(2,1)S(1)} %get-tuple-element.24), channel_id=1, source_target_pairs={{0,24},{2,26},{4,28},{6,30},{8,16},{10,18},{12,20},{14,22},{16,8},... | collective-permute-start | bytes 307208 | tf_op jit(solution)/shard_map/ppermute | solution.py:431
  35.4 7.9 %collective-permute-start.10 = (bf16[400,128]{1,0:T(8,128)(2,1)S(1)}, bf16[400,128]{1,0:T(8,128)(2,1)S(1)}, u32[]{:S(2)}, u32[]{:S(2)}) collective-permute-start(bf16[400,128]{1,0:T(8,128)(2,1)S(1)} %get-tuple-element.25), channel_id=1, source_target_pairs={{0,16},{2,18},{4,20},{6,22},{8,24},{10,26},{12,28},{14,30},{16,0},... | collective-permute-start | bytes 307208 | tf_op jit(solution)/shard_map/ppermute | solution.py:431
  38.2 6.0 %collective-permute-start.11 = (bf16[400,128]{1,0:T(8,128)(2,1)S(1)}, bf16[400,128]{1,0:T(8,128)(2,1)S(1)}, u32[]{:S(2)}, u32[]{:S(2)}) collective-permute-start(bf16[400,128]{1,0:T(8,128)(2,1)S(1)} %shard_map.100), channel_id=1, source_target_pairs={{0,8},{2,10},{4,12},{6,14},{8,0},{10,2},{12,4},{14,6},{16,24},{18,... | collective-permute-start | bytes 307208 | tf_op jit(solution)/shard_map/ppermute | solution.py:431
  46.5 5.6 %collective-permute-start.14 = (bf16[24,2048]{1,0:T(8,128)(2,1)S(1)}, bf16[24,2048]{1,0:T(8,128)(2,1)S(1)}, u32[]{:S(2)}, u32[]{:S(2)}) collective-permute-start(bf16[24,2048]{1,0:T(8,128)(2,1)S(1)} %get-tuple-element.30), channel_id=1, source_target_pairs={{0,5},{1,4},{2,7},{3,6},{4,1},{5,0},{6,3},{7,2},{8,13},{9,12},{10,... | collective-permute-start | bytes 294920 | tf_op jit(solution)/shard_map/ppermute | solution.py:443
  48.1 4.9 %collective-permute-start.13 = (bf16[24,2048]{1,0:T(8,128)(2,1)S(1)}, bf16[24,2048]{1,0:T(8,128)(2,1)S(1)}, u32[]{:S(2)}, u32[]{:S(2)}) collective-permute-start(bf16[24,2048]{1,0:T(8,128)(2,1)S(1)} %get-tuple-element.29), channel_id=1, source_target_pairs={{0,1},{1,0},{2,3},{3,2},{4,5},{5,4},{6,7},{7,6},{8,9},{9,8},{10,11... | collective-permute-start | bytes 294920 | tf_op jit(solution)/shard_map/ppermute | solution.py:443
  49.4 4.6 %collective-permute-start.12 = (bf16[24,2048]{1,0:T(8,128)(2,1)S(1)}, bf16[24,2048]{1,0:T(8,128)(2,1)S(1)}, u32[]{:S(2)}, u32[]{:S(2)}) collective-permute-start(bf16[24,2048]{1,0:T(8,128)(2,1)S(1)} %get-tuple-element.28), channel_id=1, source_target_pairs={{0,4},{1,5},{2,6},{3,7},{4,0},{5,1},{6,2},{7,3},{8,12},{9,13},{10,... | collective-permute-start | bytes 294920 | tf_op jit(solution)/shard_map/ppermute | solution.py:443
